TPU v7x, 32 devices: a whole 2x2x4 slice. The times are simulated.
32 devices in a mesh: rep: 8 (over z, core), fsdp: 4 (over y, x).
Axes of the slice: x: 2, y: 2, z: 4, core: 2. Of those that a mesh axis runs over, the one named last changes fastest.
Arguments:
- hidden: bfloat16 [8, 768, 8192], P('rep', 'fsdp'), may hold values from -6 to 6
- key_cotangent: bfloat16 [8, 768, 1024], P('rep', 'fsdp'), may hold values from -6 to 6
- local_weight: float32 [8, 8192, 1024], P('rep', 'fsdp'), may hold values from -6 to 6
- adam_first: float32 [8, 8192, 1024], P('rep', 'fsdp'), may hold values from -2 to 2
- adam_second: float32 [8, 8192, 1024], P('rep', 'fsdp'), may hold values from 0.02 to 0.3
- outer_weight: float32 [4, 2048, 1024], P('fsdp', 'rep'), may hold values from -6 to 6
- outer_momentum: float32 [4, 2048, 1024], P('fsdp', 'rep'), may hold values from -2 to 2
- roster: int32 [8, 4], replicated, may hold values from 0 to 3, each once within a row
- step_count: int32 [1], replicated, may hold values from 0 to 31
Outputs:
- projected_keys: bfloat16 [8, 768, 1024], P('rep', 'fsdp')
- input_grad: bfloat16 [8, 768, 8192], P('rep', 'fsdp')
- new_local: float32 [8, 8192, 1024], P('rep', 'fsdp')
- new_outer: float32 [4, 2048, 1024], P('fsdp', 'rep')
- new_momentum: float32 [4, 2048, 1024], P('fsdp', 'rep')
Inputs may be any that keep to these rules, and one draw needn't show every extreme that they name: `roster`: each row names every fragment index once.
All inputs are finite; a program needn't handle non-finite values.
Results may differ from a plain program's by a relative error of at most 0.0045.
The roundings to bfloat16 on the way count: a program that leaves them out, or rounds other values in their place, can miss the bound.
Values may be sent and summed in bfloat16 or wider, within the bound.
No kernel may reach another device: no remote copies, remote signals or barrier semaphores. Data moves between devices by JAX's collectives and lax.ppermute only.
A program may use at most 192 MiB of HBM per device.

v0:
```python
import math

import jax
import jax.numpy as jnp
from jax import lax
from jax.sharding import PartitionSpec as P

D = 8192
FRAGS = 4
ROUNDS = 8


def adam_update(weight, first, second, grad, steps_done):
    first_new = 0.9 * first + 0.1 * grad
    second_new = 0.95 * second + 0.05 * grad * grad
    first_hat = first_new / (1.0 - jnp.power(jnp.float32(0.9), steps_done))
    second_hat = second_new / (1.0 - jnp.power(jnp.float32(0.95), steps_done))
    return weight - 0.1 * (first_hat / (jnp.sqrt(second_hat) + 1e-08) + 0.1 * weight)


def per_device(
    hidden,
    key_cotangent,
    local_weight,
    adam_first,
    adam_second,
    outer_weight,
    outer_momentum,
    roster,
    step_count,
):
    factor = 1.0 / math.sqrt(D)
    tokens = hidden[0]
    cotangent = key_cotangent[0]
    weight = local_weight[0]
    key_cols = weight.shape[1]
    frag_cols = key_cols // FRAGS
    fragment = roster[step_count[0] // FRAGS % ROUNDS, step_count[0] % FRAGS]
    column = fragment * frag_cols
    steps_done = (step_count[0] + 1).astype(jnp.float32)
    replicas = lax.axis_size("rep")
    outer_now = outer_weight[0]
    moment_now = outer_momentum[0]
    outer_frag = lax.dynamic_slice_in_dim(outer_now, column, frag_cols, 1)
    moment_frag = lax.dynamic_slice_in_dim(moment_now, column, frag_cols, 1)
    weight_half = weight.astype(jnp.bfloat16)
    piece = lax.all_gather(weight_half, "fsdp", axis=0, tiled=True)
    columns = tokens
    key_acc = jnp.dot(columns, piece, preferred_element_type=jnp.float32)
    back_part = lax.dot_general(
        cotangent, piece, (((1,), (1,)), ((), ())), preferred_element_type=jnp.float32
    )
    back_acc = back_part
    key_acc, back_acc = (key_acc, back_acc)
    keys_out = (key_acc * factor).astype(jnp.bfloat16)
    back_out = (back_acc * factor).astype(jnp.bfloat16)
    columns = tokens
    grad = lax.psum_scatter(
        (
            lax.dot_general(
                columns, cotangent, (((0,), (0,)), ((), ())), preferred_element_type=jnp.float32
            )
            * factor
        ).astype(jnp.bfloat16),
        "fsdp",
        scatter_dimension=0,
        tiled=True,
    ).astype(jnp.float32)
    inner = adam_update(weight, adam_first[0], adam_second[0], grad, steps_done)
    inner_frag = lax.dynamic_slice_in_dim(inner, column, frag_cols, 1)
    total = lax.psum_scatter(
        inner_frag.astype(jnp.bfloat16), "rep", scatter_dimension=0, tiled=True
    ).astype(jnp.float32)
    pseudo = outer_frag - total / replicas
    moment_own = 0.9 * moment_frag + pseudo
    outer_own = outer_frag - 0.7 * (pseudo + 0.9 * moment_own)
    outer_back = lax.all_gather(outer_own.astype(jnp.bfloat16), "rep", axis=0, tiled=True).astype(
        outer_own.dtype
    )
    inner = lax.dynamic_update_slice_in_dim(inner, outer_back, column, 1)
    outer_next = lax.dynamic_update_slice_in_dim(outer_now, outer_own, column, 1)
    moment_next = lax.dynamic_update_slice_in_dim(moment_now, moment_own, column, 1)
    return (keys_out[None], back_out[None], inner[None], outer_next[None], moment_next[None])


def solution(mesh):
    in_specs = (
        P("rep", "fsdp", None),
        P("rep", "fsdp", None),
        P("rep", "fsdp", None),
        P("rep", "fsdp", None),
        P("rep", "fsdp", None),
        P("fsdp", "rep", None),
        P("fsdp", "rep", None),
        P(),
        P(),
    )
    out_specs = (
        P("rep", "fsdp", None),
        P("rep", "fsdp", None),
        P("rep", "fsdp", None),
        P("fsdp", "rep", None),
        P("fsdp", "rep", None),
    )
    return jax.shard_map(
        per_device, mesh=mesh, in_specs=in_specs, out_specs=out_specs, check_vma=False
    )
```

profile of v0, /device:TPU:0, one launch (start us, length us, event | category | flops | bytes accessed | tf_op | source)
XLA Modules:
  0.0 418.0 jit_solution(1283709625633318950)
XLA Ops:
  7.2 0.0 copy-start
  7.2 0.0 reduce-scatter.3.cloned.1.call-start
  7.2 2.5 copy.20
  9.7 2.3 copy.21
  12.0 0.0 copy-done
  12.0 9.1 %multiply_convert_fusion = bf16[8192,1024]{1,0:T(8,128)(2,1)} fusion(bf16[1,192,8192]{2,1,0:T(8,128)(2,1)S(1)} %copy-done, bf16[1,192,1024]{2,1,0:T(8,128)(2,1)} %param.10), kind=kOutput, calls=%fused_computation | convolution fusion | flops 3238002688 | bytes 20316160 | tf_op jit(solution)/shard_map/dot_general | solution.py:60
  21.1 0.0 reduce-scatter.3.cloned.1.call-update
  21.1 0.0 reduce-scatter.5.cloned.1.call-start
  22.0 1.3 dynamic_slice.14
  23.9 153.9 %reduce-scatter.3.cloned.1.call-done = bf16[2048,1024]{1,0:T(8,128)(2,1)} async-done(((bf16[8192,1024]{1,0:T(8,128)(2,1)}), bf16[2048,1024]{1,0:T(8,128)(2,1)}) %reduce-scatter.3.cloned.1.call-update) | async-done | bytes 4194320 | tf_op jit(solution)/shard_map/reduce_scatter | solution.py:58
  177.8 12.7 %fusion.6 = f32[2048,1024]{1,0:T(8,128)S(1)} fusion(bf16[2048,1024]{1,0:T(8,128)(2,1)} %reduce-scatter.3.cloned.1.call-done, f32[1,2048,1024]{2,1,0:T(8,128)} %param.11, f32[1,2048,1024]{2,1,0:T(8,128)} %param.13, f32[1,2048,1024]{2,1,0:T(8,128)} %param.12, f32[]{:T(128)S(6)} %sub.20, f32[]{:T(128)S(6)} %sub.19), kind=kLoop, calls=%fused_computation.10 | loop fusion | flops 33554432 | bytes 37748744 | tf_op jit(solution)/shard_map/sub | solution.py:18
  190.6 0.0 copy-start.1
  190.6 3.4 copy-done.1
  194.0 1.1 dynamic-slice_convert_fusion
  195.1 0.0 reduce-scatter.5.cloned.1.call-update
  195.1 0.0 all-gather.3.cloned.1.call-start
  195.2 6.0 %bitcast_convert_fusion = bf16[2048,1024]{1,0:T(8,128)(2,1)} fusion(f32[1,2048,1024]{2,1,0:T(8,128)} %param.11), kind=kLoop, calls=%fused_computation.17 | loop fusion | flops 2097152 | bytes 12582912 | tf_op jit(solution)/shard_map/convert_element_type | solution.py:46
  201.2 0.0 all-gather.3.cloned.1.call-update
  201.2 0.2 all-gather.5.cloned.1.call-start
  201.4 26.0 %reduce-scatter.5.cloned.1.call-done = bf16[256,256]{1,0:T(8,128)(2,1)} async-done(((bf16[2048,256]{1,0:T(8,128)(2,1)}), bf16[256,256]{1,0:T(8,128)(2,1)}) %reduce-scatter.5.cloned.1.call-update) | async-done | bytes 131088 | tf_op jit(solution)/shard_map/reduce_scatter | solution.py:71
  227.5 2.0 fusion.26
  229.4 0.0 all-gather.5.cloned.1.call-update
  229.4 155.7 %all-gather.3.cloned.1.call-done = bf16[8192,1024]{1,0:T(8,128)(2,1)} async-done(((bf16[2048,1024]{1,0:T(8,128)(2,1)}), bf16[8192,1024]{1,0:T(8,128)(2,1)}) %all-gather.3.cloned.1.call-update) | async-done | bytes 16777232 | tf_op jit(solution)/shard_map/all_gather | solution.py:47
  385.1 13.2 %fusion.1 = bf16[1,192,8192]{2,1,0:T(8,128)(2,1)} fusion(bf16[8192,1024]{1,0:T(8,128)(2,1)} %all-gather.3.cloned.1.call-done, bf16[1,192,1024]{2,1,0:T(8,128)(2,1)} %param.10), kind=kOutput, calls=%fused_computation.5 | convolution fusion | flops 3224371200 | bytes 20316160 | tf_op jit(solution)/shard_map/dot_general | solution.py:50
  398.3 0.0 copy-start.2
  398.3 8.5 %fusion.21 = bf16[1,192,1024]{2,1,0:T(8,128)(2,1)} fusion(bf16[8192,1024]{1,0:T(8,128)(2,1)} %all-gather.3.cloned.1.call-done, bf16[1,192,8192]{2,1,0:T(8,128)(2,1)S(1)} %copy-done), kind=kOutput, calls=%fused_computation.25 | convolution fusion | flops 3221618688 | bytes 20316160 | tf_op jit(solution)/shard_map/dot_general | solution.py:49
  406.9 0.0 copy-done.2
  406.9 0.8 bitcast_dynamic-update-slice_fusion
  407.7 1.0 all-gather.5.cloned.1.call-done
  408.7 2.7 convert_dynamic-update-slice_fusion
Async XLA Ops:
  7.2 4.8 %copy-start = (bf16[1,192,8192]{2,1,0:T(8,128)(2,1)S(1)}, bf16[1,192,8192]{2,1,0:T(8,128)(2,1)}, u32[]{:S(2)}) copy-start(bf16[1,192,8192]{2,1,0:T(8,128)(2,1)} %param.9) | copy-start | bytes 9437188
  7.2 170.7 %reduce-scatter.3.cloned.1.call-start = ((), (), s32[]{:S(2)}) async-start(), calls=%async_computation.3 | async-start | bytes 20971520 | tf_op jit(solution)/shard_map/reduce_scatter | solution.py:58
  21.1 206.3 %reduce-scatter.5.cloned.1.call-start = ((), (), s32[]{:S(2)}) async-start(), calls=%async_computation.4 | async-start | bytes 1179648 | tf_op jit(solution)/shard_map/reduce_scatter | solution.py:71
  190.6 3.4 copy-start.1
  195.1 190.0 %all-gather.3.cloned.1.call-start = ((), (), s32[]{:S(2)}) async-start(), calls=%async_computation.2 | async-start | bytes 20971520 | tf_op jit(solution)/shard_map/all_gather | solution.py:47
  201.2 207.5 %all-gather.5.cloned.1.call-start = ((), (), s32[]{:S(2)}) async-start(), calls=%async_computation.5 | async-start | bytes 1179648 | tf_op jit(solution)/shard_map/all_gather | solution.py:77
  398.3 8.5 %copy-start.2 = (f32[256,256]{1,0:T(8,128)S(1)}, f32[256,256]{1,0:T(8,128)}, u32[]{:S(2)}) copy-start(f32[256,256]{1,0:T(8,128)} %get-tuple-element.7) | copy-start | bytes 786436
Sparse Core Ops, SparseCore 0:
  21.3 156.5 reduce-scatter.2
  195.2 32.1 reduce-scatter.4
  229.3 155.7 all-gather.2
  386.6 22.1 all-gather.4
where the time goes:
time: 418 us
  waiting for transfers between devices  337 us (81%)
  matrix products  30.9 us (7%)
  other arithmetic  23.4 us (6%)
  between operations  15.2 us (4%)
  local copies, waits for them, and re-layouts  11.4 us (3%)
    all_gather x1, waiting for transfers between devices, per_device(): piece = lax.all_gather(weight_half, 'fsdp', axis=0, tiled=True)  156 us
    reduce_scatter x1, waiting for transfers between devices, per_device(): lax.psum_scatter((lax.dot_general(columns, cotangent, (((0,), (0,)), ((),...  154 us
    reduce_scatter x1, waiting for transfers between devices, per_device(): lax.psum_scatter(inner_frag.astype(jnp.bfloat16), 'rep', scatter_dimensio...  26 us
    dot_general x1, matrix products, per_device(): lax.dot_general(cotangent, piece, (((1,), (1,)), ((), ())), preferred_ele...  13.2 us
    sub x1, other arithmetic, adam_update(): weight - 0.1 * (first_hat / (jnp.sqrt(second_hat) + 1e-08) + 0.1 * weight)  12.7 us
    dot_general x1, matrix products, per_device(): lax.dot_general(columns, cotangent, (((0,), (0,)), ((), ())), preferred_e...  9.12 us
    dot_general x1, matrix products, per_device(): key_acc = jnp.dot(columns, piece, preferred_element_type=jnp.float32)  8.52 us
  transfers between devices with their start and end apart: 4, of which 4 were waited for; matrix products, arithmetic and copies ran while one was open for 8% of the time, Pallas kernels for 0%

commit v1 on v0

v1 whole, which is shorter than its diff:
```python
import functools
import math

import jax
import jax.numpy as jnp
from jax import lax
from jax.experimental import pallas as pl
from jax.experimental.pallas import tpu as pltpu
from jax.sharding import PartitionSpec as P

FRAGS = 4
ROUNDS = 8


def pair(x, axis, offset):
    size = lax.axis_size(axis)
    return lax.ppermute(x, axis, [(i, i ^ offset) for i in range(size)])


def adam_tile(groups, factor, scal_ref, hid_refs, cot_refs, weight_ref, first_ref, second_ref):
    grad = None
    for g in range(groups):
        part = lax.dot_general(
            hid_refs[g][...], cot_refs[g][...], (((0,), (0,)), ((), ())),
            preferred_element_type=jnp.float32,
        )
        part = (part * factor).astype(jnp.bfloat16).astype(jnp.float32)
        grad = part if grad is None else grad + part
    weight = weight_ref[...]
    first = 0.9 * first_ref[...] + 0.1 * grad
    second = 0.95 * second_ref[...] + 0.05 * grad * grad
    step = (first * scal_ref[0]) / (jnp.sqrt(second * scal_ref[1]) + 1e-08)
    return weight - 0.1 * (step + 0.1 * weight)


def adam_kernel(groups, factor, where_ref, scal_ref, *refs):
    hid_refs, cot_refs = refs[:groups], refs[groups : 2 * groups]
    weight_ref, first_ref, second_ref, out_ref = refs[2 * groups :]
    out_ref[...] = adam_tile(
        groups, factor, scal_ref, hid_refs, cot_refs, weight_ref, first_ref, second_ref
    ).astype(out_ref.dtype)


def adam_call(tokens, hid_peers, cots, weight, first, second, where, scal, factor, cols, by_frag, dtype, tile):
    rows, keys = weight.shape
    toks = tokens.shape[0]
    groups = len(cots)
    steps = rows // tile

    def col(w):
        return w[1] if by_frag else 0

    own = pl.BlockSpec((toks, tile), lambda i, w: (0, w[0] * steps + i))
    peer = pl.BlockSpec((toks, tile), lambda i, w: (0, i))
    cot = pl.BlockSpec((toks, cols), lambda i, w: (0, col(w)))
    state = pl.BlockSpec((tile, cols), lambda i, w: (i, col(w)))
    return pl.pallas_call(
        functools.partial(adam_kernel, groups, factor),
        grid_spec=pltpu.PrefetchScalarGridSpec(
            num_scalar_prefetch=1,
            grid=(steps,),
            in_specs=[pl.BlockSpec(memory_space=pltpu.SMEM), own]
            + [peer] * (groups - 1)
            + [cot] * groups
            + [state] * 3,
            out_specs=pl.BlockSpec((tile, cols), lambda i, w: (i, 0)),
        ),
        out_shape=jax.ShapeDtypeStruct((rows, cols), dtype),
        compiler_params=pltpu.CompilerParams(vmem_limit_bytes=32 * 1024 * 1024),
        cost_estimate=pl.CostEstimate(
            flops=2 * rows * cols * toks * groups,
            bytes_accessed=rows * cols * 16,
            transcendentals=2 * rows * cols,
        ),
    )(where, scal, tokens, *hid_peers, *cots, weight, first, second)


def per_device(
    hidden,
    key_cotangent,
    local_weight,
    adam_first,
    adam_second,
    outer_weight,
    outer_momentum,
    roster,
    step_count,
):
    tokens = hidden[0]
    cotangent = key_cotangent[0]
    weight = local_weight[0]
    outer_now = outer_weight[0]
    moment_now = outer_momentum[0]
    toks, width = tokens.shape
    rows, keys = weight.shape
    factor = 1.0 / math.sqrt(width)
    frag_cols = keys // FRAGS
    shards = lax.axis_size("fsdp")
    replicas = lax.axis_size("rep")
    shard = lax.axis_index("fsdp")
    replica = lax.axis_index("rep")
    offsets = list(range(1, shards))

    fragment = roster[step_count[0] // FRAGS % ROUNDS, step_count[0] % FRAGS]
    column = fragment * frag_cols
    steps_done = (step_count[0] + 1).astype(jnp.float32)
    scal = jnp.stack(
        [
            1.0 / (1.0 - jnp.power(jnp.float32(0.9), steps_done)),
            1.0 / (1.0 - jnp.power(jnp.float32(0.95), steps_done)),
        ]
    )
    where = jnp.stack([shard, fragment]).astype(jnp.int32)

    cots = [cotangent] + [pair(cotangent, "fsdp", m) for m in offsets]
    hid_peers = [
        pair(lax.dynamic_slice_in_dim(tokens, (shard ^ m) * rows, rows, 1), "fsdp", m)
        for m in offsets
    ]
    hid_own = lax.dynamic_slice_in_dim(tokens, shard * rows, rows, 1)

    weight_half = weight.astype(jnp.bfloat16)

    def back(cot):
        out = lax.dot_general(
            cot, weight_half, (((1,), (1,)), ((), ())), preferred_element_type=jnp.float32
        )
        return (out * factor).astype(jnp.bfloat16)

    def forward(hid):
        return jnp.dot(hid, weight_half, preferred_element_type=jnp.float32)

    back_blocks = [back(cotangent)] + [pair(back(cots[m]), "fsdp", m) for m in offsets]

    inner_frag = adam_call(
        tokens, hid_peers, cots, weight, adam_first[0], adam_second[0], where, scal, factor,
        frag_cols, True, jnp.bfloat16, 256,
    )
    chips = replicas // 2
    core, chip = replica % 2, replica // 2
    own_rows = rows // replicas
    blocks = inner_frag.reshape(chips, 2, own_rows, frag_cols)
    keep = lax.dynamic_index_in_dim(blocks, core, 1, keepdims=False)
    give = lax.dynamic_index_in_dim(blocks, 1 - core, 1, keepdims=False)
    pair_sum = keep.astype(jnp.float32) + pair(give, "rep", 1).astype(jnp.float32)
    pair_half = pair_sum.astype(jnp.bfloat16)
    total = lax.dynamic_index_in_dim(pair_sum, chip, 0, keepdims=False)
    for k in range(1, chips):
        block = lax.dynamic_index_in_dim(pair_half, chip ^ k, 0, keepdims=False)
        total = total + pair(block, "rep", 2 * k).astype(jnp.float32)
    outer_frag = lax.dynamic_slice_in_dim(outer_now, column, frag_cols, 1)
    moment_frag = lax.dynamic_slice_in_dim(moment_now, column, frag_cols, 1)
    pseudo = outer_frag - total / replicas
    moment_own = 0.9 * moment_frag + pseudo
    outer_own = outer_frag - 0.7 * (pseudo + 0.9 * moment_own)
    outer_half = outer_own.astype(jnp.bfloat16)
    same_core = jnp.zeros((chips, own_rows, frag_cols), jnp.bfloat16)
    same_core = lax.dynamic_update_index_in_dim(same_core, outer_half, chip, 0)
    for k in range(1, chips):
        same_core = lax.dynamic_update_index_in_dim(
            same_core, pair(outer_half, "rep", 2 * k), chip ^ k, 0
        )
    other_core = pair(same_core, "rep", 1)
    low = jnp.where(core == 0, same_core, other_core)
    high = jnp.where(core == 0, other_core, same_core)
    outer_back = jnp.stack([low, high], axis=1).reshape(rows, frag_cols).astype(jnp.float32)

    inner = adam_call(
        tokens, hid_peers, cots, weight, adam_first[0], adam_second[0], where, scal, factor,
        keys, False, jnp.float32, 256,
    )
    new_local = lax.dynamic_update_slice_in_dim(inner, outer_back, column, 1)

    key_acc = forward(hid_own)
    for m in offsets:
        part = forward(hid_peers[m - 1]).astype(jnp.bfloat16)
        key_acc = key_acc + pair(part, "fsdp", m).astype(jnp.float32)
    keys_out = (key_acc * factor).astype(jnp.bfloat16)

    back_out = jnp.zeros((toks, width), jnp.bfloat16)
    for m in range(shards):
        back_out = lax.dynamic_update_slice_in_dim(back_out, back_blocks[m], (shard ^ m) * rows, 1)

    outer_next = lax.dynamic_update_slice_in_dim(outer_now, outer_own, column, 1)
    moment_next = lax.dynamic_update_slice_in_dim(moment_now, moment_own, column, 1)
    return (keys_out[None], back_out[None], new_local[None], outer_next[None], moment_next[None])


def solution(mesh):
    in_specs = (
        P("rep", "fsdp", None),
        P("rep", "fsdp", None),
        P("rep", "fsdp", None),
        P("rep", "fsdp", None),
        P("rep", "fsdp", None),
        P("fsdp", "rep", None),
        P("fsdp", "rep", None),
        P(),
        P(),
    )
    out_specs = (
        P("rep", "fsdp", None),
        P("rep", "fsdp", None),
        P("rep", "fsdp", None),
        P("fsdp", "rep", None),
        P("fsdp", "rep", None),
    )
    return jax.shard_map(
        per_device, mesh=mesh, in_specs=in_specs, out_specs=out_specs, check_vma=False
    )
```

time: 418 us -> 131 us (0.31)
  waiting for transfers between devices: 337 us -> 31 us
  Pallas kernels: 0 us -> 26.5 us
  starting transfers between devices: 0.34 us -> 26.4 us
  other arithmetic: 23.4 us -> 9.81 us
  between operations: 15.2 us -> 2.5 us
  matrix products: 30.9 us -> 25.6 us
    reduce_scatter x2 -> x0, waiting for transfers between devices: 180 us -> none  [the longest x1 154 us: per_device(): lax.psum_scatter((lax.dot_general(columns, cotangent, (((0,), (0,)), ((),...]
    all_gather x2 -> x0, waiting for transfers between devices: 157 us -> none  [the longest x1 156 us: per_device(): piece = lax.all_gather(weight_half, 'fsdp', axis=0, tiled=True)]
    ppermute x0 -> x20, waiting for transfers between devices: none -> 31 us  [pair(): return lax.ppermute(x, axis, [(i, i ^ offset) for i in range(size)])]
    pallas_call x0 -> x2, Pallas kernels: none -> 26.5 us  [adam_call(): pl.pallas_call(functools.partial(adam_kernel, groups, factor), grid_spec=...]
    ppermute x0 -> x20, starting transfers between devices: none -> 26.4 us  [pair(): return lax.ppermute(x, axis, [(i, i ^ offset) for i in range(size)])]
    sub x1 -> x0, other arithmetic: 12.7 us -> none  [adam_update(): weight - 0.1 * (first_hat / (jnp.sqrt(second_hat) + 1e-08) + 0.1 * weight)]
    dot_general x3 -> x8, matrix products: 30.9 us -> 25.6 us  [the longest x4 13.9 us: back(): lax.dot_general(cot, weight_half, (((1,), (1,)), ((), ())), preferred_ele...]
  transfers between devices with their start and end apart: 4 -> 20, of which waited for: 4 -> 8; matrix products, arithmetic and copies ran while one was open for 8% -> 29% of each run, Pallas kernels for 0% -> 20%
where the time goes in v1:
time: 131 us; the launch traced here: 130 us
  waiting for transfers between devices  31 us (24%)
  Pallas kernels  26.5 us (20%)
  starting transfers between devices  26.4 us (20%)
  matrix products  25.6 us (20%)
  other arithmetic  9.81 us (7%)
  local copies, waits for them, and re-layouts  8.38 us (6%)
  between operations  2.5 us (2%)
    ppermute x20, waiting for transfers between devices, pair(): return lax.ppermute(x, axis, [(i, i ^ offset) for i in range(size)])  31 us
    pallas_call x2, Pallas kernels, adam_call(): pl.pallas_call(functools.partial(adam_kernel, groups, factor), grid_spec=...  26.5 us
    ppermute x20, starting transfers between devices, pair(): return lax.ppermute(x, axis, [(i, i ^ offset) for i in range(size)])  26.4 us
    dot_general x4, matrix products, back(): lax.dot_general(cot, weight_half, (((1,), (1,)), ((), ())), preferred_ele...  13.9 us
    dot_general x4, matrix products, forward(): return jnp.dot(hid, weight_half, preferred_element_type=jnp.float32)  11.6 us
    convert_element_type x1, other arithmetic, per_device(): weight_half = weight.astype(jnp.bfloat16)  6.06 us
    unnamed x28, local copies, waits for them, and re-layouts  4.85 us
  transfers between devices with their start and end apart: 20, of which 8 were waited for; matrix products, arithmetic and copies ran while one was open for 29% of the time, Pallas kernels for 20%

profile of v1, /device:TPU:0, one launch (start us, length us, event | category | flops | bytes accessed | tf_op | source)
XLA Modules:
  0.0 130.2 jit_solution(16674968344121854852)
XLA Ops:
  0.7 2.5 %copy.29 = f32[1,256,1024]{2,1,0:T(8,128)} copy(f32[1,256,1024]{2,1,0:T(8,128)} %param.14) | data formatting | bytes 2097152
  3.1 2.3 %copy.30 = f32[1,256,1024]{2,1,0:T(8,128)} copy(f32[1,256,1024]{2,1,0:T(8,128)} %param.15) | data formatting | bytes 2097152
  5.4 3.9 %collective-permute-start.10 = (bf16[192,1024]{1,0:T(8,128)(2,1)S(1)}, bf16[192,1024]{1,0:T(8,128)(2,1)}, u32[]{:S(2)}, u32[]{:S(2)}) collective-permute-start(bf16[192,1024]{1,0:T(8,128)(2,1)S(1)} %bitcast.128), channel_id=1, source_target_pairs={{0,3},{1,2},{2,1},{3,0},{4,7},{5,6},{6,5},{7,4},{8,11},{9,10},{10,... | collective-permute-start | bytes 1179656 | tf_op jit(solution)/shard_map/ppermute | solution.py:17
  9.3 0.5 collective-permute-start.8
  9.9 1.5 %dynamic-slice_bitcast_fusion.2 = (bf16[192,2048]{1,0:T(8,128)(2,1)}, bf16[192,2048]{1,0:T(8,128)(2,1)}, bf16[192,2048]{1,0:T(8,128)(2,1)}) fusion(bf16[1,192,8192]{2,1,0:T(8,128)(2,1)S(1)} %copy-done, s32[]{:T(128)S(6)} %select_n.90, s32[]{:T(128)S(6)} %select_n.91, s32[]{:T(128)S(6)} %select_n.92), kind=kLoop, calls=%fused_computation.29 | loop fusion | bytes 4718604 | tf_op jit(solution)/shard_map/dynamic_slice | solution.py:117
  11.4 2.0 %collective-permute-start = (bf16[192,2048]{1,0:T(8,128)(2,1)}, bf16[192,2048]{1,0:T(8,128)(2,1)}, u32[]{:S(2)}, u32[]{:S(2)}) collective-permute-start(bf16[192,2048]{1,0:T(8,128)(2,1)} %get-tuple-element.12), channel_id=1, source_target_pairs={{0,1},{1,0},{2,3},{3,2},{4,5},{5,4},{6,7},{7,6},{8,9},{9,8},{10,11... | collective-permute-start | bytes 2359304 | tf_op jit(solution)/shard_map/ppermute | solution.py:17
  13.4 1.5 %collective-permute-start.2 = (bf16[192,2048]{1,0:T(8,128)(2,1)}, bf16[192,2048]{1,0:T(8,128)(2,1)}, u32[]{:S(2)}, u32[]{:S(2)}) collective-permute-start(bf16[192,2048]{1,0:T(8,128)(2,1)} %get-tuple-element.13), channel_id=1, source_target_pairs={{0,2},{1,3},{2,0},{3,1},{4,6},{5,7},{6,4},{7,5},{8,10},{9,11},{10,... | collective-permute-start | bytes 2359304 | tf_op jit(solution)/shard_map/ppermute | solution.py:17
  14.9 6.1 %bitcast_convert_fusion = bf16[2048,1024]{1,0:T(8,128)(2,1)} fusion(f32[1,2048,1024]{2,1,0:T(8,128)} %param.11), kind=kLoop, calls=%fused_computation.55 | loop fusion | flops 2097152 | bytes 12582912 | tf_op jit(solution)/shard_map/convert_element_type | solution.py:122
  20.9 0.3 broadcast_in_dim.41
  21.3 4.9 %fusion.16 = bf16[1,192,8192]{2,1,0:T(8,128)(2,1)S(1)} fusion(bf16[1,192,8192]{2,1,0:T(8,128)(2,1)S(1)} %broadcast_in_dim.41, s32[]{:T(128)S(6)} %select_n.89, f32[1,2048,1024]{2,1,0:T(8,128)} %param.11, bf16[1,192,1024]{2,1,0:T(8,128)(2,1)S(1)} %copy-done.1), kind=kOutput, calls=%fused_computation.13 | convolution fusion | flops 808189952 | bytes 9568260 | tf_op jit(solution)/shard_map/dot_general | solution.py:125
  26.2 6.4 %fusion.2 = f32[192,1024]{1,0:T(8,128)} fusion(f32[1,2048,1024]{2,1,0:T(8,128)} %param.11, bf16[1,192,8192]{2,1,0:T(8,128)(2,1)S(1)} %copy-done, s32[]{:T(128)S(6)} %select_n.89), kind=kOutput, calls=%fused_computation.2 | convolution fusion | flops 807403520 | bytes 9961476 | tf_op jit(solution)/shard_map/dot_general | solution.py:131
  33.5 1.3 dynamic_slice.60
  34.8 0.1 pad_maximum_fusion.1.scal_ref
  34.8 0.6 pad_add_fusion.where_ref
  36.1 0.1 collective-permute-start.4
  36.2 4.0 %fusion.7 = bf16[192,2048]{1,0:T(8,128)(2,1)S(1)} fusion(bf16[192,1024]{1,0:T(8,128)(2,1)} %collective-permute-done.6.refs_5_, bf16[2048,1024]{1,0:T(8,128)(2,1)} %bitcast_convert_fusion), kind=kOutput, calls=%fused_computation.8 | convolution fusion | flops 806092800 | bytes 5373952 | tf_op jit(solution)/shard_map/dot_general | solution.py:125
  40.2 2.0 %collective-permute-start.7 = (bf16[192,2048]{1,0:T(8,128)(2,1)S(1)}, bf16[192,2048]{1,0:T(8,128)(2,1)S(1)}, u32[]{:S(2)}, u32[]{:S(2)}) collective-permute-start(bf16[192,2048]{1,0:T(8,128)(2,1)S(1)} %fusion.7), channel_id=1, source_target_pairs={{0,1},{1,0},{2,3},{3,2},{4,5},{5,4},{6,7},{7,6},{8,9},{9,8},{10,11... | collective-permute-start | bytes 2359304 | tf_op jit(solution)/shard_map/ppermute | solution.py:17
  42.2 2.5 %fusion.8 = bf16[192,2048]{1,0:T(8,128)(2,1)S(1)} fusion(bf16[192,1024]{1,0:T(8,128)(2,1)} %collective-permute-done.8.refs_6_, bf16[2048,1024]{1,0:T(8,128)(2,1)S(1)} %copy-done.3), kind=kOutput, calls=%fused_computation.9 | convolution fusion | flops 806092800 | bytes 5373952 | tf_op jit(solution)/shard_map/dot_general | solution.py:125
  44.8 1.6 %collective-permute-start.9 = (bf16[192,2048]{1,0:T(8,128)(2,1)S(1)}, bf16[192,2048]{1,0:T(8,128)(2,1)S(1)}, u32[]{:S(2)}, u32[]{:S(2)}) collective-permute-start(bf16[192,2048]{1,0:T(8,128)(2,1)S(1)} %fusion.8), channel_id=1, source_target_pairs={{0,2},{1,3},{2,0},{3,1},{4,6},{5,7},{6,4},{7,5},{8,10},{9,11},{10,... | collective-permute-start | bytes 2359304 | tf_op jit(solution)/shard_map/ppermute | solution.py:17
  46.4 2.5 %fusion.9 = bf16[192,2048]{1,0:T(8,128)(2,1)S(1)} fusion(bf16[192,1024]{1,0:T(8,128)(2,1)} %collective-permute-done.10.refs_7_, bf16[2048,1024]{1,0:T(8,128)(2,1)S(1)} %copy-done.3), kind=kOutput, calls=%fused_computation.10 | convolution fusion | flops 806092800 | bytes 5373952 | tf_op jit(solution)/shard_map/dot_general | solution.py:125
  48.9 0.4 collective-permute-start.11
  49.3 12.2 %collective-permute-done.4.refs_3_ = bf16[192,2048]{1,0:T(8,128)(2,1)S(1)} collective-permute-done((bf16[192,2048]{1,0:T(8,128)(2,1)}, bf16[192,2048]{1,0:T(8,128)(2,1)S(1)}, u32[]{:S(2)}, u32[]{:S(2)}) %collective-permute-start.4) | collective-permute-done | bytes 786464 | tf_op jit(solution)/shard_map/ppermute | solution.py:17
  61.5 8.6 %shard_map.129 = bf16[2048,256]{1,0:T(8,128)(2,1)S(1)} custom-call(s32[2]{0:T(128)S(1)} %pad_add_fusion.where_ref, f32[2]{0:T(128)S(1)} %pad_maximum_fusion.1.scal_ref, bf16[192,8192]{1,0:T(8,128)(2,1)S(1)} %bitcast.124, bf16[192,2048]{1,0:T(8,128)(2,1)} %collective-permute-done.refs_1_, bf16[192,2048]{1,0:T(8,128)(2,1)} %collective-permute-done.2.refs_2_, ...), custom_call_target="tpu_custom_call" | custom-call | flops 805306368 | bytes 8388608 | tf_op jit(solution)/shard_map/pallas_call | solution.py:57
  70.3 2.1 %convolution_convert_fusion.2 = bf16[192,1024]{1,0:T(8,128)(2,1)S(1)} fusion(bf16[192,2048]{1,0:T(8,128)(2,1)} %collective-permute-done.refs_1_, bf16[2048,1024]{1,0:T(8,128)(2,1)S(1)} %copy-done.3), kind=kOutput, calls=%fused_computation.19 | convolution fusion | flops 805502976 | bytes 5373952 | tf_op jit(solution)/shard_map/dot_general | solution.py:131
  72.4 2.1 %collective-permute-start.1 = (bf16[192,1024]{1,0:T(8,128)(2,1)S(1)}, bf16[192,1024]{1,0:T(8,128)(2,1)S(1)}, u32[]{:S(2)}, u32[]{:S(2)}) collective-permute-start(bf16[192,1024]{1,0:T(8,128)(2,1)S(1)} %convolution_convert_fusion.2), channel_id=1, source_target_pairs={{0,1},{1,0},{2,3},{3,2},{4,5},{5,4},{6,7},{7,6},{8,9},{9,8},{10,11... | collective-permute-start | bytes 1179656 | tf_op jit(solution)/shard_map/ppermute | solution.py:17
  74.5 1.0 convolution_convert_fusion
  75.4 2.1 %convolution_convert_fusion.1 = bf16[192,1024]{1,0:T(8,128)(2,1)S(1)} fusion(bf16[192,2048]{1,0:T(8,128)(2,1)} %collective-permute-done.2.refs_2_, bf16[2048,1024]{1,0:T(8,128)(2,1)S(1)} %copy-done.3), kind=kOutput, calls=%fused_computation.18 | convolution fusion | flops 805502976 | bytes 5373952 | tf_op jit(solution)/shard_map/dot_general | solution.py:131
  77.6 17.9 %shard_map.128 = f32[2048,1024]{1,0:T(8,128)} custom-call(s32[2]{0:T(128)S(1)} %pad_add_fusion.where_ref, f32[2]{0:T(128)S(1)} %pad_maximum_fusion.1.scal_ref, bf16[192,8192]{1,0:T(8,128)(2,1)S(1)} %bitcast.125, bf16[192,2048]{1,0:T(8,128)(2,1)} %collective-permute-done.refs_1_, bf16[192,2048]{1,0:T(8,128)(2,1)} %collective-permute-done.2.refs_2_, ...), custom_call_target="tpu_custom_call" | custom-call | flops 3221225472 | bytes 33554432 | tf_op jit(solution)/shard_map/pallas_call | solution.py:57
  95.6 0.1 fusion.31
  95.8 1.6 %collective-permute-start.13 = (bf16[256,256]{1,0:T(8,128)(2,1)S(1)}, bf16[256,256]{1,0:T(8,128)(2,1)S(1)}, u32[]{:S(2)}, u32[]{:S(2)}) collective-permute-start(bf16[256,256]{1,0:T(8,128)(2,1)S(1)} %get-tuple-element.17), channel_id=1, source_target_pairs={{0,8},{4,12},{8,0},{12,4},{16,24},{20,28},{24,16},{28,20},{1,9},{5... | collective-permute-start | bytes 393224 | tf_op jit(solution)/shard_map/ppermute | solution.py:17
  97.4 2.5 %collective-permute-start.15 = (bf16[256,256]{1,0:T(8,128)(2,1)S(1)}, bf16[256,256]{1,0:T(8,128)(2,1)S(1)}, u32[]{:S(2)}, u32[]{:S(2)}) collective-permute-start(bf16[256,256]{1,0:T(8,128)(2,1)S(1)} %get-tuple-element.18), channel_id=1, source_target_pairs={{0,24},{4,28},{8,16},{12,20},{16,8},{20,12},{24,0},{28,4},{1,25},{... | collective-permute-start | bytes 393224 | tf_op jit(solution)/shard_map/ppermute | solution.py:17
  99.9 0.1 collective-permute-start.14
  100.1 1.4 %collective-permute-done.13 = bf16[256,256]{1,0:T(8,128)(2,1)S(1)} collective-permute-done((bf16[256,256]{1,0:T(8,128)(2,1)S(1)}, bf16[256,256]{1,0:T(8,128)(2,1)S(1)}, u32[]{:S(2)}, u32[]{:S(2)}) %collective-permute-start.13) | collective-permute-done | bytes 131104 | tf_op jit(solution)/shard_map/ppermute | solution.py:17
  101.5 1.5 %collective-permute-start.3 = (bf16[192,1024]{1,0:T(8,128)(2,1)S(1)}, bf16[192,1024]{1,0:T(8,128)(2,1)S(1)}, u32[]{:S(2)}, u32[]{:S(2)}) collective-permute-start(bf16[192,1024]{1,0:T(8,128)(2,1)S(1)} %convolution_convert_fusion.1), channel_id=1, source_target_pairs={{0,2},{1,3},{2,0},{3,1},{4,6},{5,7},{6,4},{7,5},{8,10},{9,11},{10,... | collective-permute-start | bytes 1179656 | tf_op jit(solution)/shard_map/ppermute | solution.py:17
  103.0 4.2 %collective-permute-done.15 = bf16[256,256]{1,0:T(8,128)(2,1)S(1)} collective-permute-done((bf16[256,256]{1,0:T(8,128)(2,1)S(1)}, bf16[256,256]{1,0:T(8,128)(2,1)S(1)}, u32[]{:S(2)}, u32[]{:S(2)}) %collective-permute-start.15) | collective-permute-done | bytes 131104 | tf_op jit(solution)/shard_map/ppermute | solution.py:17
  107.1 1.5 %collective-permute-start.5 = (bf16[192,1024]{1,0:T(8,128)(2,1)S(1)}, bf16[192,1024]{1,0:T(8,128)(2,1)S(1)}, u32[]{:S(2)}, u32[]{:S(2)}) collective-permute-start(bf16[192,1024]{1,0:T(8,128)(2,1)S(1)} %convolution_convert_fusion), channel_id=1, source_target_pairs={{0,3},{1,2},{2,1},{3,0},{4,7},{5,6},{6,5},{7,4},{8,11},{9,10},{10,... | collective-permute-start | bytes 1179656 | tf_op jit(solution)/shard_map/ppermute | solution.py:17
  108.6 3.4 %collective-permute-done.14 = bf16[256,256]{1,0:T(8,128)(2,1)S(1)} collective-permute-done((bf16[256,256]{1,0:T(8,128)(2,1)S(1)}, bf16[256,256]{1,0:T(8,128)(2,1)S(1)}, u32[]{:S(2)}, u32[]{:S(2)}) %collective-permute-start.14) | collective-permute-done | bytes 131104 | tf_op jit(solution)/shard_map/ppermute | solution.py:17
  112.1 0.1 bitcast_add_fusion
  112.2 0.1 bitcast_dynamic-update-slice_fusion.8
  112.5 3.2 %collective-permute-start.17 = (bf16[256,256]{1,0:T(8,128)(2,1)S(1)}, bf16[256,256]{1,0:T(8,128)(2,1)S(1)}, u32[]{:S(2)}, u32[]{:S(2)}) collective-permute-start(bf16[256,256]{1,0:T(8,128)(2,1)S(1)} %get-tuple-element.8), channel_id=1, source_target_pairs={{0,16},{4,20},{8,24},{12,28},{16,0},{20,4},{24,8},{28,12},{1,17},{... | collective-permute-start | bytes 393224 | tf_op jit(solution)/shard_map/ppermute | solution.py:17
  115.8 3.9 %collective-permute-done.16 = bf16[256,256]{1,0:T(8,128)(2,1)S(1)} collective-permute-done((bf16[256,256]{1,0:T(8,128)(2,1)S(1)}, bf16[256,256]{1,0:T(8,128)(2,1)S(1)}, u32[]{:S(2)}, u32[]{:S(2)}) %collective-permute-start.16) | collective-permute-done | bytes 131104 | tf_op jit(solution)/shard_map/ppermute | solution.py:17
  119.7 1.7 %collective-permute-start.18 = (bf16[256,256]{1,0:T(8,128)(2,1)S(1)}, bf16[256,256]{1,0:T(8,128)(2,1)S(1)}, u32[]{:S(2)}, u32[]{:S(2)}) collective-permute-start(bf16[256,256]{1,0:T(8,128)(2,1)S(1)} %get-tuple-element.8), channel_id=1, source_target_pairs={{0,24},{4,28},{8,16},{12,20},{16,8},{20,12},{24,0},{28,4},{1,25},{... | collective-permute-start | bytes 393224 | tf_op jit(solution)/shard_map/ppermute | solution.py:17
  121.4 0.5 collective-permute-done.17
  121.9 4.7 %collective-permute-done.18 = bf16[256,256]{1,0:T(8,128)(2,1)S(1)} collective-permute-done((bf16[256,256]{1,0:T(8,128)(2,1)S(1)}, bf16[256,256]{1,0:T(8,128)(2,1)S(1)}, u32[]{:S(2)}, u32[]{:S(2)}) %collective-permute-start.18) | collective-permute-done | bytes 131104 | tf_op jit(solution)/shard_map/ppermute | solution.py:17
  126.7 1.0 fusion.23
  127.8 0.8 collective-permute-done.19
  128.6 0.1 pad_maximum_fusion
  128.7 1.5 %convert_dynamic-update-slice_fusion = f32[1,2048,1024]{2,1,0:T(8,128)} fusion(f32[1,2048,1024]{2,1,0:T(8,128)} %bitcast.137, s32[]{:T(128)S(6)} %select_n.100, bf16[1,2048,256]{2,1,0:T(8,128)(2,1)S(1)} %bitcast.138), kind=kLoop, calls=%fused_computation.14 | loop fusion | flops 524288 | bytes 3145732 | tf_op jit(solution)/shard_map/dynamic_update_slice | solution.py:172
  (54 shorter events, 0.9 us)
Async XLA Ops:
  0.6 9.3 %copy-start = (bf16[1,192,8192]{2,1,0:T(8,128)(2,1)S(1)}, bf16[1,192,8192]{2,1,0:T(8,128)(2,1)}, u32[]{:S(2)}) copy-start(bf16[1,192,8192]{2,1,0:T(8,128)(2,1)} %param.9) | copy-start | bytes 9437188
  0.6 4.8 %copy-start.1 = (bf16[1,192,1024]{2,1,0:T(8,128)(2,1)S(1)}, bf16[1,192,1024]{2,1,0:T(8,128)(2,1)}, u32[]{:S(2)}) copy-start(bf16[1,192,1024]{2,1,0:T(8,128)(2,1)} %param.10) | copy-start | bytes 1179652
  5.4 39.3 %collective-permute-start.10 = (bf16[192,1024]{1,0:T(8,128)(2,1)S(1)}, bf16[192,1024]{1,0:T(8,128)(2,1)}, u32[]{:S(2)}, u32[]{:S(2)}) collective-permute-start(bf16[192,1024]{1,0:T(8,128)(2,1)S(1)} %bitcast.128), channel_id=1, source_target_pairs={{0,3},{1,2},{2,1},{3,0},{4,7},{5,6},{6,5},{7,4},{8,11},{9,10},{10,... | collective-permute-start | bytes 1179656 | tf_op jit(solution)/shard_map/ppermute | solution.py:17
  9.3 30.9 %collective-permute-start.8 = (bf16[192,1024]{1,0:T(8,128)(2,1)S(1)}, bf16[192,1024]{1,0:T(8,128)(2,1)}, u32[]{:S(2)}, u32[]{:S(2)}) collective-permute-start(bf16[192,1024]{1,0:T(8,128)(2,1)S(1)} %bitcast.129), channel_id=1, source_target_pairs={{0,2},{1,3},{2,0},{3,1},{4,6},{5,7},{6,4},{7,5},{8,10},{9,11},{10,... | collective-permute-start | bytes 1179656 | tf_op jit(solution)/shard_map/ppermute | solution.py:17
  9.8 26.3 %collective-permute-start.6 = (bf16[192,1024]{1,0:T(8,128)(2,1)S(1)}, bf16[192,1024]{1,0:T(8,128)(2,1)}, u32[]{:S(2)}, u32[]{:S(2)}) collective-permute-start(bf16[192,1024]{1,0:T(8,128)(2,1)S(1)} %bitcast.130), channel_id=1, source_target_pairs={{0,1},{1,0},{2,3},{3,2},{4,5},{5,4},{6,7},{7,6},{8,9},{9,8},{10,11... | collective-permute-start | bytes 1179656 | tf_op jit(solution)/shard_map/ppermute | solution.py:17
  11.4 37.5 %collective-permute-start = (bf16[192,2048]{1,0:T(8,128)(2,1)}, bf16[192,2048]{1,0:T(8,128)(2,1)}, u32[]{:S(2)}, u32[]{:S(2)}) collective-permute-start(bf16[192,2048]{1,0:T(8,128)(2,1)} %get-tuple-element.12), channel_id=1, source_target_pairs={{0,1},{1,0},{2,3},{3,2},{4,5},{5,4},{6,7},{7,6},{8,9},{9,8},{10,11... | collective-permute-start | bytes 2359304 | tf_op jit(solution)/shard_map/ppermute | solution.py:17
  13.4 35.9 %collective-permute-start.2 = (bf16[192,2048]{1,0:T(8,128)(2,1)}, bf16[192,2048]{1,0:T(8,128)(2,1)}, u32[]{:S(2)}, u32[]{:S(2)}) collective-permute-start(bf16[192,2048]{1,0:T(8,128)(2,1)} %get-tuple-element.13), channel_id=1, source_target_pairs={{0,2},{1,3},{2,0},{3,1},{4,6},{5,7},{6,4},{7,5},{8,10},{9,11},{10,... | collective-permute-start | bytes 2359304 | tf_op jit(solution)/shard_map/ppermute | solution.py:17
  26.2 6.4 %copy-start.4 = (bf16[1,192,8192]{2,1,0:T(8,128)(2,1)}, bf16[1,192,8192]{2,1,0:T(8,128)(2,1)S(1)}, u32[]{:S(2)}) copy-start(bf16[1,192,8192]{2,1,0:T(8,128)(2,1)S(1)} %fusion.16) | copy-start | bytes 9437188
  36.1 6.1 %copy-start.3 = (bf16[2048,1024]{1,0:T(8,128)(2,1)S(1)}, bf16[2048,1024]{1,0:T(8,128)(2,1)}, u32[]{:S(2)}) copy-start(bf16[2048,1024]{1,0:T(8,128)(2,1)} %bitcast_convert_fusion) | copy-start | bytes 12582916
  36.1 25.4 %collective-permute-start.4 = (bf16[192,2048]{1,0:T(8,128)(2,1)}, bf16[192,2048]{1,0:T(8,128)(2,1)S(1)}, u32[]{:S(2)}, u32[]{:S(2)}) collective-permute-start(bf16[192,2048]{1,0:T(8,128)(2,1)} %get-tuple-element.14), channel_id=1, source_target_pairs={{0,3},{1,2},{2,1},{3,0},{4,7},{5,6},{6,5},{7,4},{8,11},{9,10},{10,... | collective-permute-start | bytes 2359304 | tf_op jit(solution)/shard_map/ppermute | solution.py:17
  36.2 25.3 %slice-start = ((s8[8388608]{0:T(1024)(128)(4,1)}), s8[4194304]{0:T(1024)(128)(4,1)S(1)}, s32[]{:S(2)}) async-start(s8[8388608]{0:T(1024)(128)(4,1)} %bitcast.120), calls=%async_computation | async-start | bytes 8388608
  40.2 21.3 %slice-start.1 = ((s8[8388608]{0:T(1024)(128)(4,1)}), s8[4194304]{0:T(1024)(128)(4,1)S(1)}, s32[]{:S(2)}) async-start(s8[8388608]{0:T(1024)(128)(4,1)} %bitcast.120), calls=%async_computation.1 | async-start | bytes 8388608
  40.2 55.3 %collective-permute-start.7 = (bf16[192,2048]{1,0:T(8,128)(2,1)S(1)}, bf16[192,2048]{1,0:T(8,128)(2,1)S(1)}, u32[]{:S(2)}, u32[]{:S(2)}) collective-permute-start(bf16[192,2048]{1,0:T(8,128)(2,1)S(1)} %fusion.7), channel_id=1, source_target_pairs={{0,1},{1,0},{2,3},{3,2},{4,5},{5,4},{6,7},{7,6},{8,9},{9,8},{10,11... | collective-permute-start | bytes 2359304 | tf_op jit(solution)/shard_map/ppermute | solution.py:17
  44.8 55.1 %collective-permute-start.9 = (bf16[192,2048]{1,0:T(8,128)(2,1)S(1)}, bf16[192,2048]{1,0:T(8,128)(2,1)S(1)}, u32[]{:S(2)}, u32[]{:S(2)}) collective-permute-start(bf16[192,2048]{1,0:T(8,128)(2,1)S(1)} %fusion.8), channel_id=1, source_target_pairs={{0,2},{1,3},{2,0},{3,1},{4,6},{5,7},{6,4},{7,5},{8,10},{9,11},{10,... | collective-permute-start | bytes 2359304 | tf_op jit(solution)/shard_map/ppermute | solution.py:17
  48.9 63.5 %collective-permute-start.11 = (bf16[192,2048]{1,0:T(8,128)(2,1)S(1)}, bf16[192,2048]{1,0:T(8,128)(2,1)S(1)}, u32[]{:S(2)}, u32[]{:S(2)}) collective-permute-start(bf16[192,2048]{1,0:T(8,128)(2,1)S(1)} %fusion.9), channel_id=1, source_target_pairs={{0,3},{1,2},{2,1},{3,0},{4,7},{5,6},{6,5},{7,4},{8,11},{9,10},{10,... | collective-permute-start | bytes 2359304 | tf_op jit(solution)/shard_map/ppermute | solution.py:17
  70.2 25.4 %collective-permute-start.12 = (bf16[4,256,256]{2,1,0:T(8,128)(2,1)S(1)}, bf16[4,256,256]{2,1,0:T(8,128)(2,1)S(1)}, u32[]{:S(2)}, u32[]{:S(2)}) collective-permute-start(bf16[4,256,256]{2,1,0:T(8,128)(2,1)S(1)} %dynamic-slice_bitcast_fusion.3), channel_id=1, source_target_pairs={{0,4},{4,0},{8,12},{12,8},{16,20},{20,16},{24,28},{28,24},{1,5},{5... | collective-permute-start | bytes 1572872 | tf_op jit(solution)/shard_map/ppermute | solution.py:17
  72.4 54.3 %collective-permute-start.1 = (bf16[192,1024]{1,0:T(8,128)(2,1)S(1)}, bf16[192,1024]{1,0:T(8,128)(2,1)S(1)}, u32[]{:S(2)}, u32[]{:S(2)}) collective-permute-start(bf16[192,1024]{1,0:T(8,128)(2,1)S(1)} %convolution_convert_fusion.2), channel_id=1, source_target_pairs={{0,1},{1,0},{2,3},{3,2},{4,5},{5,4},{6,7},{7,6},{8,9},{9,8},{10,11... | collective-permute-start | bytes 1179656 | tf_op jit(solution)/shard_map/ppermute | solution.py:17
  77.6 17.9 %copy-start.5 = (bf16[1,192,8192]{2,1,0:T(8,128)(2,1)S(1)}, bf16[1,192,8192]{2,1,0:T(8,128)(2,1)}, u32[]{:S(2)}) copy-start(bf16[1,192,8192]{2,1,0:T(8,128)(2,1)} %copy-done.4) | copy-start | bytes 9437188
  95.5 16.6 %copy-start.7 = (f32[1,256,1024]{2,1,0:T(8,128)S(1)}, f32[1,256,1024]{2,1,0:T(8,128)}, u32[]{:S(2)}) copy-start(f32[1,256,1024]{2,1,0:T(8,128)} %copy.29) | copy-start | bytes 3145732
  95.5 16.6 %copy-start.9 = (f32[1,256,1024]{2,1,0:T(8,128)S(1)}, f32[1,256,1024]{2,1,0:T(8,128)}, u32[]{:S(2)}) copy-start(f32[1,256,1024]{2,1,0:T(8,128)} %copy.30) | copy-start | bytes 3145732
  95.8 30.9 %copy-start.2 = (f32[192,1024]{1,0:T(8,128)S(1)}, f32[192,1024]{1,0:T(8,128)}, u32[]{:S(2)}) copy-start(f32[192,1024]{1,0:T(8,128)} %fusion.2) | copy-start | bytes 2359300
  95.8 5.7 %collective-permute-start.13 = (bf16[256,256]{1,0:T(8,128)(2,1)S(1)}, bf16[256,256]{1,0:T(8,128)(2,1)S(1)}, u32[]{:S(2)}, u32[]{:S(2)}) collective-permute-start(bf16[256,256]{1,0:T(8,128)(2,1)S(1)} %get-tuple-element.17), channel_id=1, source_target_pairs={{0,8},{4,12},{8,0},{12,4},{16,24},{20,28},{24,16},{28,20},{1,9},{5... | collective-permute-start | bytes 393224 | tf_op jit(solution)/shard_map/ppermute | solution.py:17
  97.4 9.7 %collective-permute-start.15 = (bf16[256,256]{1,0:T(8,128)(2,1)S(1)}, bf16[256,256]{1,0:T(8,128)(2,1)S(1)}, u32[]{:S(2)}, u32[]{:S(2)}) collective-permute-start(bf16[256,256]{1,0:T(8,128)(2,1)S(1)} %get-tuple-element.18), channel_id=1, source_target_pairs={{0,24},{4,28},{8,16},{12,20},{16,8},{20,12},{24,0},{28,4},{1,25},{... | collective-permute-start | bytes 393224 | tf_op jit(solution)/shard_map/ppermute | solution.py:17
  99.9 12.1 %collective-permute-start.14 = (bf16[256,256]{1,0:T(8,128)(2,1)S(1)}, bf16[256,256]{1,0:T(8,128)(2,1)S(1)}, u32[]{:S(2)}, u32[]{:S(2)}) collective-permute-start(bf16[256,256]{1,0:T(8,128)(2,1)S(1)} %get-tuple-element.19), channel_id=1, source_target_pairs={{0,16},{4,20},{8,24},{12,28},{16,0},{20,4},{24,8},{28,12},{1,17},{... | collective-permute-start | bytes 393224 | tf_op jit(solution)/shard_map/ppermute | solution.py:17
  101.5 25.2 %collective-permute-start.3 = (bf16[192,1024]{1,0:T(8,128)(2,1)S(1)}, bf16[192,1024]{1,0:T(8,128)(2,1)S(1)}, u32[]{:S(2)}, u32[]{:S(2)}) collective-permute-start(bf16[192,1024]{1,0:T(8,128)(2,1)S(1)} %convolution_convert_fusion.1), channel_id=1, source_target_pairs={{0,2},{1,3},{2,0},{3,1},{4,6},{5,7},{6,4},{7,5},{8,10},{9,11},{10,... | collective-permute-start | bytes 1179656 | tf_op jit(solution)/shard_map/ppermute | solution.py:17
  107.1 19.5 %collective-permute-start.5 = (bf16[192,1024]{1,0:T(8,128)(2,1)S(1)}, bf16[192,1024]{1,0:T(8,128)(2,1)S(1)}, u32[]{:S(2)}, u32[]{:S(2)}) collective-permute-start(bf16[192,1024]{1,0:T(8,128)(2,1)S(1)} %convolution_convert_fusion), channel_id=1, source_target_pairs={{0,3},{1,2},{2,1},{3,0},{4,7},{5,6},{6,5},{7,4},{8,11},{9,10},{10,... | collective-permute-start | bytes 1179656 | tf_op jit(solution)/shard_map/ppermute | solution.py:17
  112.3 7.3 %collective-permute-start.16 = (bf16[256,256]{1,0:T(8,128)(2,1)S(1)}, bf16[256,256]{1,0:T(8,128)(2,1)S(1)}, u32[]{:S(2)}, u32[]{:S(2)}) collective-permute-start(bf16[256,256]{1,0:T(8,128)(2,1)S(1)} %get-tuple-element.8), channel_id=1, source_target_pairs={{0,8},{4,12},{8,0},{12,4},{16,24},{20,28},{24,16},{28,20},{1,9},{5... | collective-permute-start | bytes 393224 | tf_op jit(solution)/shard_map/ppermute | solution.py:17
  112.5 16.2 %copy-start.6 = (bf16[1,192,8192]{2,1,0:T(8,128)(2,1)}, bf16[1,192,8192]{2,1,0:T(8,128)(2,1)S(1)}, u32[]{:S(2)}) copy-start(bf16[1,192,8192]{2,1,0:T(8,128)(2,1)S(1)} %bitcast_dynamic-update-slice_fusion) | copy-start | bytes 9437188
  112.5 9.3 %collective-permute-start.17 = (bf16[256,256]{1,0:T(8,128)(2,1)S(1)}, bf16[256,256]{1,0:T(8,128)(2,1)S(1)}, u32[]{:S(2)}, u32[]{:S(2)}) collective-permute-start(bf16[256,256]{1,0:T(8,128)(2,1)S(1)} %get-tuple-element.8), channel_id=1, source_target_pairs={{0,16},{4,20},{8,24},{12,28},{16,0},{20,4},{24,8},{28,12},{1,17},{... | collective-permute-start | bytes 393224 | tf_op jit(solution)/shard_map/ppermute | solution.py:17
  119.7 6.9 %collective-permute-start.18 = (bf16[256,256]{1,0:T(8,128)(2,1)S(1)}, bf16[256,256]{1,0:T(8,128)(2,1)S(1)}, u32[]{:S(2)}, u32[]{:S(2)}) collective-permute-start(bf16[256,256]{1,0:T(8,128)(2,1)S(1)} %get-tuple-element.8), channel_id=1, source_target_pairs={{0,24},{4,28},{8,16},{12,20},{16,8},{20,12},{24,0},{28,4},{1,25},{... | collective-permute-start | bytes 393224 | tf_op jit(solution)/shard_map/ppermute | solution.py:17
  126.6 2.0 %collective-permute-start.19 = (bf16[4,256,256]{2,1,0:T(8,128)(2,1)S(1)}, bf16[4,256,256]{2,1,0:T(8,128)(2,1)S(1)}, u32[]{:S(2)}, u32[]{:S(2)}) collective-permute-start(bf16[4,256,256]{2,1,0:T(8,128)(2,1)S(1)} %bitcast_dynamic-update-slice_fusion.5), channel_id=1, source_target_pairs={{0,4},{4,0},{8,12},{12,8},{16,20},{20,16},{24,28},{28,24},{1,5},{5... | collective-permute-start | bytes 1572872 | tf_op jit(solution)/shard_map/ppermute | solution.py:17
  127.7 2.5 %copy-start.8 = (f32[1,256,1024]{2,1,0:T(8,128)}, f32[1,256,1024]{2,1,0:T(8,128)S(1)}, u32[]{:S(2)}) copy-start(f32[1,256,1024]{2,1,0:T(8,128)S(1)} %get-tuple-element.21) | copy-start | bytes 3145732
  127.7 2.5 %copy-start.10 = (f32[1,256,1024]{2,1,0:T(8,128)}, f32[1,256,1024]{2,1,0:T(8,128)S(1)}, u32[]{:S(2)}) copy-start(f32[1,256,1024]{2,1,0:T(8,128)S(1)} %get-tuple-element.20) | copy-start | bytes 3145732

commit v2 on v0

v2 whole, which is shorter than its diff:
```python
import functools
import math

import jax
import jax.numpy as jnp
from jax import lax
from jax.experimental import pallas as pl
from jax.experimental.pallas import tpu as pltpu
from jax.sharding import PartitionSpec as P

FRAGS = 4
ROUNDS = 8
MIB = 1024 * 1024
VMEM = 48 * MIB
SMALL = pl.CostEstimate(flops=1, bytes_accessed=1, transcendentals=0)


def pair(x, axis, offset):
    size = lax.axis_size(axis)
    return lax.ppermute(x, axis, [(i, i ^ offset) for i in range(size)])


def after(x, *others):
    return lax.optimization_barrier((x, *others))[0]


def row_dot(hid, cot, factor):
    part = lax.dot_general(
        hid, cot, (((0,), (0,)), ((), ())), preferred_element_type=jnp.float32
    )
    return (part * factor).astype(jnp.bfloat16).astype(jnp.float32)


def dot_keys(hid, weight):
    return jnp.dot(hid, weight, preferred_element_type=jnp.float32)


def dot_back(cot, weight, factor):
    out = lax.dot_general(
        cot, weight, (((1,), (1,)), ((), ())), preferred_element_type=jnp.float32
    )
    return (out * factor).astype(jnp.bfloat16)


def add_keys(ref, value):
    @pl.when(pl.program_id(0) == 0)
    def _():
        ref[...] = value

    @pl.when(pl.program_id(0) > 0)
    def _():
        ref[...] += value


def own_kernel(factor, where_ref, tokens_ref, cot_ref, weight_ref, half_ref, back_ref, keys_ref, frag_ref):
    cols = frag_ref.shape[1]
    frag_ref[...] = weight_ref[:, pl.ds(pl.multiple_of(where_ref[1] * cols, cols), cols)]
    half = weight_ref[...].astype(jnp.bfloat16)
    half_ref[...] = half
    back_ref[...] = dot_back(cot_ref[...], half, factor)
    add_keys(keys_ref, dot_keys(tokens_ref[...], half))


def own_call(tokens, cot, weight, where, factor, tile, frag_cols):
    rows, keys = weight.shape
    toks, width = tokens.shape
    steps = rows // tile
    here = pl.BlockSpec((toks, tile), lambda i, w: (0, w[0] * steps + i))
    block = pl.BlockSpec((tile, keys), lambda i, w: (i, 0))
    whole = pl.BlockSpec((toks, keys), lambda i, w: (0, 0))
    return pl.pallas_call(
        functools.partial(own_kernel, factor),
        grid_spec=pltpu.PrefetchScalarGridSpec(
            num_scalar_prefetch=1,
            grid=(steps,),
            in_specs=[here, whole, block],
            out_specs=[block, here, whole, pl.BlockSpec((tile, frag_cols), lambda i, w: (i, 0))],
        ),
        out_shape=[
            jax.ShapeDtypeStruct((rows, keys), jnp.bfloat16),
            jax.ShapeDtypeStruct((toks, width), jnp.bfloat16),
            jax.ShapeDtypeStruct((toks, keys), jnp.float32),
            jax.ShapeDtypeStruct((rows, frag_cols), jnp.float32),
        ],
        compiler_params=pltpu.CompilerParams(vmem_limit_bytes=VMEM),
        cost_estimate=SMALL,
    )(where, tokens, cot, weight)


def cut_kernel(count, where_ref, *refs):
    for i in range(count):
        refs[count + i][...] = refs[i][...]


def cut_call(where, arrays, cols):
    count = len(arrays)
    rows = arrays[0].shape[0]
    return pl.pallas_call(
        functools.partial(cut_kernel, count),
        grid_spec=pltpu.PrefetchScalarGridSpec(
            num_scalar_prefetch=1,
            grid=(2,),
            in_specs=[pl.BlockSpec((rows // 2, cols), lambda i, w: (i, w[1]))] * count,
            out_specs=[pl.BlockSpec((rows // 2, cols), lambda i, w: (i, 0))] * count,
        ),
        out_shape=[jax.ShapeDtypeStruct((rows, cols), x.dtype) for x in arrays],
        compiler_params=pltpu.CompilerParams(vmem_limit_bytes=VMEM),
        cost_estimate=SMALL,
    )(where, *arrays)


def pack(outs, accs, hids, cots, weight, factor, step, steps):
    toks = hids[0].shape[0]
    tile = weight.shape[0]
    rows = tile * steps
    at = pl.ds(pl.multiple_of(step * tile, tile), tile)
    back = dot_back(jnp.concatenate(cots, axis=0), weight, factor)
    part = dot_keys(jnp.concatenate(hids, axis=0), weight)
    for g, (out, acc) in enumerate(zip(outs, accs)):
        mine = slice(g * toks, (g + 1) * toks)
        out[:, at] = back[mine]
        add_keys(acc, part[mine])

    @pl.when(step == steps - 1)
    def _():
        for out, acc in zip(outs, accs):
            out[:, rows:] = acc[...].astype(out.dtype)


def near_kernel(groups, factor, steps, where_ref, *refs):
    hids, cots, weight_ref = refs[:groups], refs[groups : 2 * groups], refs[2 * groups]
    all_ref, frag_ref, *outs = refs[2 * groups + 1 :]
    total = row_dot(hids[0][...], cots[0][...], factor)
    for g in range(1, groups):
        total = total + row_dot(hids[g][...], cots[g][...], factor)
    all_ref[...] = total
    cols = frag_ref.shape[1]
    frag_ref[...] = all_ref[:, pl.ds(pl.multiple_of(where_ref[1] * cols, cols), cols)]
    peers = groups - 1
    pack(
        outs[:peers], outs[peers:], [h[...] for h in hids[1:]], [c[...] for c in cots[1:]],
        weight_ref[...], factor, pl.program_id(0), steps,
    )


def near_call(tokens, hids, cots, weight_half, where, factor, tile, frag_cols):
    rows, keys = weight_half.shape
    toks = tokens.shape[0]
    groups = len(cots)
    peers = groups - 1
    steps = rows // tile
    block = pl.BlockSpec((tile, keys), lambda i, w: (i, 0))
    whole = pl.BlockSpec((toks, keys), lambda i, w: (0, 0))
    column = pl.BlockSpec((toks, tile), lambda i, w: (0, i))
    out = pl.pallas_call(
        functools.partial(near_kernel, groups, factor, steps),
        grid_spec=pltpu.PrefetchScalarGridSpec(
            num_scalar_prefetch=1,
            grid=(steps,),
            in_specs=[pl.BlockSpec((toks, tile), lambda i, w: (0, w[0] * steps + i))]
            + [column] * peers
            + [whole] * groups
            + [block],
            out_specs=[block, pl.BlockSpec((tile, frag_cols), lambda i, w: (i, 0))]
            + [pl.BlockSpec((toks, rows + keys), lambda i, w: (0, 0))] * peers,
            scratch_shapes=[pltpu.VMEM((toks, keys), jnp.float32)] * peers,
        ),
        out_shape=[
            jax.ShapeDtypeStruct((rows, keys), jnp.float32),
            jax.ShapeDtypeStruct((rows, frag_cols), jnp.float32),
        ]
        + [jax.ShapeDtypeStruct((toks, rows + keys), jnp.bfloat16)] * peers,
        compiler_params=pltpu.CompilerParams(vmem_limit_bytes=VMEM),
        cost_estimate=SMALL,
    )(where, tokens, *hids, *cots, weight_half)
    return out[0], out[1], list(out[2:])


def last_kernel(factor, steps, low_ref, high_ref, cot_ref, weight_ref, out_ref, acc_ref):
    step = pl.program_id(0)
    hid = jnp.where(step < steps // 2, low_ref[...], high_ref[...])
    pack([out_ref], [acc_ref], [hid], [cot_ref[...]], weight_ref[...], factor, step, steps)


def last_call(hid_low, hid_high, cot, weight_half, factor, tile):
    rows, keys = weight_half.shape
    toks = cot.shape[0]
    steps = rows // tile
    return pl.pallas_call(
        functools.partial(last_kernel, factor, steps),
        grid=(steps,),
        in_specs=[
            pl.BlockSpec((toks, tile), lambda i: (0, jnp.minimum(i, steps // 2 - 1))),
            pl.BlockSpec((toks, tile), lambda i: (0, jnp.maximum(i - steps // 2, 0))),
            pl.BlockSpec((toks, keys), lambda i: (0, 0)),
            pl.BlockSpec((tile, keys), lambda i: (i, 0)),
        ],
        out_specs=pl.BlockSpec((toks, rows + keys), lambda i: (0, 0)),
        out_shape=jax.ShapeDtypeStruct((toks, rows + keys), jnp.bfloat16),
        scratch_shapes=[pltpu.VMEM((toks, keys), jnp.float32)],
        compiler_params=pltpu.CompilerParams(vmem_limit_bytes=32 * MIB),
        cost_estimate=SMALL,
    )(hid_low, hid_high, cot, weight_half)


def adam_step(grad, weight, first, second, scal_ref):
    first = scal_ref[0] * first + scal_ref[1] * grad
    second = scal_ref[2] * second + scal_ref[3] * (grad * grad)
    return 0.99 * weight - 0.1 * (first / (jnp.sqrt(second) + 1e-08))


def frag_kernel(factor, where_ref, scal_ref, low_ref, high_ref, cot_ref, grad_ref, weight_ref, first_ref, second_ref, keep_ref, give_ref):
    chips, size = keep_ref.shape[:2]
    even_mine = where_ref[2] == 0
    half = chips // 2

    for hid_ref, start in ((low_ref, 0), (high_ref, half)):

        @pl.loop(start, start + half)
        def _(j):
            at = pl.ds(pl.multiple_of(2 * j * size, 2 * size), 2 * size)
            hid = hid_ref[:, pl.ds(pl.multiple_of(2 * (j - start) * size, 2 * size), 2 * size)]
            grad = grad_ref[at, :] + row_dot(hid, cot_ref[...], factor)
            inner = adam_step(
                grad, weight_ref[at, :], first_ref[at, :], second_ref[at, :], scal_ref
            )
            even, odd = inner[:size], inner[size:]
            keep_ref[j] = jnp.where(even_mine, even, odd).astype(keep_ref.dtype)
            give_ref[j] = jnp.where(even_mine, odd, even).astype(give_ref.dtype)


def local_call(kernel, outs, *args, smem=1, limit=24):
    vmem = pl.BlockSpec(memory_space=pltpu.VMEM)
    return pl.pallas_call(
        kernel,
        in_specs=[pl.BlockSpec(memory_space=pltpu.SMEM)] * smem + [vmem] * (len(args) - smem),
        out_specs=[vmem] * len(outs),
        out_shape=outs,
        compiler_params=pltpu.CompilerParams(vmem_limit_bytes=limit * MIB),
        cost_estimate=SMALL,
    )(*args)


def frag_call(hid_low, hid_high, cot, grad, weight, first, second, where, scal, factor, own_rows):
    rows, cols = weight.shape
    out = jax.ShapeDtypeStruct((rows // (2 * own_rows), own_rows, cols), jnp.bfloat16)
    return local_call(
        functools.partial(frag_kernel, factor), [out, out],
        where, scal, hid_low, hid_high, cot, grad, weight, first, second, smem=2,
    )


def split_kernel(bit, where_ref, mine_ref, got_ref, stay_ref, leave_ref):
    low = ((where_ref[3] >> bit) & 1) == 0
    for i in range(stay_ref.shape[0]):
        sums = [
            mine_ref[j].astype(jnp.float32) + got_ref[j].astype(jnp.float32)
            for j in (2 * i, 2 * i + 1)
        ]
        stay_ref[i] = jnp.where(low, sums[0], sums[1])
        leave_ref[i] = jnp.where(low, sums[1], sums[0]).astype(leave_ref.dtype)


def split_call(bit, where, mine, got):
    shape = (mine.shape[0] // 2,) + mine.shape[1:]
    return local_call(
        functools.partial(split_kernel, bit),
        [jax.ShapeDtypeStruct(shape, jnp.float32), jax.ShapeDtypeStruct(shape, jnp.bfloat16)],
        where, mine, got,
    )


def halves_kernel(x_ref, y_ref, low_ref, high_ref):
    size = low_ref.shape[0]
    low_ref[...] = y_ref[:size]
    high_ref[...] = x_ref[size:]


def copy_kernel(count, *refs):
    for i in range(count):
        refs[count + i][...] = refs[i][...]


def copy_call(*arrays):
    count = len(arrays)
    rows, cols = arrays[0].shape
    block = pl.BlockSpec((rows // 2, cols), lambda i: (i, 0))
    return pl.pallas_call(
        functools.partial(copy_kernel, count),
        grid=(2,),
        in_specs=[block] * count,
        out_specs=[block] * count,
        out_shape=[jax.ShapeDtypeStruct(x.shape, x.dtype) for x in arrays],
        compiler_params=pltpu.CompilerParams(vmem_limit_bytes=VMEM),
        cost_estimate=SMALL,
    )(*arrays)


def outer_kernel(replicas, where_ref, stay_ref, got_ref, now_ref, mom_ref, _, __, next_ref, next_mom_ref, spread_ref):
    total = stay_ref[0] + got_ref[0].astype(jnp.float32)
    pseudo = now_ref[...] - total / replicas
    moment = 0.9 * mom_ref[...] + pseudo
    outer = now_ref[...] - 0.7 * (pseudo + 0.9 * moment)
    next_ref[...] = outer
    next_mom_ref[...] = moment
    spread_ref[0] = outer.astype(spread_ref.dtype)


def outer_call(replicas, where, stay, got, now, mom, now_copy, mom_copy):
    rows, cols = stay.shape[1:]
    whole = pl.BlockSpec((1, rows, cols), lambda i, w: (0, 0, 0))
    block = pl.BlockSpec((rows, cols), lambda i, w: (0, w[1]))
    anywhere = pl.BlockSpec(memory_space=pl.ANY)
    return pl.pallas_call(
        functools.partial(outer_kernel, replicas),
        grid_spec=pltpu.PrefetchScalarGridSpec(
            num_scalar_prefetch=1,
            grid=(1,),
            in_specs=[whole, whole, block, block, anywhere, anywhere],
            out_specs=[block, block, whole],
        ),
        out_shape=[jax.ShapeDtypeStruct(now.shape, now.dtype)] * 2
        + [jax.ShapeDtypeStruct((1, rows, cols), jnp.bfloat16)],
        input_output_aliases={5: 0, 6: 1},
        cost_estimate=SMALL,
    )(where, stay, got, now, mom, now_copy, mom_copy)


def place_kernel(offsets, final, factor, where_ref, *refs):
    count = len(offsets)
    msgs = refs[:count]
    acc_ref, _, back_ref, keys_ref, sems = refs[count:]
    toks, keys = acc_ref.shape
    rows = msgs[0].shape[1] - keys
    copies = []
    for i, m in enumerate(offsets):
        start = pl.multiple_of((where_ref[0] ^ m) * rows, rows)
        copy = pltpu.make_async_copy(
            msgs[i].at[:, pl.ds(0, rows)], back_ref.at[:, pl.ds(start, rows)], sems.at[i]
        )
        copy.start()
        copies.append(copy)
    total = acc_ref[...]
    for msg in msgs:
        total = total + msg[:, rows:].astype(jnp.float32)
    if final:
        total = total * factor
    keys_ref[...] = total.astype(keys_ref.dtype)
    for copy in copies:
        copy.wait()


def place_call(where, msgs, acc, back, offsets, final, factor):
    vmem = pl.BlockSpec(memory_space=pltpu.VMEM)
    anywhere = pl.BlockSpec(memory_space=pl.ANY)
    count = len(msgs)
    return pl.pallas_call(
        functools.partial(place_kernel, tuple(offsets), final, factor),
        in_specs=[pl.BlockSpec(memory_space=pltpu.SMEM)] + [vmem] * (count + 1) + [anywhere],
        out_specs=[anywhere, vmem],
        out_shape=[
            jax.ShapeDtypeStruct(back.shape, back.dtype),
            jax.ShapeDtypeStruct(acc.shape, jnp.bfloat16 if final else jnp.float32),
        ],
        input_output_aliases={count + 2: 0},
        scratch_shapes=[pltpu.SemaphoreType.DMA((count,))],
        compiler_params=pltpu.CompilerParams(vmem_limit_bytes=24 * MIB),
        cost_estimate=SMALL,
    )(where, *msgs, acc, back)


def adam_kernel(factor, scal_ref, hid_ref, cot_ref, grad_ref, weight_ref, first_ref, second_ref, *rest):
    grad = grad_ref[...] + row_dot(hid_ref[...], cot_ref[...], factor)
    rest[-1][...] = adam_step(grad, weight_ref[...], first_ref[...], second_ref[...], scal_ref)


def adam_call(hid, cot, grad, weight, first, second, scal, factor, tile, lo, hi, skip, base=None):
    rows, keys = weight.shape
    toks = hid.shape[0]
    state = pl.BlockSpec((tile, keys), lambda i: (lo + i, 0))
    in_specs = [
        pl.BlockSpec(memory_space=pltpu.SMEM),
        pl.BlockSpec((toks, tile), lambda i: (0, lo - skip + i)),
        pl.BlockSpec((toks, keys), lambda i: (0, 0)),
    ] + [state] * 4
    args = [scal, hid, cot, grad, weight, first, second]
    aliases = {}
    if base is not None:
        in_specs.append(pl.BlockSpec(memory_space=pl.ANY))
        aliases = {len(args): 0}
        args.append(base)
    return pl.pallas_call(
        functools.partial(adam_kernel, factor),
        grid=(hi - lo,),
        in_specs=in_specs,
        out_specs=state,
        out_shape=jax.ShapeDtypeStruct((rows, keys), jnp.float32),
        input_output_aliases=aliases,
        compiler_params=pltpu.CompilerParams(vmem_limit_bytes=VMEM),
        cost_estimate=SMALL,
    )(*args)


def spread_kernel(bits, where_ref, same_ref, other_ref, base_ref, out_ref, wide_ref, sems):
    chips, size, cols = same_ref.shape
    column = pl.ds(pl.multiple_of(where_ref[1] * cols, cols), cols)
    core = where_ref[2]
    copies = []
    for j in range(chips):
        offset = j ^ where_ref[3]
        at = 0
        for i, k in enumerate(reversed(bits)):
            at = at + (((offset >> k) & 1) << i)
        wide_ref[2 * j + core] = same_ref[at].astype(wide_ref.dtype)
        wide_ref[2 * j + 1 - core] = other_ref[at].astype(wide_ref.dtype)
        for b in (2 * j, 2 * j + 1):
            copy = pltpu.make_async_copy(
                wide_ref.at[b], out_ref.at[pl.ds(b * size, size), column], sems.at[b]
            )
            copy.start()
            copies.append(copy)
    for copy in copies:
        copy.wait()


def spread_call(bits, where, same, other, base):
    chips, size, cols = same.shape
    vmem = pl.BlockSpec(memory_space=pltpu.VMEM)
    anywhere = pl.BlockSpec(memory_space=pl.ANY)
    return pl.pallas_call(
        functools.partial(spread_kernel, bits),
        in_specs=[pl.BlockSpec(memory_space=pltpu.SMEM), vmem, vmem, anywhere],
        out_specs=anywhere,
        out_shape=jax.ShapeDtypeStruct(base.shape, base.dtype),
        input_output_aliases={3: 0},
        scratch_shapes=[
            pltpu.VMEM((2 * chips, size, cols), base.dtype),
            pltpu.SemaphoreType.DMA((2 * chips,)),
        ],
        compiler_params=pltpu.CompilerParams(vmem_limit_bytes=24 * MIB),
        cost_estimate=SMALL,
    )(where, same, other, base)


def per_device(
    hidden,
    key_cotangent,
    local_weight,
    adam_first,
    adam_second,
    outer_weight,
    outer_momentum,
    roster,
    step_count,
):
    tokens = hidden[0]
    cotangent = key_cotangent[0]
    weight = local_weight[0]
    outer_now = outer_weight[0]
    moment_now = outer_momentum[0]
    toks, width = tokens.shape
    rows, keys = weight.shape
    factor = 1.0 / math.sqrt(width)
    frag_cols = keys // FRAGS
    shards = lax.axis_size("fsdp")
    replicas = lax.axis_size("rep")
    shard = lax.axis_index("fsdp")
    replica = lax.axis_index("rep")
    offsets = list(range(1, shards))

    fragment = roster[step_count[0] // FRAGS % ROUNDS, step_count[0] % FRAGS]
    column = fragment * frag_cols
    steps_done = (step_count[0] + 1).astype(jnp.float32)
    scale1 = 1.0 / (1.0 - jnp.power(jnp.float32(0.9), steps_done))
    scale2 = 1.0 / (1.0 - jnp.power(jnp.float32(0.95), steps_done))
    scal = jnp.stack([0.9 * scale1, 0.1 * scale1, 0.95 * scale2, 0.05 * scale2])
    chips = replicas // 2
    core, chip = replica % 2, replica // 2
    own_rows = rows // replicas
    where = jnp.stack([shard, fragment, core, chip]).astype(jnp.int32)
    square = shards == 4
    half = toks // 2
    tile = min(512, rows // 4)
    tile_adam = min(256, rows // 4)
    tiles_adam = rows // tile_adam

    def hid_for(source, m):
        return lax.dynamic_slice_in_dim(source, (shard ^ m) * rows, rows, 1)

    def frag_of(x):
        return lax.dynamic_slice_in_dim(x, column, frag_cols, 1)

    cots = [cotangent] + [pair(cotangent, "fsdp", m) for m in ((1, 2) if square else offsets)]
    hids = [pair(hid_for(tokens, m), "fsdp", m) for m in offsets[:-1]]

    first, second = adam_first[0], adam_second[0]
    weight_half, back_out, key_acc, weight_frag = own_call(
        tokens, cotangent, weight, where, factor, tile, frag_cols
    )
    frag_state = [weight_frag] + list(cut_call(after(where, weight_half), [first, second], frag_cols))
    outer_copy, moment_copy = copy_call(after(outer_now, frag_state[-1]), moment_now)
    last = hid_for(after(tokens, weight_half), offsets[-1])
    lasts = [last[:, : rows // 2], last[:, rows // 2 :]]
    hid_low, hid_high = [pair(x, "fsdp", offsets[-1]) for x in lasts]
    if square:
        out = jax.ShapeDtypeStruct((half, keys), cotangent.dtype)
        low, high = local_call(
            halves_kernel, [out, out], after(cots[1], outer_copy, *lasts), cots[2], smem=0
        )
        cot_lo, cot_hi = pair(low, "fsdp", 1), pair(high, "fsdp", 2)
    near = cots if square else cots[:-1]
    grad, grad_frag, gives = near_call(
        tokens, hids, near, weight_half, after(where, outer_copy), factor, tile, frag_cols
    )
    if square:
        cot_lo, cot_hi = after(cot_lo, grad), after(cot_hi, grad)
        cots.append(jnp.concatenate([cot_lo, cot_hi], axis=0))
    cot_last = cots[-1]
    backs = [pair(x, "fsdp", m) for x, m in zip(gives, offsets)]

    inner, step_at = None, 0

    def inner_step(count, *tokens_ready):
        nonlocal inner, step_at
        end = min(step_at + count, tiles_adam)
        if step_at < end:
            low = end <= tiles_adam // 2
            inner = adam_call(
                after(hid_low if low else hid_high, *tokens_ready), cot_last, grad, weight, first,
                second, scal, factor, tile_adam, step_at, end, 0 if low else tiles_adam // 2,
                base=inner,
            )
            step_at = end
        return inner

    share = tiles_adam // 4
    inner_step(share, *gives)
    hid_high = after(hid_high, inner)

    keep, give = frag_call(
        hid_low, hid_high, frag_of(cot_last), grad_frag, *frag_state, where, scal, factor, own_rows
    )
    got = pair(give, "rep", 1)
    bits = [k for k in range(chips.bit_length()) if (1 << k) < chips]
    for k in bits:
        keep, leave = split_call(k, where, keep, got)
        got = pair(leave, "rep", 2 << k)
        if k == 0:
            got = after(got, inner_step(share, leave))
        elif k == 1:
            give_last = last_call(after(hid_low, leave), hid_high, cot_last, weight_half, factor, tile)
            got = after(got, give_last)
    if len(bits) < 2:
        give_last = last_call(after(hid_low, got), hid_high, cot_last, weight_half, factor, tile)
    backs.append(pair(give_last, "fsdp", offsets[-1]))
    outer_next, moment_next, spread = outer_call(
        replicas, where, keep, got, outer_now, moment_now, outer_copy, moment_copy
    )
    for k in reversed(bits):
        got = pair(spread, "rep", 2 << k)
        got = after(got, inner_step(share if k > 0 else tiles_adam, spread))
        spread = jnp.concatenate([spread, got], axis=0)
        if k == bits[-1]:
            back_out, key_acc = place_call(
                where, [after(b, inner) for b in backs[:-1]], key_acc, back_out, offsets[:-1], False,
                factor,
            )
            spread = after(spread, key_acc)
    got = pair(spread, "rep", 1)
    new_local = spread_call(bits, where, spread, got, inner)
    back_out, keys_out = place_call(
        where, [after(backs[-1], new_local)], key_acc, back_out, offsets[-1:], True, factor
    )

    return (keys_out[None], back_out[None], new_local[None], outer_next[None], moment_next[None])


def solution(mesh):
    in_specs = (
        P("rep", "fsdp", None),
        P("rep", "fsdp", None),
        P("rep", "fsdp", None),
        P("rep", "fsdp", None),
        P("rep", "fsdp", None),
        P("fsdp", "rep", None),
        P("fsdp", "rep", None),
        P(),
        P(),
    )
    out_specs = (
        P("rep", "fsdp", None),
        P("rep", "fsdp", None),
        P("rep", "fsdp", None),
        P("fsdp", "rep", None),
        P("fsdp", "rep", None),
    )
    return jax.shard_map(
        per_device, mesh=mesh, in_specs=in_specs, out_specs=out_specs, check_vma=False
    )
```

time: 418 us -> 120 us (0.29)
  waiting for transfers between devices: 337 us -> 13.4 us
  Pallas kernels: 0 us -> 66.1 us
  matrix products: 30.9 us -> 0 us
  other arithmetic: 23.4 us -> 0.81 us
  starting transfers between devices: 0.34 us -> 19.1 us
  between operations: 15.2 us -> 2.47 us
  local copies, waits for them, and re-layouts: 11.4 us -> 17.7 us
    reduce_scatter x2 -> x0, waiting for transfers between devices: 180 us -> none  [the longest x1 154 us: per_device(): lax.psum_scatter((lax.dot_general(columns, cotangent, (((0,), (0,)), ((),...]
    all_gather x2 -> x0, waiting for transfers between devices: 157 us -> none  [the longest x1 156 us: per_device(): piece = lax.all_gather(weight_half, 'fsdp', axis=0, tiled=True)]
    pallas_call x0 -> x17, Pallas kernels: none -> 66.1 us  [the longest x4 21.9 us: adam_call(): pl.pallas_call(functools.partial(adam_kernel, factor), grid=(hi - lo,), i...]
    dot_general x3 -> x0, matrix products: 30.9 us -> none  [the longest x1 13.2 us: per_device(): lax.dot_general(cotangent, piece, (((1,), (1,)), ((), ())), preferred_ele...]
    ppermute x0 -> x17, starting transfers between devices: none -> 19.1 us  [pair(): return lax.ppermute(x, axis, [(i, i ^ offset) for i in range(size)])]
    ppermute x0 -> x17, waiting for transfers between devices: none -> 13.4 us  [pair(): return lax.ppermute(x, axis, [(i, i ^ offset) for i in range(size)])]
    sub x1 -> x0, other arithmetic: 12.7 us -> none  [adam_update(): weight - 0.1 * (first_hat / (jnp.sqrt(second_hat) + 1e-08) + 0.1 * weight)]
    convert_element_type x2 -> x0, other arithmetic: 7.96 us -> none  [the longest x1 6 us: per_device(): weight_half = weight.astype(jnp.bfloat16)]
  transfers between devices with their start and end apart: 4 -> 17, of which waited for: 4 -> 7; matrix products, arithmetic and copies ran while one was open for 8% -> 5% of each run, Pallas kernels for 0% -> 53%
where the time goes in v2:
time: 120 us
  Pallas kernels  66.1 us (55%)
  starting transfers between devices  19.1 us (16%)
  local copies, waits for them, and re-layouts  17.7 us (15%)
  waiting for transfers between devices  13.4 us (11%)
  between operations  2.47 us (2%)
    pallas_call x4, Pallas kernels, adam_call(): pl.pallas_call(functools.partial(adam_kernel, factor), grid=(hi - lo,), i...  21.9 us
    ppermute x17, starting transfers between devices, pair(): return lax.ppermute(x, axis, [(i, i ^ offset) for i in range(size)])  19.1 us
    ppermute x17, waiting for transfers between devices, pair(): return lax.ppermute(x, axis, [(i, i ^ offset) for i in range(size)])  13.4 us
    pallas_call x1, Pallas kernels, near_call(): pl.pallas_call(functools.partial(near_kernel, groups, factor, steps), gri...  13.3 us
    unnamed x46, local copies, waits for them, and re-layouts  10.6 us
    pallas_call x1, Pallas kernels, own_call(): pl.pallas_call(functools.partial(own_kernel, factor), grid_spec=pltpu.Pre...  8.54 us
    pallas_call x2, Pallas kernels, place_call(): pl.pallas_call(functools.partial(place_kernel, tuple(offsets), final, fac...  4.62 us
    pallas_call x4, Pallas kernels, local_call(): pl.pallas_call(kernel, in_specs=[pl.BlockSpec(memory_space=pltpu.SMEM)] *...  4.41 us
  transfers between devices with their start and end apart: 17, of which 7 were waited for; matrix products, arithmetic and copies ran while one was open for 5% of the time, Pallas kernels for 53%

profile of v2, /device:TPU:0, one launch (start us, length us, event | category | flops | bytes accessed | tf_op | source)
XLA Modules:
  0.0 119.5 jit_solution(4905783783703962681)
XLA Ops:
  0.7 2.7 %dynamic-slice_bitcast_fusion = (bf16[192,2048]{1,0:T(8,128)(2,1)}, bf16[192,2048]{1,0:T(8,128)(2,1)}) fusion(bf16[1,192,8192]{2,1,0:T(8,128)(2,1)} %param.9, s32[]{:T(128)S(6)} %select_n.49, s32[]{:T(128)S(6)} %select_n.48), kind=kLoop, calls=%fused_computation | loop fusion | bytes 3145736 | tf_op jit(solution)/shard_map/dynamic_slice | solution.py:488
  3.4 3.0 %collective-permute-start.3 = (bf16[192,2048]{1,0:T(8,128)(2,1)}, bf16[192,2048]{1,0:T(8,128)(2,1)}, u32[]{:S(2)}, u32[]{:S(2)}) collective-permute-start(bf16[192,2048]{1,0:T(8,128)(2,1)} %get-tuple-element.101), channel_id=1, source_target_pairs={{0,2},{1,3},{2,0},{3,1},{4,6},{5,7},{6,4},{7,5},{8,10},{9,11},{10,... | collective-permute-start | bytes 2359304 | tf_op jit(solution)/shard_map/ppermute | solution.py:20
  6.4 1.5 %collective-permute-start.2 = (bf16[192,2048]{1,0:T(8,128)(2,1)}, bf16[192,2048]{1,0:T(8,128)(2,1)}, u32[]{:S(2)}, u32[]{:S(2)}) collective-permute-start(bf16[192,2048]{1,0:T(8,128)(2,1)} %get-tuple-element.102), channel_id=1, source_target_pairs={{0,1},{1,0},{2,3},{3,2},{4,5},{5,4},{6,7},{7,6},{8,9},{9,8},{10,11... | collective-permute-start | bytes 2359304 | tf_op jit(solution)/shard_map/ppermute | solution.py:20
  9.1 1.3 %dynamic_slice.19 = s32[1,1]{0,1:T(1,128)} dynamic-slice(s32[8,4]{0,1:T(4,128)} %param.16, s32[]{:T(128)S(6)} %select_n.42, s32[]{:T(128)S(6)} %select_n.44), dynamic_slice_sizes={1,1} | dynamic-slice | bytes 12 | tf_op jit(solution)/shard_map/dynamic_slice | solution.py:471
  10.5 0.7 pad_add_fusion.where_ref
  11.2 8.5 %shard_map.128 = (bf16[2048,1024]{1,0:T(8,128)(2,1)}, bf16[192,8192]{1,0:T(8,128)(2,1)}, f32[192,1024]{1,0:T(8,128)S(1)}, f32[2048,256]{1,0:T(8,128)S(1)}) custom-call(s32[4]{0:T(128)S(1)} %pad_add_fusion.where_ref, bf16[192,8192]{1,0:T(8,128)(2,1)} %bitcast.55, bf16[192,1024]{1,0:T(8,128)(2,1)S(1)} %bitcast.37, f32[2048,1024]{1,0:T(8,128)} %bitcast.50), custom_call_target="tpu_custom_call" | custom-call | flops 1 | bytes 1 | tf_op jit(solution)/shard_map/pallas_call | solution.py:71
  19.7 1.3 %copy-done.3 = f32[2048,256]{1,0:T(8,128)} copy-done((f32[2048,256]{1,0:T(8,128)}, f32[2048,256]{1,0:T(8,128)S(1)}, u32[]{:S(2)}) %copy-start.3) | copy-done | bytes 2097176
  21.0 0.9 copy-done.15
  21.9 3.0 %shard_map.129 = (f32[2048,256]{1,0:T(8,128)S(1)}, f32[2048,256]{1,0:T(8,128)S(1)}) custom-call(s32[4]{0:T(128)S(1)} %pad_add_fusion.where_ref, f32[2048,1024]{1,0:T(8,128)} %bitcast.39, f32[2048,1024]{1,0:T(8,128)} %bitcast.44), custom_call_target="tpu_custom_call" | custom-call | flops 1 | bytes 1 | tf_op jit(solution)/shard_map/pallas_call | solution.py:98
  24.9 1.3 %copy-done.5 = f32[2048,256]{1,0:T(8,128)} copy-done((f32[2048,256]{1,0:T(8,128)}, f32[2048,256]{1,0:T(8,128)S(1)}, u32[]{:S(2)}) %copy-start.5) | copy-done | bytes 2097176
  26.2 1.3 %copy-done.7 = f32[2048,256]{1,0:T(8,128)} copy-done((f32[2048,256]{1,0:T(8,128)}, f32[2048,256]{1,0:T(8,128)S(1)}, u32[]{:S(2)}) %copy-start.7) | copy-done | bytes 2097176
  27.5 1.4 %shard_map.130 = (f32[256,1024]{1,0:T(8,128)}, f32[256,1024]{1,0:T(8,128)}) custom-call(f32[256,1024]{1,0:T(8,128)S(1)} %bitcast.32, f32[256,1024]{1,0:T(8,128)S(1)} %bitcast.34), custom_call_target="tpu_custom_call" | custom-call | flops 1 | bytes 1 | tf_op jit(solution)/shard_map/pallas_call | solution.py:288
  28.9 2.1 %constant_dynamic-slice_fusion.2 = (bf16[192,1024]{1,0:T(8,128)(2,1)}, bf16[192,1024]{1,0:T(8,128)(2,1)}) fusion(bf16[192,8192]{1,0:T(8,128)(2,1)} %bitcast.56, s32[]{:T(128)S(6)} %add.46, s32[]{:T(128)S(6)} %select_n.47), kind=kLoop, calls=%fused_computation.9 | loop fusion | bytes 1572872 | tf_op jit(solution)/shard_map/slice | solution.py:503
  31.0 3.0 %collective-permute-done.4.refs_4_.x_ref = bf16[192,1024]{1,0:T(8,128)(2,1)S(1)} collective-permute-done((bf16[192,1024]{1,0:T(8,128)(2,1)S(1)}, bf16[192,1024]{1,0:T(8,128)(2,1)S(1)}, u32[]{:S(2)}, u32[]{:S(2)}) %collective-permute-start.4) | collective-permute-done | bytes 393248 | tf_op jit(solution)/shard_map/ppermute | solution.py:20
  34.8 1.5 %collective-permute-start.6 = (bf16[96,1024]{1,0:T(8,128)(2,1)S(1)}, bf16[96,1024]{1,0:T(8,128)(2,1)}, u32[]{:S(2)}, u32[]{:S(2)}) collective-permute-start(bf16[96,1024]{1,0:T(8,128)(2,1)S(1)} %get-tuple-element.64), channel_id=1, source_target_pairs={{0,1},{1,0},{2,3},{3,2},{4,5},{5,4},{6,7},{7,6},{8,9},{9,8},{10,11... | collective-permute-start | bytes 589832 | tf_op jit(solution)/shard_map/ppermute | solution.py:20
  36.3 1.4 %collective-permute-start.1 = (bf16[192,1024]{1,0:T(8,128)(2,1)}, bf16[192,1024]{1,0:T(8,128)(2,1)S(1)}, u32[]{:S(2)}, u32[]{:S(2)}) collective-permute-start(bf16[192,1024]{1,0:T(8,128)(2,1)} %get-tuple-element.103), channel_id=1, source_target_pairs={{0,3},{1,2},{2,1},{3,0},{4,7},{5,6},{6,5},{7,4},{8,11},{9,10},{10,... | collective-permute-start | bytes 1179656 | tf_op jit(solution)/shard_map/ppermute | solution.py:20
  37.8 1.6 %collective-permute-start = (bf16[192,1024]{1,0:T(8,128)(2,1)}, bf16[192,1024]{1,0:T(8,128)(2,1)S(1)}, u32[]{:S(2)}, u32[]{:S(2)}) collective-permute-start(bf16[192,1024]{1,0:T(8,128)(2,1)} %get-tuple-element.104), channel_id=1, source_target_pairs={{0,3},{1,2},{2,1},{3,0},{4,7},{5,6},{6,5},{7,4},{8,11},{9,10},{10,... | collective-permute-start | bytes 1179656 | tf_op jit(solution)/shard_map/ppermute | solution.py:20
  40.2 1.0 copy-done.12
  41.2 1.0 copy-done.14
  42.2 13.3 %shard_map.131 = (f32[2048,1024]{1,0:T(8,128)}, f32[2048,256]{1,0:T(8,128)}, bf16[192,3072]{1,0:T(8,128)(2,1)}, bf16[192,3072]{1,0:T(8,128)(2,1)}) custom-call(s32[4]{0:T(128)S(1)} %pad_add_fusion.where_ref, bf16[192,8192]{1,0:T(8,128)(2,1)} %bitcast.57, bf16[192,2048]{1,0:T(8,128)(2,1)} %collective-permute-done.2.refs_1_, ...), custom_call_target="tpu_custom_call" | custom-call | flops 1 | bytes 1 | tf_op jit(solution)/shard_map/pallas_call | solution.py:155
  55.5 0.6 collective-permute-start.13
  56.1 1.4 %collective-permute-start.14 = (bf16[192,3072]{1,0:T(8,128)(2,1)}, bf16[192,3072]{1,0:T(8,128)(2,1)S(1)}, u32[]{:S(2)}, u32[]{:S(2)}) collective-permute-start(bf16[192,3072]{1,0:T(8,128)(2,1)} %get-tuple-element.61), channel_id=1, source_target_pairs={{0,2},{1,3},{2,0},{3,1},{4,6},{5,7},{6,4},{7,5},{8,10},{9,11},{10,... | collective-permute-start | bytes 3538952 | tf_op jit(solution)/shard_map/ppermute | solution.py:20
  57.5 0.9 constant_dynamic-update-slice_fusion.1
  58.4 0.9 constant_dynamic-update-slice_fusion.cot_ref
  59.5 5.5 %shard_map.133.rest_0_ = f32[2048,1024]{1,0:T(8,128)} custom-call(f32[4]{0:T(128)S(1)} %pad_maximum_fusion.1.scal_ref, bf16[192,1024]{1,0:T(8,128)(2,1)S(1)} %collective-permute-done.hid_ref.low_ref, bf16[192,1024]{1,0:T(8,128)(2,1)S(1)} %constant_dynamic-update-slice_fusion.cot_ref, f32[2048,1024]{1,0:T(8,128)} %get-tuple-element.65.grad_ref, ...), custom_call_target="tpu_custom_call" | custom-call | flops 1 | bytes 1 | tf_op jit(solution)/shard_map/pallas_call | solution.py:392
  65.3 0.8 copy-done.9
  66.1 3.1 %shard_map.134 = (bf16[4,256,256]{2,1,0:T(8,128)(2,1)S(1)}, bf16[4,256,256]{2,1,0:T(8,128)(2,1)S(1)}) custom-call(s32[4]{0:T(128)S(1)} %pad_add_fusion.where_ref, f32[4]{0:T(128)S(1)} %pad_maximum_fusion.1.scal_ref, bf16[192,1024]{1,0:T(8,128)(2,1)S(1)} %collective-permute-done.hid_ref.low_ref, ...), custom_call_target="tpu_custom_call" | custom-call | flops 1 | bytes 1 | tf_op jit(solution)/shard_map/pallas_call | solution.py:234
  69.3 1.9 %collective-permute-done.8.got_ref = bf16[4,256,256]{2,1,0:T(8,128)(2,1)S(1)} collective-permute-done((bf16[4,256,256]{2,1,0:T(8,128)(2,1)S(1)}, bf16[4,256,256]{2,1,0:T(8,128)(2,1)S(1)}, u32[]{:S(2)}, u32[]{:S(2)}) %collective-permute-start.8) | collective-permute-done | bytes 524320 | tf_op jit(solution)/shard_map/ppermute | solution.py:20
  71.2 0.7 shard_map.135
  71.9 1.6 %collective-permute-start.9 = (bf16[2,256,256]{2,1,0:T(8,128)(2,1)S(1)}, bf16[2,256,256]{2,1,0:T(8,128)(2,1)S(1)}, u32[]{:S(2)}, u32[]{:S(2)}) collective-permute-start(bf16[2,256,256]{2,1,0:T(8,128)(2,1)S(1)} %get-tuple-element.76), channel_id=1, source_target_pairs={{0,8},{4,12},{8,0},{12,4},{16,24},{20,28},{24,16},{28,20},{1,9},{5... | collective-permute-start | bytes 786440 | tf_op jit(solution)/shard_map/ppermute | solution.py:20
  73.5 5.5 %shard_map.136.rest_0_ = f32[2048,1024]{1,0:T(8,128)} custom-call(f32[4]{0:T(128)S(1)} %pad_maximum_fusion.1.scal_ref, bf16[192,1024]{1,0:T(8,128)(2,1)S(1)} %collective-permute-done.hid_ref.low_ref, bf16[192,1024]{1,0:T(8,128)(2,1)S(1)} %constant_dynamic-update-slice_fusion.cot_ref, ...), custom_call_target="tpu_custom_call", output_to_operand_aliasing={{}: (7, {})} | custom-call | flops 1 | bytes 1 | tf_op jit(solution)/shard_map/pallas_call | solution.py:392
  79.0 1.2 %collective-permute-done.9.got_ref = bf16[2,256,256]{2,1,0:T(8,128)(2,1)S(1)} collective-permute-done((bf16[2,256,256]{2,1,0:T(8,128)(2,1)S(1)}, bf16[2,256,256]{2,1,0:T(8,128)(2,1)S(1)}, u32[]{:S(2)}, u32[]{:S(2)}) %collective-permute-start.9) | collective-permute-done | bytes 262176 | tf_op jit(solution)/shard_map/ppermute | solution.py:20
  80.9 0.7 copy-done.17
  81.6 2.6 %collective-permute-start.11 = (bf16[1,256,256]{2,1,0:T(8,128)(2,1)S(1)}, bf16[1,256,256]{2,1,0:T(8,128)(2,1)S(1)}, u32[]{:S(2)}, u32[]{:S(2)}) collective-permute-start(bf16[1,256,256]{2,1,0:T(8,128)(2,1)S(1)} %get-tuple-element.79), channel_id=1, source_target_pairs={{0,16},{4,20},{8,24},{12,28},{16,0},{20,4},{24,8},{28,12},{1,17},{... | collective-permute-start | bytes 393224 | tf_op jit(solution)/shard_map/ppermute | solution.py:20
  84.2 4.3 %shard_map.138 = bf16[192,3072]{1,0:T(8,128)(2,1)} custom-call(bf16[192,1024]{1,0:T(8,128)(2,1)S(1)} %collective-permute-done.hid_ref.low_ref, bf16[192,1024]{1,0:T(8,128)(2,1)S(1)} %collective-permute-done.1.high_ref.hid_ref, bf16[192,1024]{1,0:T(8,128)(2,1)S(1)} %constant_dynamic-update-slice_fusion.cot_ref, bf16[2048,1024]{1,0:T(8,128)(2,1)S(1)} %copy-done), custom_call_target="tpu_custom_call" | custom-call | flops 1 | bytes 1 | tf_op jit(solution)/shard_map/pallas_call | solution.py:189
  88.5 1.6 %collective-permute-start.10 = (bf16[192,3072]{1,0:T(8,128)(2,1)}, bf16[192,3072]{1,0:T(8,128)(2,1)}, u32[]{:S(2)}, u32[]{:S(2)}) collective-permute-start(bf16[192,3072]{1,0:T(8,128)(2,1)} %shard_map.138), channel_id=1, source_target_pairs={{0,3},{1,2},{2,1},{3,0},{4,7},{5,6},{6,5},{7,4},{8,11},{9,10},{10,... | collective-permute-start | bytes 3538952 | tf_op jit(solution)/shard_map/ppermute | solution.py:20
  90.1 0.6 copy-done.20
  90.7 2.7 %shard_map.139 = (f32[256,1024]{1,0:T(8,128)}, f32[256,1024]{1,0:T(8,128)}, bf16[1,256,256]{2,1,0:T(8,128)(2,1)}) custom-call(s32[4]{0:T(128)} %copy-done.18, f32[1,256,256]{2,1,0:T(8,128)} %copy-done.17, bf16[1,256,256]{2,1,0:T(8,128)(2,1)} %copy-done.20, f32[256,1024]{1,0:T(8,128)} %bitcast.31, ...), custom_call_target="tpu_custom_call", output_to_operand_aliasing={{0}: (5, {}), {1}: (6, {})} | custom-call | flops 1 | bytes 1 | tf_op jit(solution)/shard_map/pallas_call | solution.py:314
  93.8 5.4 %shard_map.140.rest_0_ = f32[2048,1024]{1,0:T(8,128)} custom-call(f32[4]{0:T(128)S(1)} %pad_maximum_fusion.1.scal_ref, bf16[192,1024]{1,0:T(8,128)(2,1)S(1)} %collective-permute-done.1.high_ref.hid_ref, bf16[192,1024]{1,0:T(8,128)(2,1)S(1)} %constant_dynamic-update-slice_fusion.cot_ref, ...), custom_call_target="tpu_custom_call", output_to_operand_aliasing={{}: (7, {})} | custom-call | flops 1 | bytes 1 | tf_op jit(solution)/shard_map/pallas_call | solution.py:392
  99.2 2.8 %collective-permute-done.12 = bf16[1,256,256]{2,1,0:T(8,128)(2,1)S(1)} collective-permute-done((bf16[1,256,256]{2,1,0:T(8,128)(2,1)}, bf16[1,256,256]{2,1,0:T(8,128)(2,1)S(1)}, u32[]{:S(2)}, u32[]{:S(2)}) %collective-permute-start.12) | collective-permute-done | bytes 131104 | tf_op jit(solution)/shard_map/ppermute | solution.py:20
  102.2 1.7 %shard_map.141 = (bf16[192,8192]{1,0:T(8,128)(2,1)}, f32[192,1024]{1,0:T(8,128)S(1)}) custom-call(s32[4]{0:T(128)S(1)} %copy-done.19, bf16[192,3072]{1,0:T(8,128)(2,1)S(1)} %collective-permute-done.13.refs_0_, bf16[192,3072]{1,0:T(8,128)(2,1)S(1)} %collective-permute-done.14.refs_1_, f32[192,1024]{1,0:T(8,128)S(1)} %copy-done.16, ...), custom_call_target="tpu_custom_call", output_to_operand_aliasing={{0}: (4, {})} | custom-call | flops 1 | bytes 1 | tf_op jit(solution)/shard_map/pallas_call | solution.py:357
  103.9 0.9 collective-permute-start.15
  104.8 5.4 %shard_map.142.base_ref = f32[2048,1024]{1,0:T(8,128)} custom-call(f32[4]{0:T(128)S(1)} %pad_maximum_fusion.1.scal_ref, bf16[192,1024]{1,0:T(8,128)(2,1)S(1)} %collective-permute-done.1.high_ref.hid_ref, bf16[192,1024]{1,0:T(8,128)(2,1)S(1)} %constant_dynamic-update-slice_fusion.cot_ref, ...), custom_call_target="tpu_custom_call", output_to_operand_aliasing={{}: (7, {})} | custom-call | flops 1 | bytes 1 | tf_op jit(solution)/shard_map/pallas_call | solution.py:392
  110.2 0.6 collective-permute-done.15
  110.9 1.9 %collective-permute-done.16.other_ref = bf16[4,256,256]{2,1,0:T(8,128)(2,1)S(1)} collective-permute-done((bf16[4,256,256]{2,1,0:T(8,128)(2,1)S(1)}, bf16[4,256,256]{2,1,0:T(8,128)(2,1)S(1)}, u32[]{:S(2)}, u32[]{:S(2)}) %collective-permute-start.16) | collective-permute-done | bytes 524320 | tf_op jit(solution)/shard_map/ppermute | solution.py:20
  112.8 2.0 %shard_map.143 = f32[2048,1024]{1,0:T(8,128)} custom-call(s32[4]{0:T(128)S(1)} %copy-done.19, bf16[4,256,256]{2,1,0:T(8,128)(2,1)S(1)} %constant_dynamic-update-slice_fusion.2.same_ref, bf16[4,256,256]{2,1,0:T(8,128)(2,1)S(1)} %collective-permute-done.16.other_ref, f32[2048,1024]{1,0:T(8,128)} %shard_map.142.base_ref), custom_call_target="tpu_custom_call", output_to_operand_aliasing={{}: (3, {})} | custom-call | flops 1 | bytes 1 | tf_op jit(solution)/shard_map/pallas_call | solution.py:430
  114.8 1.9 %collective-permute-done.10.refs_0_ = bf16[192,3072]{1,0:T(8,128)(2,1)} collective-permute-done((bf16[192,3072]{1,0:T(8,128)(2,1)}, bf16[192,3072]{1,0:T(8,128)(2,1)}, u32[]{:S(2)}, u32[]{:S(2)}) %collective-permute-start.10) | collective-permute-done | bytes 1179680 | tf_op jit(solution)/shard_map/ppermute | solution.py:20
  116.6 2.9 %shard_map.144 = (bf16[192,8192]{1,0:T(8,128)(2,1)}, bf16[192,1024]{1,0:T(8,128)(2,1)}) custom-call(s32[4]{0:T(128)S(1)} %copy-done.19, bf16[192,3072]{1,0:T(8,128)(2,1)} %collective-permute-done.10.refs_0_, f32[192,1024]{1,0:T(8,128)S(1)} %get-tuple-element.91.refs_1_, bf16[192,8192]{1,0:T(8,128)(2,1)} %get-tuple-element.96.refs_2_), custom_call_target="tpu_custom_call", output_to_operand_aliasing={{0}: (3, {})} | custom-call | flops 1 | bytes 1 | tf_op jit(solution)/shard_map/pallas_call | solution.py:357
  (58 shorter events, 2.9 us)
Async XLA Ops:
  0.6 7.2 %copy-start.10 = (bf16[1,192,1024]{2,1,0:T(8,128)(2,1)S(1)}, bf16[1,192,1024]{2,1,0:T(8,128)(2,1)}, u32[]{:S(2)}) copy-start(bf16[1,192,1024]{2,1,0:T(8,128)(2,1)} %param.10) | copy-start | bytes 1179652
  3.4 34.4 %collective-permute-start.3 = (bf16[192,2048]{1,0:T(8,128)(2,1)}, bf16[192,2048]{1,0:T(8,128)(2,1)}, u32[]{:S(2)}, u32[]{:S(2)}) collective-permute-start(bf16[192,2048]{1,0:T(8,128)(2,1)} %get-tuple-element.101), channel_id=1, source_target_pairs={{0,2},{1,3},{2,0},{3,1},{4,6},{5,7},{6,4},{7,5},{8,10},{9,11},{10,... | collective-permute-start | bytes 2359304 | tf_op jit(solution)/shard_map/ppermute | solution.py:20
  6.4 33.8 %collective-permute-start.2 = (bf16[192,2048]{1,0:T(8,128)(2,1)}, bf16[192,2048]{1,0:T(8,128)(2,1)}, u32[]{:S(2)}, u32[]{:S(2)}) collective-permute-start(bf16[192,2048]{1,0:T(8,128)(2,1)} %get-tuple-element.102), channel_id=1, source_target_pairs={{0,1},{1,0},{2,3},{3,2},{4,5},{5,4},{6,7},{7,6},{8,9},{9,8},{10,11... | collective-permute-start | bytes 2359304 | tf_op jit(solution)/shard_map/ppermute | solution.py:20
  7.9 26.1 %collective-permute-start.4 = (bf16[192,1024]{1,0:T(8,128)(2,1)S(1)}, bf16[192,1024]{1,0:T(8,128)(2,1)S(1)}, u32[]{:S(2)}, u32[]{:S(2)}) collective-permute-start(bf16[192,1024]{1,0:T(8,128)(2,1)S(1)} %bitcast.35), channel_id=1, source_target_pairs={{0,1},{1,0},{2,3},{3,2},{4,5},{5,4},{6,7},{7,6},{8,9},{9,8},{10,11... | collective-permute-start | bytes 1179656 | tf_op jit(solution)/shard_map/ppermute | solution.py:20
  8.4 25.6 %collective-permute-start.5 = (bf16[192,1024]{1,0:T(8,128)(2,1)S(1)}, bf16[192,1024]{1,0:T(8,128)(2,1)S(1)}, u32[]{:S(2)}, u32[]{:S(2)}) collective-permute-start(bf16[192,1024]{1,0:T(8,128)(2,1)S(1)} %bitcast.36), channel_id=1, source_target_pairs={{0,2},{1,3},{2,0},{3,1},{4,6},{5,7},{6,4},{7,5},{8,10},{9,11},{10,... | collective-permute-start | bytes 1179656 | tf_op jit(solution)/shard_map/ppermute | solution.py:20
  11.2 69.1 %copy-start.18 = (s32[4]{0:T(128)}, s32[4]{0:T(128)S(1)}, u32[]{:S(2)}) copy-start(s32[4]{0:T(128)S(1)} %pad_add_fusion.where_ref) | copy-start | bytes 52
  19.7 1.3 %copy-start.3 = (f32[2048,256]{1,0:T(8,128)}, f32[2048,256]{1,0:T(8,128)S(1)}, u32[]{:S(2)}) copy-start(f32[2048,256]{1,0:T(8,128)S(1)} %get-tuple-element.71.weight_ref) | copy-start | bytes 6291460
  21.0 0.9 copy-start.15
  21.9 5.6 %copy-start.1 = (f32[1,256,1024]{2,1,0:T(8,128)S(1)}, f32[1,256,1024]{2,1,0:T(8,128)}, u32[]{:S(2)}) copy-start(f32[1,256,1024]{2,1,0:T(8,128)} %param.14) | copy-start | bytes 3145732
  21.9 5.6 %copy-start.2 = (f32[1,256,1024]{2,1,0:T(8,128)S(1)}, f32[1,256,1024]{2,1,0:T(8,128)}, u32[]{:S(2)}) copy-start(f32[1,256,1024]{2,1,0:T(8,128)} %param.15) | copy-start | bytes 3145732
  24.9 1.3 %copy-start.5 = (f32[2048,256]{1,0:T(8,128)}, f32[2048,256]{1,0:T(8,128)S(1)}, u32[]{:S(2)}) copy-start(f32[2048,256]{1,0:T(8,128)S(1)} %get-tuple-element.72.first_ref) | copy-start | bytes 6291460
  26.2 1.3 %copy-start.7 = (f32[2048,256]{1,0:T(8,128)}, f32[2048,256]{1,0:T(8,128)S(1)}, u32[]{:S(2)}) copy-start(f32[2048,256]{1,0:T(8,128)S(1)} %get-tuple-element.56.second_ref) | copy-start | bytes 6291460
  34.0 0.8 copy-start.11
  34.0 3.8 %copy-start.13 = (bf16[192,1024]{1,0:T(8,128)(2,1)}, bf16[192,1024]{1,0:T(8,128)(2,1)S(1)}, u32[]{:S(2)}) copy-start(bf16[192,1024]{1,0:T(8,128)(2,1)S(1)} %collective-permute-done.5.refs_5_.y_ref) | copy-start | bytes 1179652
  34.0 21.4 %collective-permute-start.7 = (bf16[96,1024]{1,0:T(8,128)(2,1)S(1)}, bf16[96,1024]{1,0:T(8,128)(2,1)}, u32[]{:S(2)}, u32[]{:S(2)}) collective-permute-start(bf16[96,1024]{1,0:T(8,128)(2,1)S(1)} %get-tuple-element.67), channel_id=1, source_target_pairs={{0,2},{1,3},{2,0},{3,1},{4,6},{5,7},{6,4},{7,5},{8,10},{9,11},{10,... | collective-permute-start | bytes 589832 | tf_op jit(solution)/shard_map/ppermute | solution.py:20
  34.8 20.7 %collective-permute-start.6 = (bf16[96,1024]{1,0:T(8,128)(2,1)S(1)}, bf16[96,1024]{1,0:T(8,128)(2,1)}, u32[]{:S(2)}, u32[]{:S(2)}) collective-permute-start(bf16[96,1024]{1,0:T(8,128)(2,1)S(1)} %get-tuple-element.64), channel_id=1, source_target_pairs={{0,1},{1,0},{2,3},{3,2},{4,5},{5,4},{6,7},{7,6},{8,9},{9,8},{10,11... | collective-permute-start | bytes 589832 | tf_op jit(solution)/shard_map/ppermute | solution.py:20
  36.3 28.8 %collective-permute-start.1 = (bf16[192,1024]{1,0:T(8,128)(2,1)}, bf16[192,1024]{1,0:T(8,128)(2,1)S(1)}, u32[]{:S(2)}, u32[]{:S(2)}) collective-permute-start(bf16[192,1024]{1,0:T(8,128)(2,1)} %get-tuple-element.103), channel_id=1, source_target_pairs={{0,3},{1,2},{2,1},{3,0},{4,7},{5,6},{6,5},{7,4},{8,11},{9,10},{10,... | collective-permute-start | bytes 1179656 | tf_op jit(solution)/shard_map/ppermute | solution.py:20
  37.8 21.6 %collective-permute-start = (bf16[192,1024]{1,0:T(8,128)(2,1)}, bf16[192,1024]{1,0:T(8,128)(2,1)S(1)}, u32[]{:S(2)}, u32[]{:S(2)}) collective-permute-start(bf16[192,1024]{1,0:T(8,128)(2,1)} %get-tuple-element.104), channel_id=1, source_target_pairs={{0,3},{1,2},{2,1},{3,0},{4,7},{5,6},{6,5},{7,4},{8,11},{9,10},{10,... | collective-permute-start | bytes 1179656 | tf_op jit(solution)/shard_map/ppermute | solution.py:20
  40.2 1.0 copy-start.12
  41.2 1.0 copy-start.14
  55.5 46.6 %collective-permute-start.13 = (bf16[192,3072]{1,0:T(8,128)(2,1)}, bf16[192,3072]{1,0:T(8,128)(2,1)S(1)}, u32[]{:S(2)}, u32[]{:S(2)}) collective-permute-start(bf16[192,3072]{1,0:T(8,128)(2,1)} %get-tuple-element.60), channel_id=1, source_target_pairs={{0,1},{1,0},{2,3},{3,2},{4,5},{5,4},{6,7},{7,6},{8,9},{9,8},{10,11... | collective-permute-start | bytes 3538952 | tf_op jit(solution)/shard_map/ppermute | solution.py:20
  56.1 46.0 %collective-permute-start.14 = (bf16[192,3072]{1,0:T(8,128)(2,1)}, bf16[192,3072]{1,0:T(8,128)(2,1)S(1)}, u32[]{:S(2)}, u32[]{:S(2)}) collective-permute-start(bf16[192,3072]{1,0:T(8,128)(2,1)} %get-tuple-element.61), channel_id=1, source_target_pairs={{0,2},{1,3},{2,0},{3,1},{4,6},{5,7},{6,4},{7,5},{8,10},{9,11},{10,... | collective-permute-start | bytes 3538952 | tf_op jit(solution)/shard_map/ppermute | solution.py:20
  59.4 5.6 %copy-start.4 = (f32[2048,256]{1,0:T(8,128)S(1)}, f32[2048,256]{1,0:T(8,128)}, u32[]{:S(2)}) copy-start(f32[2048,256]{1,0:T(8,128)} %copy-done.3) | copy-start | bytes 6291460
  59.4 5.6 %copy-start.6 = (f32[2048,256]{1,0:T(8,128)S(1)}, f32[2048,256]{1,0:T(8,128)}, u32[]{:S(2)}) copy-start(f32[2048,256]{1,0:T(8,128)} %copy-done.5) | copy-start | bytes 6291460
  59.4 5.9 %copy-start.8 = (f32[2048,256]{1,0:T(8,128)S(1)}, f32[2048,256]{1,0:T(8,128)}, u32[]{:S(2)}) copy-start(f32[2048,256]{1,0:T(8,128)} %copy-done.7) | copy-start | bytes 6291460
  59.4 6.7 %copy-start.9 = (f32[2048,256]{1,0:T(8,128)S(1)}, f32[2048,256]{1,0:T(8,128)}, u32[]{:S(2)}) copy-start(f32[2048,256]{1,0:T(8,128)} %get-tuple-element.70.grad_ref) | copy-start | bytes 6291460
  69.2 2.0 %collective-permute-start.8 = (bf16[4,256,256]{2,1,0:T(8,128)(2,1)S(1)}, bf16[4,256,256]{2,1,0:T(8,128)(2,1)S(1)}, u32[]{:S(2)}, u32[]{:S(2)}) collective-permute-start(bf16[4,256,256]{2,1,0:T(8,128)(2,1)S(1)} %get-tuple-element.74), channel_id=1, source_target_pairs={{0,4},{4,0},{8,12},{12,8},{16,20},{20,16},{24,28},{28,24},{1,5},{5... | collective-permute-start | bytes 1572872 | tf_op jit(solution)/shard_map/ppermute | solution.py:20
  71.9 8.4 %collective-permute-start.9 = (bf16[2,256,256]{2,1,0:T(8,128)(2,1)S(1)}, bf16[2,256,256]{2,1,0:T(8,128)(2,1)S(1)}, u32[]{:S(2)}, u32[]{:S(2)}) collective-permute-start(bf16[2,256,256]{2,1,0:T(8,128)(2,1)S(1)} %get-tuple-element.76), channel_id=1, source_target_pairs={{0,8},{4,12},{8,0},{12,4},{16,24},{20,28},{24,16},{28,20},{1,9},{5... | collective-permute-start | bytes 786440 | tf_op jit(solution)/shard_map/ppermute | solution.py:20
  73.5 10.7 %copy-start = (bf16[2048,1024]{1,0:T(8,128)(2,1)S(1)}, bf16[2048,1024]{1,0:T(8,128)(2,1)}, u32[]{:S(2)}) copy-start(bf16[2048,1024]{1,0:T(8,128)(2,1)} %get-tuple-element.53.refs_6_.weight_ref) | copy-start | bytes 12582916
  80.9 0.7 copy-start.17
  81.6 8.5 %collective-permute-start.11 = (bf16[1,256,256]{2,1,0:T(8,128)(2,1)S(1)}, bf16[1,256,256]{2,1,0:T(8,128)(2,1)S(1)}, u32[]{:S(2)}, u32[]{:S(2)}) collective-permute-start(bf16[1,256,256]{2,1,0:T(8,128)(2,1)S(1)} %get-tuple-element.79), channel_id=1, source_target_pairs={{0,16},{4,20},{8,24},{12,28},{16,0},{20,4},{24,8},{28,12},{1,17},{... | collective-permute-start | bytes 393224 | tf_op jit(solution)/shard_map/ppermute | solution.py:20
  88.5 28.1 %collective-permute-start.10 = (bf16[192,3072]{1,0:T(8,128)(2,1)}, bf16[192,3072]{1,0:T(8,128)(2,1)}, u32[]{:S(2)}, u32[]{:S(2)}) collective-permute-start(bf16[192,3072]{1,0:T(8,128)(2,1)} %shard_map.138), channel_id=1, source_target_pairs={{0,3},{1,2},{2,1},{3,0},{4,7},{5,6},{6,5},{7,4},{8,11},{9,10},{10,... | collective-permute-start | bytes 3538952 | tf_op jit(solution)/shard_map/ppermute | solution.py:20
  90.1 0.6 copy-start.20
  93.4 8.6 %copy-start.21 = (bf16[1,256,256]{2,1,0:T(8,128)(2,1)S(1)}, bf16[1,256,256]{2,1,0:T(8,128)(2,1)}, u32[]{:S(2)}) copy-start(bf16[1,256,256]{2,1,0:T(8,128)(2,1)} %get-tuple-element.84) | copy-start | bytes 393220
  93.4 8.7 %copy-start.16 = (f32[192,1024]{1,0:T(8,128)S(1)}, f32[192,1024]{1,0:T(8,128)}, u32[]{:S(2)}) copy-start(f32[192,1024]{1,0:T(8,128)} %copy-done.15) | copy-start | bytes 2359300
  93.4 8.7 %copy-start.19 = (s32[4]{0:T(128)S(1)}, s32[4]{0:T(128)}, u32[]{:S(2)}) copy-start(s32[4]{0:T(128)} %copy-done.18) | copy-start | bytes 52
  93.4 8.6 %collective-permute-start.12 = (bf16[1,256,256]{2,1,0:T(8,128)(2,1)}, bf16[1,256,256]{2,1,0:T(8,128)(2,1)S(1)}, u32[]{:S(2)}, u32[]{:S(2)}) collective-permute-start(bf16[1,256,256]{2,1,0:T(8,128)(2,1)} %get-tuple-element.84), channel_id=1, source_target_pairs={{0,16},{4,20},{8,24},{12,28},{16,0},{20,4},{24,8},{28,12},{1,17},{... | collective-permute-start | bytes 393224 | tf_op jit(solution)/shard_map/ppermute | solution.py:20
  103.9 7.0 %collective-permute-start.15 = (bf16[2,256,256]{2,1,0:T(8,128)(2,1)S(1)}, bf16[2,256,256]{2,1,0:T(8,128)(2,1)S(1)}, u32[]{:S(2)}, u32[]{:S(2)}) collective-permute-start(bf16[2,256,256]{2,1,0:T(8,128)(2,1)S(1)} %pad_maximum_fusion), channel_id=1, source_target_pairs={{0,8},{4,12},{8,0},{12,4},{16,24},{20,28},{24,16},{28,20},{1,9},{5... | collective-permute-start | bytes 786440 | tf_op jit(solution)/shard_map/ppermute | solution.py:20
  110.8 2.0 %collective-permute-start.16 = (bf16[4,256,256]{2,1,0:T(8,128)(2,1)S(1)}, bf16[4,256,256]{2,1,0:T(8,128)(2,1)S(1)}, u32[]{:S(2)}, u32[]{:S(2)}) collective-permute-start(bf16[4,256,256]{2,1,0:T(8,128)(2,1)S(1)} %constant_dynamic-update-slice_fusion.2.same_ref), channel_id=1, source_target_pairs={{0,4},{4,0},{8,12},{12,8},{16,20},{20,16},{24,28},{28,24},{1,5},{5... | collective-permute-start | bytes 1572872 | tf_op jit(solution)/shard_map/ppermute | solution.py:20

commit v3 on v2

v3 whole, which is shorter than its diff:
```python
import functools
import math

import jax
import jax.numpy as jnp
from jax import lax
from jax.experimental import pallas as pl
from jax.experimental.pallas import tpu as pltpu
from jax.sharding import PartitionSpec as P

FRAGS = 4
ROUNDS = 8
MIB = 1024 * 1024
VMEM = 48 * MIB
SMALL = pl.CostEstimate(flops=1, bytes_accessed=1, transcendentals=0)


def pair(x, axis, offset):
    size = lax.axis_size(axis)
    return lax.ppermute(x, axis, [(i, i ^ offset) for i in range(size)])


def after(x, *others):
    return lax.optimization_barrier((x, *others))[0]


def row_dot(hid, cot, factor):
    part = lax.dot_general(
        hid, cot, (((0,), (0,)), ((), ())), preferred_element_type=jnp.float32
    )
    return (part * factor).astype(jnp.bfloat16).astype(jnp.float32)


def frag_of_ref(ref, where_ref, like_ref):
    cols = like_ref.shape[-1]
    return ref[:, pl.ds(pl.multiple_of(where_ref[1] * cols, cols), cols)]


def part_sum(hids, cots, factor):
    total = row_dot(hids[0][...], cots[0], factor)
    for hid, cot in zip(hids[1:], cots[1:]):
        total = total + row_dot(hid[...], cot, factor)
    return total


def dot_keys(hid, weight):
    return jnp.dot(hid, weight, preferred_element_type=jnp.float32)


def dot_back(cot, weight, factor):
    out = lax.dot_general(
        cot, weight, (((1,), (1,)), ((), ())), preferred_element_type=jnp.float32
    )
    return (out * factor).astype(jnp.bfloat16)


def add_keys(ref, value):
    @pl.when(pl.program_id(0) == 0)
    def _():
        ref[...] = value

    @pl.when(pl.program_id(0) > 0)
    def _():
        ref[...] += value


def send_kernel(peers, where_ref, *refs):
    hids, cot_ref, outs = refs[:peers], refs[peers], refs[peers + 1 :]
    head = pl.program_id(0) == 0
    for hid_ref, out_ref in zip(hids, outs):
        out_ref[...] = jnp.where(head, cot_ref[...], hid_ref[...])


def send_call(tokens, cot, rows, shard, offsets):
    toks, keys = cot.shape
    steps = rows // keys

    def column(m):
        return pl.BlockSpec(
            (toks, keys), lambda i, w, m=m: (0, (w[0] ^ m) * steps + jnp.maximum(i - 1, 0))
        )

    return pl.pallas_call(
        functools.partial(send_kernel, len(offsets)),
        grid_spec=pltpu.PrefetchScalarGridSpec(
            num_scalar_prefetch=1,
            grid=(1 + steps,),
            in_specs=[column(m) for m in offsets] + [pl.BlockSpec((toks, keys), lambda i, w: (0, 0))],
            out_specs=[pl.BlockSpec((toks, keys), lambda i, w: (0, i))] * len(offsets),
        ),
        out_shape=[jax.ShapeDtypeStruct((toks, keys + rows), cot.dtype)] * len(offsets),
        cost_estimate=SMALL,
    )(shard.reshape(1).astype(jnp.int32), *[tokens] * len(offsets), cot)


def own_kernel(factor, where_ref, tokens_ref, cot_ref, weight_ref, half_ref, back_ref, keys_ref):
    half = weight_ref[...].astype(jnp.bfloat16)
    half_ref[...] = half
    back_ref[...] = dot_back(cot_ref[...], half, factor)
    add_keys(keys_ref, dot_keys(tokens_ref[...], half))


def own_call(tokens, cot, weight, where, factor, tile):
    rows, keys = weight.shape
    toks, width = tokens.shape
    steps = rows // tile
    here = pl.BlockSpec((toks, tile), lambda i, w: (0, w[0] * steps + i))
    block = pl.BlockSpec((tile, keys), lambda i, w: (i, 0))
    whole = pl.BlockSpec((toks, keys), lambda i, w: (0, 0))
    return pl.pallas_call(
        functools.partial(own_kernel, factor),
        grid_spec=pltpu.PrefetchScalarGridSpec(
            num_scalar_prefetch=1,
            grid=(steps,),
            in_specs=[here, whole, block],
            out_specs=[block, here, whole],
        ),
        out_shape=[
            jax.ShapeDtypeStruct((rows, keys), jnp.bfloat16),
            jax.ShapeDtypeStruct((toks, width), jnp.bfloat16),
            jax.ShapeDtypeStruct((toks, keys), jnp.float32),
        ],
        compiler_params=pltpu.CompilerParams(vmem_limit_bytes=VMEM),
        cost_estimate=SMALL,
    )(where, tokens, cot, weight)


def pack(outs, accs, hids, cots, weight, factor, step, steps):
    toks = hids[0].shape[0]
    tile = weight.shape[0]
    rows = tile * steps
    at = pl.ds(pl.multiple_of(step * tile, tile), tile)
    back = dot_back(jnp.concatenate(cots, axis=0), weight, factor)
    part = dot_keys(jnp.concatenate(hids, axis=0), weight)
    for g, (out, acc) in enumerate(zip(outs, accs)):
        mine = slice(g * toks, (g + 1) * toks)
        out[:, at] = back[mine]
        add_keys(acc, part[mine])

    @pl.when(step == steps - 1)
    def _():
        for out, acc in zip(outs, accs):
            out[:, rows:] = acc[...].astype(out.dtype)


def near_kernel(groups, factor, steps, where_ref, *refs):
    hids, cots, weight_ref = refs[:groups], refs[groups : 2 * groups], refs[2 * groups]
    frag_ref, *outs = refs[2 * groups + 1 :]
    frag_ref[...] = part_sum(hids, [frag_of_ref(c, where_ref, frag_ref) for c in cots], factor)
    peers = groups - 1
    pack(
        outs[:peers], outs[peers:], [h[...] for h in hids[1:]], [c[...] for c in cots[1:]],
        weight_ref[...], factor, pl.program_id(0), steps,
    )


def near_call(tokens, cot, packs, weight_half, where, factor, tile, frag_cols):
    rows, keys = weight_half.shape
    toks = tokens.shape[0]
    peers = len(packs)
    groups = peers + 1
    steps = rows // tile
    skip = keys // tile
    block = pl.BlockSpec((tile, keys), lambda i, w: (i, 0))
    whole = pl.BlockSpec((toks, keys), lambda i, w: (0, 0))
    column = pl.BlockSpec((toks, tile), lambda i, w: (0, skip + i))
    out = pl.pallas_call(
        functools.partial(near_kernel, groups, factor, steps),
        grid_spec=pltpu.PrefetchScalarGridSpec(
            num_scalar_prefetch=1,
            grid=(steps,),
            in_specs=[pl.BlockSpec((toks, tile), lambda i, w: (0, w[0] * steps + i))]
            + [column] * peers
            + [whole] * groups
            + [block],
            out_specs=[pl.BlockSpec((tile, frag_cols), lambda i, w: (i, 0))]
            + [pl.BlockSpec((toks, rows + keys), lambda i, w: (0, 0))] * peers,
            scratch_shapes=[pltpu.VMEM((toks, keys), jnp.float32)] * peers,
        ),
        out_shape=[jax.ShapeDtypeStruct((rows, frag_cols), jnp.float32)]
        + [jax.ShapeDtypeStruct((toks, rows + keys), jnp.bfloat16)] * peers,
        compiler_params=pltpu.CompilerParams(vmem_limit_bytes=VMEM),
        cost_estimate=SMALL,
    )(where, tokens, *packs, cot, *packs, weight_half)
    return out[0], list(out[1:])


def last_kernel(factor, steps, hid_ref, weight_ref, *refs):
    *cots, out_ref, acc_ref = refs
    cot = jnp.concatenate([c[...] for c in cots], axis=0)
    pack(
        [out_ref], [acc_ref], [hid_ref[...]], [cot], weight_ref[...], factor, pl.program_id(0), steps
    )


def last_call(hid, cots, weight_half, factor, tile):
    rows, keys = weight_half.shape
    toks = hid.shape[0]
    steps = rows // tile
    return pl.pallas_call(
        functools.partial(last_kernel, factor, steps),
        grid=(steps,),
        in_specs=[
            pl.BlockSpec((toks, tile), lambda i: (0, i)),
            pl.BlockSpec((tile, keys), lambda i: (i, 0)),
        ]
        + [pl.BlockSpec(c.shape, lambda i: (0, 0)) for c in cots],
        out_specs=pl.BlockSpec((toks, rows + keys), lambda i: (0, 0)),
        out_shape=jax.ShapeDtypeStruct((toks, rows + keys), jnp.bfloat16),
        scratch_shapes=[pltpu.VMEM((toks, keys), jnp.float32)],
        compiler_params=pltpu.CompilerParams(vmem_limit_bytes=32 * MIB),
        cost_estimate=SMALL,
    )(hid, weight_half, *cots)


def adam_step(grad, weight, first, second, scal_ref):
    first = scal_ref[0] * first + scal_ref[1] * grad
    second = scal_ref[2] * second + scal_ref[3] * (grad * grad)
    return 0.99 * weight - 0.1 * (first / (jnp.sqrt(second) + 1e-08))


def frag_kernel(factor, where_ref, scal_ref, hid_ref, *refs):
    *cots, grad_ref, weight_ref, first_ref, second_ref, keep_ref, give_ref, here_ref, sems = refs
    chips, size = keep_ref.shape[:2]
    cols = keep_ref.shape[2]
    even_mine = where_ref[2] == 0
    column = pl.ds(pl.multiple_of(where_ref[1] * cols, cols), cols)
    copies = []
    for j in range(chips):
        at = pl.ds(2 * j * size, 2 * size)
        sources = [grad_ref.at[at, :]] + [
            x.at[at, column] for x in (weight_ref, first_ref, second_ref)
        ]
        copies.append(
            [
                pltpu.make_async_copy(source, here_ref.at[i, at, :], sems.at[i, j])
                for i, source in enumerate(sources)
            ]
        )
        for copy in copies[-1]:
            copy.start()
    cot = jnp.concatenate([c[:, column] for c in cots], axis=0)
    for j in range(chips):
        at = pl.ds(2 * j * size, 2 * size)
        part = row_dot(hid_ref[:, at], cot, factor)
        for copy in copies[j]:
            copy.wait()
        inner = adam_step(
            here_ref[0, at, :] + part, here_ref[1, at, :], here_ref[2, at, :], here_ref[3, at, :],
            scal_ref,
        )
        even, odd = inner[:size], inner[size:]
        keep_ref[j] = jnp.where(even_mine, even, odd).astype(keep_ref.dtype)
        give_ref[j] = jnp.where(even_mine, odd, even).astype(give_ref.dtype)


def local_call(kernel, outs, *args, smem=1, limit=24):
    vmem = pl.BlockSpec(memory_space=pltpu.VMEM)
    return pl.pallas_call(
        kernel,
        in_specs=[pl.BlockSpec(memory_space=pltpu.SMEM)] * smem + [vmem] * (len(args) - smem),
        out_specs=[vmem] * len(outs),
        out_shape=outs,
        compiler_params=pltpu.CompilerParams(vmem_limit_bytes=limit * MIB),
        cost_estimate=SMALL,
    )(*args)


def frag_call(hid, cots, grad, weight, first, second, where, scal, factor, own_rows):
    rows, cols = grad.shape
    chips = rows // (2 * own_rows)
    vmem = pl.BlockSpec(memory_space=pltpu.VMEM)
    out = jax.ShapeDtypeStruct((chips, own_rows, cols), jnp.bfloat16)
    return pl.pallas_call(
        functools.partial(frag_kernel, factor),
        in_specs=[pl.BlockSpec(memory_space=pltpu.SMEM)] * 2
        + [vmem] * (1 + len(cots))
        + [pl.BlockSpec(memory_space=pl.ANY)] * 4,
        out_specs=[vmem, vmem],
        out_shape=[out, out],
        scratch_shapes=[
            pltpu.VMEM((4, rows, cols), jnp.float32), pltpu.SemaphoreType.DMA((4, chips))
        ],
        compiler_params=pltpu.CompilerParams(vmem_limit_bytes=VMEM),
        cost_estimate=SMALL,
    )(where, scal, hid, *cots, grad, weight, first, second)


def split_kernel(bit, where_ref, mine_ref, got_ref, stay_ref, leave_ref):
    low = ((where_ref[3] >> bit) & 1) == 0
    for i in range(stay_ref.shape[0]):
        sums = [
            mine_ref[j].astype(jnp.float32) + got_ref[j].astype(jnp.float32)
            for j in (2 * i, 2 * i + 1)
        ]
        stay_ref[i] = jnp.where(low, sums[0], sums[1])
        leave_ref[i] = jnp.where(low, sums[1], sums[0]).astype(leave_ref.dtype)


def split_call(bit, where, mine, got):
    shape = (mine.shape[0] // 2,) + mine.shape[1:]
    return local_call(
        functools.partial(split_kernel, bit),
        [jax.ShapeDtypeStruct(shape, jnp.float32), jax.ShapeDtypeStruct(shape, jnp.bfloat16)],
        where, mine, got,
    )


def halves_kernel(x_ref, y_ref, low_ref, high_ref):
    low_ref[...] = y_ref[...]
    high_ref[...] = x_ref[...]


def halves_call(pack_x, pack_y, keys):
    half = pack_x.shape[0] // 2
    first = pl.BlockSpec((half, keys), lambda i: (0, 0))
    second = pl.BlockSpec((half, keys), lambda i: (1, 0))
    return pl.pallas_call(
        halves_kernel,
        grid=(1,),
        in_specs=[second, first],
        out_specs=[first, first],
        out_shape=[jax.ShapeDtypeStruct((half, keys), pack_x.dtype)] * 2,
        cost_estimate=SMALL,
    )(pack_x, pack_y)


def copy_kernel(count, where_ref, *refs):
    for i in range(count):
        refs[count + i][...] = refs[i][...]
        refs[2 * count + i][...] = frag_of_ref(refs[i], where_ref, refs[2 * count + i])


def copy_call(where, arrays, frag_cols):
    count = len(arrays)
    rows, cols = arrays[0].shape
    block = pl.BlockSpec((rows // 2, cols), lambda i, w: (i, 0))
    part = pl.BlockSpec((rows // 2, frag_cols), lambda i, w: (i, 0))
    return pl.pallas_call(
        functools.partial(copy_kernel, count),
        grid_spec=pltpu.PrefetchScalarGridSpec(
            num_scalar_prefetch=1,
            grid=(2,),
            in_specs=[block] * count,
            out_specs=[block] * count + [part] * count,
        ),
        out_shape=[jax.ShapeDtypeStruct(x.shape, x.dtype) for x in arrays]
        + [jax.ShapeDtypeStruct((rows, frag_cols), x.dtype) for x in arrays],
        compiler_params=pltpu.CompilerParams(vmem_limit_bytes=VMEM),
        cost_estimate=SMALL,
    )(where, *arrays)


def outer_step(replicas, stay_ref, got_ref, now_ref, mom_ref):
    total = stay_ref[0] + got_ref[0].astype(jnp.float32)
    pseudo = now_ref[...] - total / replicas
    moment = 0.9 * mom_ref[...] + pseudo
    return now_ref[...] - 0.7 * (pseudo + 0.9 * moment), moment


def outer_kernel(replicas, *refs):
    spread_ref = refs[-1]
    spread_ref[0] = outer_step(replicas, *refs[:-1])[0].astype(spread_ref.dtype)


def outer_call(replicas, stay, got, now, mom):
    return local_call(
        functools.partial(outer_kernel, replicas),
        [jax.ShapeDtypeStruct(got.shape, got.dtype)],
        stay, got, now, mom, smem=0,
    )[0]


def put_kernel(replicas, where_ref, stay_ref, got_ref, now_ref, mom_ref, _, __, out_ref, out_mom_ref, outer_ref, moment_ref, sems):
    outer_ref[...], moment_ref[...] = outer_step(replicas, stay_ref, got_ref, now_ref, mom_ref)
    cols = now_ref.shape[1]
    at = pl.ds(pl.multiple_of(where_ref[1] * cols, cols), cols)
    copies = [
        pltpu.make_async_copy(outer_ref, out_ref.at[:, at], sems.at[0]),
        pltpu.make_async_copy(moment_ref, out_mom_ref.at[:, at], sems.at[1]),
    ]
    for copy in copies:
        copy.start()
    for copy in copies:
        copy.wait()


def put_call(replicas, where, stay, got, now, mom, now_copy, mom_copy):
    vmem = pl.BlockSpec(memory_space=pltpu.VMEM)
    anywhere = pl.BlockSpec(memory_space=pl.ANY)
    return pl.pallas_call(
        functools.partial(put_kernel, replicas),
        in_specs=[pl.BlockSpec(memory_space=pltpu.SMEM)] + [vmem] * 4 + [anywhere] * 2,
        out_specs=[anywhere] * 2,
        out_shape=[jax.ShapeDtypeStruct(now_copy.shape, now_copy.dtype)] * 2,
        input_output_aliases={5: 0, 6: 1},
        scratch_shapes=[pltpu.VMEM(now.shape, now.dtype)] * 2 + [pltpu.SemaphoreType.DMA((2,))],
        compiler_params=pltpu.CompilerParams(vmem_limit_bytes=24 * MIB),
        cost_estimate=SMALL,
    )(where, stay, got, now, mom, now_copy, mom_copy)


def place_kernel(offsets, final, factor, where_ref, *refs):
    count = len(offsets)
    msgs = refs[:count]
    acc_ref, _, back_ref, keys_ref, sems = refs[count:]
    toks, keys = acc_ref.shape
    rows = msgs[0].shape[1] - keys
    copies = []
    for i, m in enumerate(offsets):
        start = pl.multiple_of((where_ref[0] ^ m) * rows, rows)
        copy = pltpu.make_async_copy(
            msgs[i].at[:, pl.ds(0, rows)], back_ref.at[:, pl.ds(start, rows)], sems.at[i]
        )
        copy.start()
        copies.append(copy)
    total = acc_ref[...]
    for msg in msgs:
        total = total + msg[:, rows:].astype(jnp.float32)
    if final:
        total = total * factor
    keys_ref[...] = total.astype(keys_ref.dtype)
    for copy in copies:
        copy.wait()


def place_call(where, msgs, acc, back, offsets, final, factor):
    vmem = pl.BlockSpec(memory_space=pltpu.VMEM)
    anywhere = pl.BlockSpec(memory_space=pl.ANY)
    count = len(msgs)
    return pl.pallas_call(
        functools.partial(place_kernel, tuple(offsets), final, factor),
        in_specs=[pl.BlockSpec(memory_space=pltpu.SMEM)] + [vmem] * (count + 1) + [anywhere],
        out_specs=[anywhere, vmem],
        out_shape=[
            jax.ShapeDtypeStruct(back.shape, back.dtype),
            jax.ShapeDtypeStruct(acc.shape, jnp.bfloat16 if final else jnp.float32),
        ],
        input_output_aliases={count + 2: 0},
        scratch_shapes=[pltpu.SemaphoreType.DMA((count,))],
        compiler_params=pltpu.CompilerParams(vmem_limit_bytes=24 * MIB),
        cost_estimate=SMALL,
    )(where, *msgs, acc, back)


def adam_kernel(groups, pieces, factor, where_ref, scal_ref, *refs):
    hids, refs = refs[:groups], refs[groups:]
    cots = [c[...] for c in refs[: groups - 1]]
    weight_ref, first_ref, second_ref = refs[groups - 1 : groups + 2]
    *rest, out_ref = refs[groups + 2 :]
    cots.append(jnp.concatenate([c[...] for c in rest[:pieces]], axis=0))
    grad = part_sum(hids, cots, factor)
    out_ref[...] = adam_step(grad, weight_ref[...], first_ref[...], second_ref[...], scal_ref)


def adam_call(tokens, cot, packs, hid_last, cot_last, weight, first, second, where, scal, factor, frag_cols, part, *base):
    rows, keys = weight.shape
    toks = tokens.shape[0]
    tile = min(1024, rows // 2)
    steps = rows // tile
    lo = part * (steps // 2)
    skip = keys // tile
    groups = len(packs) + 2

    def col(j, w):
        return j + (j >= w[1]).astype(jnp.int32)

    def block(height):
        return pl.BlockSpec((height, frag_cols), lambda i, j, w: (0, col(j, w)))

    state = pl.BlockSpec((tile, frag_cols), lambda i, j, w: (lo + i, col(j, w)))
    return pl.pallas_call(
        functools.partial(adam_kernel, groups, len(cot_last), factor),
        grid_spec=pltpu.PrefetchScalarGridSpec(
            num_scalar_prefetch=1,
            grid=(steps // 2, keys // frag_cols - 1),
            in_specs=[
                pl.BlockSpec(memory_space=pltpu.SMEM),
                pl.BlockSpec((toks, tile), lambda i, j, w: (0, w[0] * steps + lo + i)),
            ]
            + [pl.BlockSpec((toks, tile), lambda i, j, w: (0, skip + lo + i))] * len(packs)
            + [pl.BlockSpec((toks, tile), lambda i, j, w: (0, lo + i))]
            + [block(toks)] * (groups - 1)
            + [state] * 3
            + [block(c.shape[0]) for c in cot_last]
            + [pl.BlockSpec(memory_space=pl.ANY)] * len(base),
            out_specs=state,
        ),
        out_shape=jax.ShapeDtypeStruct((rows, keys), jnp.float32),
        input_output_aliases={4 + 2 * groups + len(cot_last): 0} if base else {},
        compiler_params=pltpu.CompilerParams(vmem_limit_bytes=VMEM),
        cost_estimate=SMALL,
    )(where, scal, tokens, *packs, hid_last, cot, *packs, weight, first, second, *cot_last, *base)


def spread_kernel(bits, where_ref, same_ref, other_ref, base_ref, out_ref, wide_ref, sems):
    chips, size, cols = same_ref.shape
    column = pl.ds(pl.multiple_of(where_ref[1] * cols, cols), cols)
    core = where_ref[2]
    copies = []
    for j in range(chips):
        offset = j ^ where_ref[3]
        at = 0
        for i, k in enumerate(reversed(bits)):
            at = at + (((offset >> k) & 1) << i)
        wide_ref[2 * j + core] = same_ref[at].astype(wide_ref.dtype)
        wide_ref[2 * j + 1 - core] = other_ref[at].astype(wide_ref.dtype)
        for b in (2 * j, 2 * j + 1):
            copy = pltpu.make_async_copy(
                wide_ref.at[b], out_ref.at[pl.ds(b * size, size), column], sems.at[b]
            )
            copy.start()
            copies.append(copy)
    for copy in copies:
        copy.wait()


def spread_call(bits, where, same, other, base):
    chips, size, cols = same.shape
    vmem = pl.BlockSpec(memory_space=pltpu.VMEM)
    anywhere = pl.BlockSpec(memory_space=pl.ANY)
    return pl.pallas_call(
        functools.partial(spread_kernel, bits),
        in_specs=[pl.BlockSpec(memory_space=pltpu.SMEM), vmem, vmem, anywhere],
        out_specs=anywhere,
        out_shape=jax.ShapeDtypeStruct(base.shape, base.dtype),
        input_output_aliases={3: 0},
        scratch_shapes=[
            pltpu.VMEM((2 * chips, size, cols), base.dtype),
            pltpu.SemaphoreType.DMA((2 * chips,)),
        ],
        compiler_params=pltpu.CompilerParams(vmem_limit_bytes=24 * MIB),
        cost_estimate=SMALL,
    )(where, same, other, base)


def per_device(
    hidden,
    key_cotangent,
    local_weight,
    adam_first,
    adam_second,
    outer_weight,
    outer_momentum,
    roster,
    step_count,
):
    tokens = hidden[0]
    cotangent = key_cotangent[0]
    weight = local_weight[0]
    outer_now = outer_weight[0]
    moment_now = outer_momentum[0]
    toks, width = tokens.shape
    rows, keys = weight.shape
    factor = 1.0 / math.sqrt(width)
    frag_cols = keys // FRAGS
    shards = lax.axis_size("fsdp")
    replicas = lax.axis_size("rep")
    shard = lax.axis_index("fsdp")
    replica = lax.axis_index("rep")
    offsets = list(range(1, shards))

    fragment = roster[step_count[0] // FRAGS % ROUNDS, step_count[0] % FRAGS]
    steps_done = (step_count[0] + 1).astype(jnp.float32)
    scale1 = 1.0 / (1.0 - jnp.power(jnp.float32(0.9), steps_done))
    scale2 = 1.0 / (1.0 - jnp.power(jnp.float32(0.95), steps_done))
    scal = jnp.stack([0.9 * scale1, 0.1 * scale1, 0.95 * scale2, 0.05 * scale2])
    chips = replicas // 2
    core, chip = replica % 2, replica // 2
    own_rows = rows // replicas
    where = jnp.stack([shard, fragment, core, chip]).astype(jnp.int32)
    square = shards == 4
    tile = min(512, rows // 4)

    def hid_for(source, m):
        return lax.dynamic_slice_in_dim(source, (shard ^ m) * rows, rows, 1)

    sends = send_call(tokens, cotangent, rows, shard, offsets[:-1])
    packs = [pair(x, "fsdp", m) for x, m in zip(sends, offsets)]

    first, second = adam_first[0], adam_second[0]
    weight_half, back_out, key_acc = own_call(tokens, cotangent, weight, where, factor, tile)
    outer_copy, moment_copy, *outer_frag = copy_call(
        after(where, weight_half), [outer_now, moment_now], frag_cols
    )
    hid_last = hid_for(after(tokens, weight_half), offsets[-1])
    hid_last = pair(after(hid_last, outer_copy, *packs), "fsdp", offsets[-1])
    if square:
        low, high = halves_call(after(packs[0], outer_copy), packs[1], keys)
        cot_last = [pair(low, "fsdp", 1), pair(high, "fsdp", 2)]
    else:
        cot_last = [pair(cotangent, "fsdp", offsets[-1])]
    grad_frag, gives = near_call(
        tokens, cotangent, packs, weight_half, after(where, outer_copy), factor, tile, frag_cols
    )
    backs = [pair(x, "fsdp", m) for x, m in zip(gives, offsets)]
    cot_last = [after(c, *gives) for c in cot_last]

    def inner_half(part, hid, *base):
        return adam_call(
            tokens, cotangent, packs, hid, cot_last, weight, first, second, where, scal, factor,
            frag_cols, part, *base,
        )

    keep, give = frag_call(
        hid_last, cot_last, grad_frag, weight, first, second, where, scal, factor, own_rows
    )
    got = pair(give, "rep", 1)
    bits = [k for k in range(chips.bit_length()) if (1 << k) < chips]
    for k in bits:
        keep, leave = split_call(k, where, keep, got)
        got = pair(leave, "rep", 2 << k)
        if k == 0:
            give_last = last_call(after(hid_last, leave), cot_last, weight_half, factor, tile)
            got = after(got, give_last)
        if k == bits[-1]:
            inner = inner_half(0, after(hid_last, leave, give_last))
            got = after(got, inner)
    backs.append(pair(give_last, "fsdp", offsets[-1]))
    outer_args = (keep, got, *outer_frag)
    spread = outer_call(replicas, *outer_args)
    for k in reversed(bits):
        got = pair(spread, "rep", 2 << k)
        if k == bits[-1]:
            outer_next, moment_next = put_call(
                replicas, where, after(keep, spread), *outer_args[1:], outer_copy, moment_copy
            )
            back_out, key_acc = place_call(
                where, [after(b, outer_next) for b in backs[:-1]], key_acc, back_out, offsets[:-1],
                False, factor,
            )
            got = after(got, key_acc)
        if k == 0:
            inner = inner_half(1, after(hid_last, spread), inner)
            got = after(got, inner)
        spread = jnp.concatenate([spread, got], axis=0)
    got = pair(spread, "rep", 1)
    new_local = spread_call(bits, where, spread, got, inner)
    back_out, keys_out = place_call(
        where, [after(backs[-1], new_local)], key_acc, back_out, offsets[-1:], True, factor
    )

    return (keys_out[None], back_out[None], new_local[None], outer_next[None], moment_next[None])


def solution(mesh):
    in_specs = (
        P("rep", "fsdp", None),
        P("rep", "fsdp", None),
        P("rep", "fsdp", None),
        P("rep", "fsdp", None),
        P("rep", "fsdp", None),
        P("fsdp", "rep", None),
        P("fsdp", "rep", None),
        P(),
        P(),
    )
    out_specs = (
        P("rep", "fsdp", None),
        P("rep", "fsdp", None),
        P("rep", "fsdp", None),
        P("fsdp", "rep", None),
        P("fsdp", "rep", None),
    )
    return jax.shard_map(
        per_device, mesh=mesh, in_specs=in_specs, out_specs=out_specs, check_vma=False
    )
```

time: 120 us -> 117 us (0.975)
  waiting for transfers between devices: 13.4 us -> 29.4 us
  local copies, waits for them, and re-layouts: 17.7 us -> 6.21 us
  starting transfers between devices: 19.1 us -> 15.3 us
  Pallas kernels: 66.1 us -> 63 us
    ppermute x17 -> x14, waiting for transfers between devices: 13.4 us -> 29.4 us  [pair(): return lax.ppermute(x, axis, [(i, i ^ offset) for i in range(size)])]
    unnamed x46 -> x24, local copies, waits for them, and re-layouts: 10.6 us -> 3.98 us
    pallas_call x7, Pallas kernels: 28.9 us -> 33.5 us  [the longest x2 18.6 us: adam_call(): pl.pallas_call(functools.partial(adam_kernel, groups, len(cot_last), fact...]
    ppermute x17 -> x14, starting transfers between devices: 19.1 us -> 15.3 us  [pair(): return lax.ppermute(x, axis, [(i, i ^ offset) for i in range(size)])]
    pallas_call x1, Pallas kernels: 13.3 us -> 10 us  [near_call(): pl.pallas_call(functools.partial(near_kernel, groups, factor, steps), gri...]
    pallas_call x4 -> x3, Pallas kernels: 4.41 us -> 1.4 us  [local_call(): pl.pallas_call(kernel, in_specs=[pl.BlockSpec(memory_space=pltpu.SMEM)] *...]
    slice x1 -> x0, local copies, waits for them, and re-layouts: 2.05 us -> none  [per_device(): lasts = [last[:, :rows // 2], last[:, rows // 2:]]]
    dynamic_slice x1, local copies, waits for them, and re-layouts: 2.74 us -> 0.96 us  [hid_for(): return lax.dynamic_slice_in_dim(source, (shard ^ m) * rows, rows, 1)]
  transfers between devices with their start and end apart: 17 -> 14, of which waited for: 7 -> 8; matrix products, arithmetic and copies ran while one was open for 5% -> 3% of each run, Pallas kernels for 53% -> 49%
where the time goes in v3:
time: 117 us; the launch traced here: 116 us
  Pallas kernels  63 us (54%)
  waiting for transfers between devices  29.4 us (25%)
  starting transfers between devices  15.3 us (13%)
  local copies, waits for them, and re-layouts  6.21 us (5%)
  between operations  1.74 us (1%)
    ppermute x14, waiting for transfers between devices, pair(): return lax.ppermute(x, axis, [(i, i ^ offset) for i in range(size)])  29.4 us
    pallas_call x2, Pallas kernels, adam_call(): pl.pallas_call(functools.partial(adam_kernel, groups, len(cot_last), fact...  18.6 us
    ppermute x14, starting transfers between devices, pair(): return lax.ppermute(x, axis, [(i, i ^ offset) for i in range(size)])  15.3 us
    pallas_call x1, Pallas kernels, near_call(): pl.pallas_call(functools.partial(near_kernel, groups, factor, steps), gri...  10 us
    pallas_call x1, Pallas kernels, own_call(): pl.pallas_call(functools.partial(own_kernel, factor), grid_spec=pltpu.Pre...  8.21 us
    pallas_call x1, Pallas kernels, frag_call(): pl.pallas_call(functools.partial(frag_kernel, factor), in_specs=[pl.Block...  5.52 us
    pallas_call x2, Pallas kernels, place_call(): pl.pallas_call(functools.partial(place_kernel, tuple(offsets), final, fac...  4.63 us
    pallas_call x1, Pallas kernels, send_call(): pl.pallas_call(functools.partial(send_kernel, len(offsets)), grid_spec=pl...  4.19 us
  transfers between devices with their start and end apart: 14, of which 8 were waited for; matrix products, arithmetic and copies ran while one was open for 3% of the time, Pallas kernels for 49%

profile of v3, /device:TPU:0, one launch (start us, length us, event | category | flops | bytes accessed | tf_op | source)
XLA Modules:
  0.0 116.5 jit_solution(10649299967690788524)
XLA Ops:
  0.6 0.0 copy-start
  0.7 4.2 %shard_map.130 = (bf16[192,3072]{1,0:T(8,128)(2,1)}, bf16[192,3072]{1,0:T(8,128)(2,1)}) custom-call(s32[1]{0:T(128)} %bitcast.where_ref, bf16[192,8192]{1,0:T(8,128)(2,1)} %bitcast.26, bf16[192,8192]{1,0:T(8,128)(2,1)} %bitcast.27, bf16[192,1024]{1,0:T(8,128)(2,1)} %bitcast.33), custom_call_target="tpu_custom_call" | custom-call | flops 1 | bytes 1 | tf_op jit(solution)/shard_map/pallas_call | solution.py:83
  4.9 2.9 %collective-permute-start = (bf16[192,3072]{1,0:T(8,128)(2,1)}, bf16[192,3072]{1,0:T(8,128)(2,1)}, u32[]{:S(2)}, u32[]{:S(2)}) collective-permute-start(bf16[192,3072]{1,0:T(8,128)(2,1)} %get-tuple-element.53), channel_id=1, source_target_pairs={{0,1},{1,0},{2,3},{3,2},{4,5},{5,4},{6,7},{7,6},{8,9},{9,8},{10,11... | collective-permute-start | bytes 3538952 | tf_op jit(solution)/shard_map/ppermute | solution.py:20
  7.8 1.5 %collective-permute-start.1 = (bf16[192,3072]{1,0:T(8,128)(2,1)}, bf16[192,3072]{1,0:T(8,128)(2,1)}, u32[]{:S(2)}, u32[]{:S(2)}) collective-permute-start(bf16[192,3072]{1,0:T(8,128)(2,1)} %get-tuple-element.54), channel_id=1, source_target_pairs={{0,2},{1,3},{2,0},{3,1},{4,6},{5,7},{6,4},{7,5},{8,10},{9,11},{10,... | collective-permute-start | bytes 3538952 | tf_op jit(solution)/shard_map/ppermute | solution.py:20
  10.0 1.3 %dynamic_slice.6 = s32[1,1]{0,1:T(1,128)} dynamic-slice(s32[8,4]{0,1:T(4,128)} %param.16, s32[]{:T(128)S(6)} %select_n.33, s32[]{:T(128)S(6)} %select_n.35), dynamic_slice_sizes={1,1} | dynamic-slice | bytes 12 | tf_op jit(solution)/shard_map/dynamic_slice | solution.py:563
  11.3 0.7 pad_add_fusion.where_ref
  12.0 8.2 %shard_map.128 = (bf16[2048,1024]{1,0:T(8,128)(2,1)}, bf16[192,8192]{1,0:T(8,128)(2,1)}, f32[192,1024]{1,0:T(8,128)S(1)}) custom-call(s32[4]{0:T(128)S(1)} %pad_add_fusion.where_ref, bf16[192,8192]{1,0:T(8,128)(2,1)S(1)} %bitcast.31, bf16[192,1024]{1,0:T(8,128)(2,1)S(1)} %bitcast.34, f32[2048,1024]{1,0:T(8,128)} %bitcast.40), custom_call_target="tpu_custom_call" | custom-call | flops 1 | bytes 1 | tf_op jit(solution)/shard_map/pallas_call | solution.py:110
  20.2 0.9 copy-done.10
  21.2 2.0 %shard_map.129 = (f32[256,1024]{1,0:T(8,128)}, f32[256,1024]{1,0:T(8,128)}, f32[256,256]{1,0:T(8,128)S(1)}, f32[256,256]{1,0:T(8,128)S(1)}) custom-call(s32[4]{0:T(128)S(1)} %pad_add_fusion.where_ref, f32[256,1024]{1,0:T(8,128)S(1)} %bitcast.38, f32[256,1024]{1,0:T(8,128)S(1)} %bitcast.39), custom_call_target="tpu_custom_call" | custom-call | flops 1 | bytes 1 | tf_op jit(solution)/shard_map/pallas_call | solution.py:339
  23.2 0.7 copy-done.6
  23.9 0.7 copy-done.8
  24.6 1.0 constant_dynamic-slice_fusion
  25.5 8.5 %collective-permute-done.x_ref.refs_1_.refs_4_.refs_5_ = bf16[192,3072]{1,0:T(8,128)(2,1)} collective-permute-done((bf16[192,3072]{1,0:T(8,128)(2,1)}, bf16[192,3072]{1,0:T(8,128)(2,1)}, u32[]{:S(2)}, u32[]{:S(2)}) %collective-permute-start) | collective-permute-done | bytes 1179680 | tf_op jit(solution)/shard_map/ppermute | solution.py:20
  34.1 1.5 %collective-permute-done.1.y_ref.refs_2_.refs_5_.refs_6_ = bf16[192,3072]{1,0:T(8,128)(2,1)} collective-permute-done((bf16[192,3072]{1,0:T(8,128)(2,1)}, bf16[192,3072]{1,0:T(8,128)(2,1)}, u32[]{:S(2)}, u32[]{:S(2)}) %collective-permute-start.1) | collective-permute-done | bytes 1179680 | tf_op jit(solution)/shard_map/ppermute | solution.py:20
  35.5 1.5 %collective-permute-start.2 = (bf16[192,2048]{1,0:T(8,128)(2,1)}, bf16[192,2048]{1,0:T(8,128)(2,1)S(1)}, u32[]{:S(2)}, u32[]{:S(2)}) collective-permute-start(bf16[192,2048]{1,0:T(8,128)(2,1)} %constant_dynamic-slice_fusion), channel_id=1, source_target_pairs={{0,3},{1,2},{2,1},{3,0},{4,7},{5,6},{6,5},{7,4},{8,11},{9,10},{10,... | collective-permute-start | bytes 2359304 | tf_op jit(solution)/shard_map/ppermute | solution.py:20
  37.0 1.8 %shard_map.131 = (bf16[96,1024]{1,0:T(8,128)(2,1)}, bf16[96,1024]{1,0:T(8,128)(2,1)}) custom-call(bf16[192,3072]{1,0:T(8,128)(2,1)} %collective-permute-done.x_ref.refs_1_.refs_4_.refs_5_, bf16[192,3072]{1,0:T(8,128)(2,1)} %collective-permute-done.1.y_ref.refs_2_.refs_5_.refs_6_), custom_call_target="tpu_custom_call" | custom-call | flops 1 | bytes 1 | tf_op jit(solution)/shard_map/pallas_call | solution.py:318
  38.8 0.3 collective-permute-start.4
  39.1 1.7 %collective-permute-start.3 = (bf16[96,1024]{1,0:T(8,128)(2,1)}, bf16[96,1024]{1,0:T(8,128)(2,1)S(1)}, u32[]{:S(2)}, u32[]{:S(2)}) collective-permute-start(bf16[96,1024]{1,0:T(8,128)(2,1)} %get-tuple-element.57), channel_id=1, source_target_pairs={{0,1},{1,0},{2,3},{3,2},{4,5},{5,4},{6,7},{7,6},{8,9},{9,8},{10,11... | collective-permute-start | bytes 589832 | tf_op jit(solution)/shard_map/ppermute | solution.py:20
  40.8 10.0 %shard_map.132 = (f32[2048,256]{1,0:T(8,128)}, bf16[192,3072]{1,0:T(8,128)(2,1)}, bf16[192,3072]{1,0:T(8,128)(2,1)}) custom-call(s32[4]{0:T(128)S(1)} %pad_add_fusion.where_ref, bf16[192,8192]{1,0:T(8,128)(2,1)} %bitcast.28, bf16[192,3072]{1,0:T(8,128)(2,1)} %collective-permute-done.x_ref.refs_1_.refs_4_.refs_5_, ...), custom_call_target="tpu_custom_call" | custom-call | flops 1 | bytes 1 | tf_op jit(solution)/shard_map/pallas_call | solution.py:167
  50.9 1.6 %collective-permute-start.11 = (bf16[192,3072]{1,0:T(8,128)(2,1)}, bf16[192,3072]{1,0:T(8,128)(2,1)S(1)}, u32[]{:S(2)}, u32[]{:S(2)}) collective-permute-start(bf16[192,3072]{1,0:T(8,128)(2,1)} %get-tuple-element.60), channel_id=1, source_target_pairs={{0,2},{1,3},{2,0},{3,1},{4,6},{5,7},{6,4},{7,5},{8,10},{9,11},{10,... | collective-permute-start | bytes 3538952 | tf_op jit(solution)/shard_map/ppermute | solution.py:20
  52.5 0.5 collective-permute-start.10
  53.2 0.1 pad_maximum_fusion.2.scal_ref
  53.2 5.8 %collective-permute-done.4.refs_1_.refs_11_ = bf16[96,1024]{1,0:T(8,128)(2,1)S(1)} collective-permute-done((bf16[96,1024]{1,0:T(8,128)(2,1)}, bf16[96,1024]{1,0:T(8,128)(2,1)S(1)}, u32[]{:S(2)}, u32[]{:S(2)}) %collective-permute-start.4) | collective-permute-done | bytes 196640 | tf_op jit(solution)/shard_map/ppermute | solution.py:20
  59.0 2.4 %collective-permute-done.3.refs_0_.refs_10_ = bf16[96,1024]{1,0:T(8,128)(2,1)S(1)} collective-permute-done((bf16[96,1024]{1,0:T(8,128)(2,1)}, bf16[96,1024]{1,0:T(8,128)(2,1)S(1)}, u32[]{:S(2)}, u32[]{:S(2)}) %collective-permute-start.3) | collective-permute-done | bytes 196640 | tf_op jit(solution)/shard_map/ppermute | solution.py:20
  61.4 1.6 %copy-done.3 = f32[2048,256]{1,0:T(8,128)S(1)} copy-done((f32[2048,256]{1,0:T(8,128)S(1)}, f32[2048,256]{1,0:T(8,128)}, u32[]{:S(2)}) %copy-start.3) | copy-done | bytes 2097176
  63.0 5.5 %shard_map.133 = (bf16[4,256,256]{2,1,0:T(8,128)(2,1)S(1)}, bf16[4,256,256]{2,1,0:T(8,128)(2,1)S(1)}) custom-call(s32[4]{0:T(128)S(1)} %pad_add_fusion.where_ref, f32[4]{0:T(128)S(1)} %pad_maximum_fusion.2.scal_ref, bf16[192,2048]{1,0:T(8,128)(2,1)S(1)} %collective-permute-done.2.hid_ref.refs_3_, ...), custom_call_target="tpu_custom_call" | custom-call | flops 1 | bytes 1 | tf_op jit(solution)/shard_map/pallas_call | solution.py:274
  68.6 0.1 collective-permute-start.5
  68.6 1.9 %collective-permute-done.5.got_ref = bf16[4,256,256]{2,1,0:T(8,128)(2,1)S(1)} collective-permute-done((bf16[4,256,256]{2,1,0:T(8,128)(2,1)S(1)}, bf16[4,256,256]{2,1,0:T(8,128)(2,1)S(1)}, u32[]{:S(2)}, u32[]{:S(2)}) %collective-permute-start.5) | collective-permute-done | bytes 524320 | tf_op jit(solution)/shard_map/ppermute | solution.py:20
  70.5 0.7 shard_map.134
  71.2 1.6 %collective-permute-start.7 = (bf16[2,256,256]{2,1,0:T(8,128)(2,1)S(1)}, bf16[2,256,256]{2,1,0:T(8,128)(2,1)S(1)}, u32[]{:S(2)}, u32[]{:S(2)}) collective-permute-start(bf16[2,256,256]{2,1,0:T(8,128)(2,1)S(1)} %get-tuple-element.67), channel_id=1, source_target_pairs={{0,8},{4,12},{8,0},{12,4},{16,24},{20,28},{24,16},{28,20},{1,9},{5... | collective-permute-start | bytes 786440 | tf_op jit(solution)/shard_map/ppermute | solution.py:20
  72.9 3.3 %shard_map.135 = bf16[192,3072]{1,0:T(8,128)(2,1)S(1)} custom-call(bf16[192,2048]{1,0:T(8,128)(2,1)S(1)} %collective-permute-done.2.hid_ref.refs_3_, bf16[2048,1024]{1,0:T(8,128)(2,1)S(1)} %copy-done.1, bf16[96,1024]{1,0:T(8,128)(2,1)S(1)} %collective-permute-done.3.refs_0_.refs_10_, bf16[96,1024]{1,0:T(8,128)(2,1)S(1)} %collective-permute-done.4.refs_1_.refs_11_), custom_call_target="tpu_custom_call" | custom-call | flops 1 | bytes 1 | tf_op jit(solution)/shard_map/pallas_call | solution.py:200
  76.2 3.5 %collective-permute-done.7.got_ref = bf16[2,256,256]{2,1,0:T(8,128)(2,1)S(1)} collective-permute-done((bf16[2,256,256]{2,1,0:T(8,128)(2,1)S(1)}, bf16[2,256,256]{2,1,0:T(8,128)(2,1)S(1)}, u32[]{:S(2)}, u32[]{:S(2)}) %collective-permute-start.7) | collective-permute-done | bytes 262176 | tf_op jit(solution)/shard_map/ppermute | solution.py:20
  79.7 0.6 shard_map.136
  80.3 2.7 %collective-permute-start.8 = (bf16[1,256,256]{2,1,0:T(8,128)(2,1)S(1)}, bf16[1,256,256]{2,1,0:T(8,128)(2,1)S(1)}, u32[]{:S(2)}, u32[]{:S(2)}) collective-permute-start(bf16[1,256,256]{2,1,0:T(8,128)(2,1)S(1)} %get-tuple-element.72), channel_id=1, source_target_pairs={{0,16},{4,20},{8,24},{12,28},{16,0},{20,4},{24,8},{28,12},{1,17},{... | collective-permute-start | bytes 393224 | tf_op jit(solution)/shard_map/ppermute | solution.py:20
  82.9 0.5 collective-permute-start.6
  83.4 9.3 %shard_map.137.refs_12_ = f32[2048,1024]{1,0:T(8,128)} custom-call(s32[4]{0:T(128)S(1)} %pad_add_fusion.where_ref, f32[4]{0:T(128)S(1)} %pad_maximum_fusion.2.scal_ref, bf16[192,8192]{1,0:T(8,128)(2,1)} %bitcast.29, bf16[192,3072]{1,0:T(8,128)(2,1)} %collective-permute-done.x_ref.refs_1_.refs_4_.refs_5_, ...), custom_call_target="tpu_custom_call" | custom-call | flops 1 | bytes 1 | tf_op jit(solution)/shard_map/pallas_call | solution.py:472
  92.7 0.1 shard_map.138
  92.8 0.2 collective-permute-start.9
  93.1 1.4 %shard_map.139 = (f32[256,1024]{1,0:T(8,128)}, f32[256,1024]{1,0:T(8,128)}) custom-call(s32[4]{0:T(128)S(1)} %pad_add_fusion.where_ref, f32[1,256,256]{2,1,0:T(8,128)S(1)} %get-tuple-element.77.refs_0_.stay_ref, bf16[1,256,256]{2,1,0:T(8,128)(2,1)S(1)} %collective-permute-done.8.refs_1_.got_ref, ...), custom_call_target="tpu_custom_call", output_to_operand_aliasing={{0}: (5, {}), {1}: (6, {})} | custom-call | flops 1 | bytes 1 | tf_op jit(solution)/shard_map/pallas_call | solution.py:391
  94.6 2.4 %shard_map.140 = (bf16[192,8192]{1,0:T(8,128)(2,1)}, f32[192,1024]{1,0:T(8,128)S(1)}) custom-call(s32[4]{0:T(128)S(1)} %pad_add_fusion.where_ref, bf16[192,3072]{1,0:T(8,128)(2,1)} %collective-permute-done.10.refs_0_, bf16[192,3072]{1,0:T(8,128)(2,1)S(1)} %collective-permute-done.11.refs_1_, ...), custom_call_target="tpu_custom_call", output_to_operand_aliasing={{0}: (4, {})} | custom-call | flops 1 | bytes 1 | tf_op jit(solution)/shard_map/pallas_call | solution.py:431
  97.0 3.9 %collective-permute-done.9 = bf16[1,256,256]{2,1,0:T(8,128)(2,1)S(1)} collective-permute-done((bf16[1,256,256]{2,1,0:T(8,128)(2,1)S(1)}, bf16[1,256,256]{2,1,0:T(8,128)(2,1)S(1)}, u32[]{:S(2)}, u32[]{:S(2)}) %collective-permute-start.9) | collective-permute-done | bytes 131104 | tf_op jit(solution)/shard_map/ppermute | solution.py:20
  100.9 0.1 collective-permute-start.12
  101.0 9.3 %shard_map.141.base_ref = f32[2048,1024]{1,0:T(8,128)} custom-call(s32[4]{0:T(128)S(1)} %pad_add_fusion.where_ref, f32[4]{0:T(128)S(1)} %pad_maximum_fusion.2.scal_ref, bf16[192,8192]{1,0:T(8,128)(2,1)} %bitcast.30, bf16[192,3072]{1,0:T(8,128)(2,1)} %collective-permute-done.x_ref.refs_1_.refs_4_.refs_5_, ...), custom_call_target="tpu_custom_call", output_to_operand_aliasing={{}: (14, {})} | custom-call | flops 1 | bytes 1 | tf_op jit(solution)/shard_map/pallas_call | solution.py:472
  110.3 0.1 pad_maximum_fusion.same_ref
  110.3 0.1 collective-permute-start.13
  110.4 1.9 %collective-permute-done.13.other_ref = bf16[4,256,256]{2,1,0:T(8,128)(2,1)S(1)} collective-permute-done((bf16[4,256,256]{2,1,0:T(8,128)(2,1)S(1)}, bf16[4,256,256]{2,1,0:T(8,128)(2,1)S(1)}, u32[]{:S(2)}, u32[]{:S(2)}) %collective-permute-start.13) | collective-permute-done | bytes 524320 | tf_op jit(solution)/shard_map/ppermute | solution.py:20
  112.3 2.0 %shard_map.142 = f32[2048,1024]{1,0:T(8,128)} custom-call(s32[4]{0:T(128)S(1)} %pad_add_fusion.where_ref, bf16[4,256,256]{2,1,0:T(8,128)(2,1)S(1)} %pad_maximum_fusion.same_ref, bf16[4,256,256]{2,1,0:T(8,128)(2,1)S(1)} %collective-permute-done.13.other_ref, f32[2048,1024]{1,0:T(8,128)} %shard_map.141.base_ref), custom_call_target="tpu_custom_call", output_to_operand_aliasing={{}: (3, {})} | custom-call | flops 1 | bytes 1 | tf_op jit(solution)/shard_map/pallas_call | solution.py:522
  114.3 2.2 %shard_map.143 = (bf16[192,8192]{1,0:T(8,128)(2,1)}, bf16[192,1024]{1,0:T(8,128)(2,1)}) custom-call(s32[4]{0:T(128)S(1)} %pad_add_fusion.where_ref, bf16[192,3072]{1,0:T(8,128)(2,1)S(1)} %collective-permute-done.6.refs_0_, f32[192,1024]{1,0:T(8,128)S(1)} %get-tuple-element.84.refs_1_, ...), custom_call_target="tpu_custom_call", output_to_operand_aliasing={{0}: (3, {})} | custom-call | flops 1 | bytes 1 | tf_op jit(solution)/shard_map/pallas_call | solution.py:431
  (26 shorter events, 0.1 us)
Async XLA Ops:
  0.6 11.4 %copy-start = (bf16[1,192,8192]{2,1,0:T(8,128)(2,1)S(1)}, bf16[1,192,8192]{2,1,0:T(8,128)(2,1)}, u32[]{:S(2)}) copy-start(bf16[1,192,8192]{2,1,0:T(8,128)(2,1)} %param.9) | copy-start | bytes 9437188
  0.6 11.4 %copy-start.2 = (bf16[1,192,1024]{2,1,0:T(8,128)(2,1)S(1)}, bf16[1,192,1024]{2,1,0:T(8,128)(2,1)}, u32[]{:S(2)}) copy-start(bf16[1,192,1024]{2,1,0:T(8,128)(2,1)} %param.10) | copy-start | bytes 1179652
  4.9 29.2 %collective-permute-start = (bf16[192,3072]{1,0:T(8,128)(2,1)}, bf16[192,3072]{1,0:T(8,128)(2,1)}, u32[]{:S(2)}, u32[]{:S(2)}) collective-permute-start(bf16[192,3072]{1,0:T(8,128)(2,1)} %get-tuple-element.53), channel_id=1, source_target_pairs={{0,1},{1,0},{2,3},{3,2},{4,5},{5,4},{6,7},{7,6},{8,9},{9,8},{10,11... | collective-permute-start | bytes 3538952 | tf_op jit(solution)/shard_map/ppermute | solution.py:20
  7.8 27.7 %collective-permute-start.1 = (bf16[192,3072]{1,0:T(8,128)(2,1)}, bf16[192,3072]{1,0:T(8,128)(2,1)}, u32[]{:S(2)}, u32[]{:S(2)}) collective-permute-start(bf16[192,3072]{1,0:T(8,128)(2,1)} %get-tuple-element.54), channel_id=1, source_target_pairs={{0,2},{1,3},{2,0},{3,1},{4,6},{5,7},{6,4},{7,5},{8,10},{9,11},{10,... | collective-permute-start | bytes 3538952 | tf_op jit(solution)/shard_map/ppermute | solution.py:20
  12.0 9.2 %copy-start.4 = (f32[1,256,1024]{2,1,0:T(8,128)S(1)}, f32[1,256,1024]{2,1,0:T(8,128)}, u32[]{:S(2)}) copy-start(f32[1,256,1024]{2,1,0:T(8,128)} %param.14) | copy-start | bytes 3145732
  12.0 9.2 %copy-start.5 = (f32[1,256,1024]{2,1,0:T(8,128)S(1)}, f32[1,256,1024]{2,1,0:T(8,128)}, u32[]{:S(2)}) copy-start(f32[1,256,1024]{2,1,0:T(8,128)} %param.15) | copy-start | bytes 3145732
  20.2 0.9 copy-start.10
  23.2 0.7 copy-start.6
  23.9 0.7 copy-start.8
  35.5 25.9 %collective-permute-start.2 = (bf16[192,2048]{1,0:T(8,128)(2,1)}, bf16[192,2048]{1,0:T(8,128)(2,1)S(1)}, u32[]{:S(2)}, u32[]{:S(2)}) collective-permute-start(bf16[192,2048]{1,0:T(8,128)(2,1)} %constant_dynamic-slice_fusion), channel_id=1, source_target_pairs={{0,3},{1,2},{2,1},{3,0},{4,7},{5,6},{6,5},{7,4},{8,11},{9,10},{10,... | collective-permute-start | bytes 2359304 | tf_op jit(solution)/shard_map/ppermute | solution.py:20
  38.8 20.2 %collective-permute-start.4 = (bf16[96,1024]{1,0:T(8,128)(2,1)}, bf16[96,1024]{1,0:T(8,128)(2,1)S(1)}, u32[]{:S(2)}, u32[]{:S(2)}) collective-permute-start(bf16[96,1024]{1,0:T(8,128)(2,1)} %get-tuple-element.62), channel_id=1, source_target_pairs={{0,2},{1,3},{2,0},{3,1},{4,6},{5,7},{6,4},{7,5},{8,10},{9,11},{10,... | collective-permute-start | bytes 589832 | tf_op jit(solution)/shard_map/ppermute | solution.py:20
  39.1 22.3 %collective-permute-start.3 = (bf16[96,1024]{1,0:T(8,128)(2,1)}, bf16[96,1024]{1,0:T(8,128)(2,1)S(1)}, u32[]{:S(2)}, u32[]{:S(2)}) collective-permute-start(bf16[96,1024]{1,0:T(8,128)(2,1)} %get-tuple-element.57), channel_id=1, source_target_pairs={{0,1},{1,0},{2,3},{3,2},{4,5},{5,4},{6,7},{7,6},{8,9},{9,8},{10,11... | collective-permute-start | bytes 589832 | tf_op jit(solution)/shard_map/ppermute | solution.py:20
  50.9 43.7 %collective-permute-start.11 = (bf16[192,3072]{1,0:T(8,128)(2,1)}, bf16[192,3072]{1,0:T(8,128)(2,1)S(1)}, u32[]{:S(2)}, u32[]{:S(2)}) collective-permute-start(bf16[192,3072]{1,0:T(8,128)(2,1)} %get-tuple-element.60), channel_id=1, source_target_pairs={{0,2},{1,3},{2,0},{3,1},{4,6},{5,7},{6,4},{7,5},{8,10},{9,11},{10,... | collective-permute-start | bytes 3538952 | tf_op jit(solution)/shard_map/ppermute | solution.py:20
  52.5 42.1 %collective-permute-start.10 = (bf16[192,3072]{1,0:T(8,128)(2,1)}, bf16[192,3072]{1,0:T(8,128)(2,1)}, u32[]{:S(2)}, u32[]{:S(2)}) collective-permute-start(bf16[192,3072]{1,0:T(8,128)(2,1)} %get-tuple-element.59), channel_id=1, source_target_pairs={{0,1},{1,0},{2,3},{3,2},{4,5},{5,4},{6,7},{7,6},{8,9},{9,8},{10,11... | collective-permute-start | bytes 3538952 | tf_op jit(solution)/shard_map/ppermute | solution.py:20
  61.4 1.6 %copy-start.3 = (f32[2048,256]{1,0:T(8,128)S(1)}, f32[2048,256]{1,0:T(8,128)}, u32[]{:S(2)}) copy-start(f32[2048,256]{1,0:T(8,128)} %get-tuple-element.64.refs_2_) | copy-start | bytes 6291460
  63.0 9.9 %copy-start.1 = (bf16[2048,1024]{1,0:T(8,128)(2,1)S(1)}, bf16[2048,1024]{1,0:T(8,128)(2,1)}, u32[]{:S(2)}) copy-start(bf16[2048,1024]{1,0:T(8,128)(2,1)} %get-tuple-element.49.refs_6_.weight_ref) | copy-start | bytes 12582916
  68.6 2.0 %collective-permute-start.5 = (bf16[4,256,256]{2,1,0:T(8,128)(2,1)S(1)}, bf16[4,256,256]{2,1,0:T(8,128)(2,1)S(1)}, u32[]{:S(2)}, u32[]{:S(2)}) collective-permute-start(bf16[4,256,256]{2,1,0:T(8,128)(2,1)S(1)} %get-tuple-element.66), channel_id=1, source_target_pairs={{0,4},{4,0},{8,12},{12,8},{16,20},{20,16},{24,28},{28,24},{1,5},{5... | collective-permute-start | bytes 1572872 | tf_op jit(solution)/shard_map/ppermute | solution.py:20
  71.2 8.4 %collective-permute-start.7 = (bf16[2,256,256]{2,1,0:T(8,128)(2,1)S(1)}, bf16[2,256,256]{2,1,0:T(8,128)(2,1)S(1)}, u32[]{:S(2)}, u32[]{:S(2)}) collective-permute-start(bf16[2,256,256]{2,1,0:T(8,128)(2,1)S(1)} %get-tuple-element.67), channel_id=1, source_target_pairs={{0,8},{4,12},{8,0},{12,4},{16,24},{20,28},{24,16},{28,20},{1,9},{5... | collective-permute-start | bytes 786440 | tf_op jit(solution)/shard_map/ppermute | solution.py:20
  80.3 12.5 %copy-start.7 = (f32[256,256]{1,0:T(8,128)S(1)}, f32[256,256]{1,0:T(8,128)}, u32[]{:S(2)}) copy-start(f32[256,256]{1,0:T(8,128)} %copy-done.6) | copy-start | bytes 786436
  80.3 12.5 %copy-start.9 = (f32[256,256]{1,0:T(8,128)S(1)}, f32[256,256]{1,0:T(8,128)}, u32[]{:S(2)}) copy-start(f32[256,256]{1,0:T(8,128)} %copy-done.8) | copy-start | bytes 786436
  80.3 12.4 %collective-permute-start.8 = (bf16[1,256,256]{2,1,0:T(8,128)(2,1)S(1)}, bf16[1,256,256]{2,1,0:T(8,128)(2,1)S(1)}, u32[]{:S(2)}, u32[]{:S(2)}) collective-permute-start(bf16[1,256,256]{2,1,0:T(8,128)(2,1)S(1)} %get-tuple-element.72), channel_id=1, source_target_pairs={{0,16},{4,20},{8,24},{12,28},{16,0},{20,4},{24,8},{28,12},{1,17},{... | collective-permute-start | bytes 393224 | tf_op jit(solution)/shard_map/ppermute | solution.py:20
  82.9 31.3 %collective-permute-start.6 = (bf16[192,3072]{1,0:T(8,128)(2,1)S(1)}, bf16[192,3072]{1,0:T(8,128)(2,1)S(1)}, u32[]{:S(2)}, u32[]{:S(2)}) collective-permute-start(bf16[192,3072]{1,0:T(8,128)(2,1)S(1)} %shard_map.135), channel_id=1, source_target_pairs={{0,3},{1,2},{2,1},{3,0},{4,7},{5,6},{6,5},{7,4},{8,11},{9,10},{10,... | collective-permute-start | bytes 3538952 | tf_op jit(solution)/shard_map/ppermute | solution.py:20
  92.7 1.8 %copy-start.11 = (f32[192,1024]{1,0:T(8,128)S(1)}, f32[192,1024]{1,0:T(8,128)}, u32[]{:S(2)}) copy-start(f32[192,1024]{1,0:T(8,128)} %copy-done.10) | copy-start | bytes 2359300
  92.8 8.0 %collective-permute-start.9 = (bf16[1,256,256]{2,1,0:T(8,128)(2,1)S(1)}, bf16[1,256,256]{2,1,0:T(8,128)(2,1)S(1)}, u32[]{:S(2)}, u32[]{:S(2)}) collective-permute-start(bf16[1,256,256]{2,1,0:T(8,128)(2,1)S(1)} %shard_map.138), channel_id=1, source_target_pairs={{0,16},{4,20},{8,24},{12,28},{16,0},{20,4},{24,8},{28,12},{1,17},{... | collective-permute-start | bytes 393224 | tf_op jit(solution)/shard_map/ppermute | solution.py:20
  100.9 9.4 %collective-permute-start.12 = (bf16[2,256,256]{2,1,0:T(8,128)(2,1)S(1)}, bf16[2,256,256]{2,1,0:T(8,128)(2,1)S(1)}, u32[]{:S(2)}, u32[]{:S(2)}) collective-permute-start(bf16[2,256,256]{2,1,0:T(8,128)(2,1)S(1)} %pad_maximum_fusion.1), channel_id=1, source_target_pairs={{0,8},{4,12},{8,0},{12,4},{16,24},{20,28},{24,16},{28,20},{1,9},{5... | collective-permute-start | bytes 786440 | tf_op jit(solution)/shard_map/ppermute | solution.py:20
  110.3 2.0 %collective-permute-start.13 = (bf16[4,256,256]{2,1,0:T(8,128)(2,1)S(1)}, bf16[4,256,256]{2,1,0:T(8,128)(2,1)S(1)}, u32[]{:S(2)}, u32[]{:S(2)}) collective-permute-start(bf16[4,256,256]{2,1,0:T(8,128)(2,1)S(1)} %pad_maximum_fusion.same_ref), channel_id=1, source_target_pairs={{0,4},{4,0},{8,12},{12,8},{16,20},{20,16},{24,28},{28,24},{1,5},{5... | collective-permute-start | bytes 1572872 | tf_op jit(solution)/shard_map/ppermute | solution.py:20

commit v4 on v3

--- a/solution.py
+++ b/solution.py
@@ -62,35 +62,6 @@
     @pl.when(pl.program_id(0) > 0)
     def _():
         ref[...] += value
-
-
-def send_kernel(peers, where_ref, *refs):
-    hids, cot_ref, outs = refs[:peers], refs[peers], refs[peers + 1 :]
-    head = pl.program_id(0) == 0
-    for hid_ref, out_ref in zip(hids, outs):
-        out_ref[...] = jnp.where(head, cot_ref[...], hid_ref[...])
-
-
-def send_call(tokens, cot, rows, shard, offsets):
-    toks, keys = cot.shape
-    steps = rows // keys
-
-    def column(m):
-        return pl.BlockSpec(
-            (toks, keys), lambda i, w, m=m: (0, (w[0] ^ m) * steps + jnp.maximum(i - 1, 0))
-        )
-
-    return pl.pallas_call(
-        functools.partial(send_kernel, len(offsets)),
-        grid_spec=pltpu.PrefetchScalarGridSpec(
-            num_scalar_prefetch=1,
-            grid=(1 + steps,),
-            in_specs=[column(m) for m in offsets] + [pl.BlockSpec((toks, keys), lambda i, w: (0, 0))],
-            out_specs=[pl.BlockSpec((toks, keys), lambda i, w: (0, i))] * len(offsets),
-        ),
-        out_shape=[jax.ShapeDtypeStruct((toks, keys + rows), cot.dtype)] * len(offsets),
-        cost_estimate=SMALL,
-    )(shard.reshape(1).astype(jnp.int32), *[tokens] * len(offsets), cot)
 
 
 def own_kernel(factor, where_ref, tokens_ref, cot_ref, weight_ref, half_ref, back_ref, keys_ref):
@@ -173,11 +144,11 @@
             + [column] * peers
             + [whole] * groups
             + [block],
-            out_specs=[pl.BlockSpec((tile, frag_cols), lambda i, w: (i, 0))]
+            out_specs=[pl.BlockSpec((tile, frag_cols), lambda i, w: (i, w[1]))]
             + [pl.BlockSpec((toks, rows + keys), lambda i, w: (0, 0))] * peers,
             scratch_shapes=[pltpu.VMEM((toks, keys), jnp.float32)] * peers,
         ),
-        out_shape=[jax.ShapeDtypeStruct((rows, frag_cols), jnp.float32)]
+        out_shape=[jax.ShapeDtypeStruct((rows, keys), jnp.float32)]
         + [jax.ShapeDtypeStruct((toks, rows + keys), jnp.bfloat16)] * peers,
         compiler_params=pltpu.CompilerParams(vmem_limit_bytes=VMEM),
         cost_estimate=SMALL,
@@ -228,9 +199,7 @@
     copies = []
     for j in range(chips):
         at = pl.ds(2 * j * size, 2 * size)
-        sources = [grad_ref.at[at, :]] + [
-            x.at[at, column] for x in (weight_ref, first_ref, second_ref)
-        ]
+        sources = [x.at[at, column] for x in (grad_ref, weight_ref, first_ref, second_ref)]
         copies.append(
             [
                 pltpu.make_async_copy(source, here_ref.at[i, at, :], sems.at[i, j])
@@ -266,8 +235,8 @@
     )(*args)
 
 
-def frag_call(hid, cots, grad, weight, first, second, where, scal, factor, own_rows):
-    rows, cols = grad.shape
+def frag_call(hid, cots, grad, weight, first, second, where, scal, factor, own_rows, cols):
+    rows = grad.shape[0]
     chips = rows // (2 * own_rows)
     vmem = pl.BlockSpec(memory_space=pltpu.VMEM)
     out = jax.ShapeDtypeStruct((chips, own_rows, cols), jnp.bfloat16)
@@ -575,8 +544,10 @@
     def hid_for(source, m):
         return lax.dynamic_slice_in_dim(source, (shard ^ m) * rows, rows, 1)
 
-    sends = send_call(tokens, cotangent, rows, shard, offsets[:-1])
-    packs = [pair(x, "fsdp", m) for x, m in zip(sends, offsets)]
+    packs = [
+        pair(jnp.concatenate([cotangent, hid_for(tokens, m)], axis=1), "fsdp", m)
+        for m in offsets[:-1]
+    ]
 
     first, second = adam_first[0], adam_second[0]
     weight_half, back_out, key_acc = own_call(tokens, cotangent, weight, where, factor, tile)
@@ -587,6 +558,7 @@
     hid_last = pair(after(hid_last, outer_copy, *packs), "fsdp", offsets[-1])
     if square:
         low, high = halves_call(after(packs[0], outer_copy), packs[1], keys)
+        packs = [after(x, low, high) for x in packs]
         cot_last = [pair(low, "fsdp", 1), pair(high, "fsdp", 2)]
     else:
         cot_last = [pair(cotangent, "fsdp", offsets[-1])]
@@ -603,18 +575,18 @@
         )
 
     keep, give = frag_call(
-        hid_last, cot_last, grad_frag, weight, first, second, where, scal, factor, own_rows
+        hid_last, cot_last, grad_frag, weight, first, second, where, scal, factor, own_rows,
+        frag_cols,
     )
     got = pair(give, "rep", 1)
+    give_last = last_call(after(hid_last, keep), cot_last, weight_half, factor, tile)
+    got = after(got, give_last)
     bits = [k for k in range(chips.bit_length()) if (1 << k) < chips]
     for k in bits:
         keep, leave = split_call(k, where, keep, got)
         got = pair(leave, "rep", 2 << k)
         if k == 0:
-            give_last = last_call(after(hid_last, leave), cot_last, weight_half, factor, tile)
-            got = after(got, give_last)
-        if k == bits[-1]:
-            inner = inner_half(0, after(hid_last, leave, give_last))
+            inner = inner_half(0, after(hid_last, leave))
             got = after(got, inner)
     backs.append(pair(give_last, "fsdp", offsets[-1]))
     outer_args = (keep, got, *outer_frag)

time: 117 us -> 115 us (0.983)
  Pallas kernels: 63 us -> 59.1 us
  starting transfers between devices: 15.3 us -> 17.3 us
  other arithmetic: 0.88 us -> 2.61 us
  waiting for transfers between devices: 29.4 us -> 27.7 us
    pallas_call x1 -> x0, Pallas kernels: 4.19 us -> none  [send_call(): pl.pallas_call(functools.partial(send_kernel, len(offsets)), grid_spec=pl...]
    ppermute x14, starting transfers between devices: 15.3 us -> 17.3 us  [pair(): return lax.ppermute(x, axis, [(i, i ^ offset) for i in range(size)])]
    concatenate x0 -> x1, other arithmetic: none -> 1.73 us  [per_device(): jnp.concatenate([cotangent, hid_for(tokens, m)], axis=1)]
    ppermute x14, waiting for transfers between devices: 29.4 us -> 27.7 us  [pair(): return lax.ppermute(x, axis, [(i, i ^ offset) for i in range(size)])]
    unnamed x24 -> x22, local copies, waits for them, and re-layouts: 3.98 us -> 2.33 us
    dynamic_slice x1 -> x2, local copies, waits for them, and re-layouts: 0.96 us -> 2.45 us  [hid_for(): return lax.dynamic_slice_in_dim(source, (shard ^ m) * rows, rows, 1)]
  transfers between devices with their start and end apart: 14 -> 14, of which waited for: 8 -> 7; matrix products, arithmetic and copies ran while one was open for 3% -> 3% of each run, Pallas kernels for 49% -> 50%
where the time goes in v4:
time: 115 us; the launch traced here: 114 us
  Pallas kernels  59.1 us (51%)
  waiting for transfers between devices  27.7 us (24%)
  starting transfers between devices  17.3 us (15%)
  local copies, waits for them, and re-layouts  6.06 us (5%)
  other arithmetic  2.61 us (2%)
  between operations  1.74 us (2%)
    ppermute x14, waiting for transfers between devices, pair(): return lax.ppermute(x, axis, [(i, i ^ offset) for i in range(size)])  27.7 us
    pallas_call x2, Pallas kernels, adam_call(): pl.pallas_call(functools.partial(adam_kernel, groups, len(cot_last), fact...  18.6 us
    ppermute x14, starting transfers between devices, pair(): return lax.ppermute(x, axis, [(i, i ^ offset) for i in range(size)])  17.3 us
    pallas_call x1, Pallas kernels, near_call(): pl.pallas_call(functools.partial(near_kernel, groups, factor, steps), gri...  10.1 us
    pallas_call x1, Pallas kernels, own_call(): pl.pallas_call(functools.partial(own_kernel, factor), grid_spec=pltpu.Pre...  8.23 us
    pallas_call x1, Pallas kernels, frag_call(): pl.pallas_call(functools.partial(frag_kernel, factor), in_specs=[pl.Block...  5.67 us
    pallas_call x2, Pallas kernels, place_call(): pl.pallas_call(functools.partial(place_kernel, tuple(offsets), final, fac...  4.63 us
    pallas_call x1, Pallas kernels, last_call(): pl.pallas_call(functools.partial(last_kernel, factor, steps), grid=(steps...  3.29 us
  transfers between devices with their start and end apart: 14, of which 7 were waited for; matrix products, arithmetic and copies ran while one was open for 3% of the time, Pallas kernels for 50%

profile of v4, /device:TPU:0, one launch (start us, length us, event | category | flops | bytes accessed | tf_op | source)
XLA Modules:
  0.0 114.4 jit_solution(16650079803775747780)
XLA Ops:
  0.7 1.5 %dynamic-slice_bitcast_fusion = (bf16[192,2048]{1,0:T(8,128)(2,1)S(1)}, bf16[192,2048]{1,0:T(8,128)(2,1)S(1)}) fusion(bf16[1,192,8192]{2,1,0:T(8,128)(2,1)} %param.9, s32[]{:T(128)S(6)} %select_n.46, s32[]{:T(128)S(6)} %select_n.45), kind=kLoop, calls=%fused_computation.2 | loop fusion | bytes 3145736 | tf_op jit(solution)/shard_map/dynamic_slice | solution.py:545
  2.2 0.0 copy-start
  2.2 1.7 %pad_maximum_fusion = (bf16[192,3072]{1,0:T(8,128)(2,1)}, bf16[192,3072]{1,0:T(8,128)(2,1)}) fusion(bf16[192,1024]{1,0:T(8,128)(2,1)S(1)} %bitcast.35, bf16[192,2048]{1,0:T(8,128)(2,1)S(1)} %get-tuple-element.93, bf16[192,2048]{1,0:T(8,128)(2,1)S(1)} %get-tuple-element.94), kind=kLoop, calls=%fused_computation | loop fusion | flops 4128768 | bytes 4325376 | tf_op jit(solution)/shard_map/concatenate | solution.py:548
  3.9 3.0 %collective-permute-start.1 = (bf16[192,3072]{1,0:T(8,128)(2,1)}, bf16[192,3072]{1,0:T(8,128)(2,1)}, u32[]{:S(2)}, u32[]{:S(2)}) collective-permute-start(bf16[192,3072]{1,0:T(8,128)(2,1)} %get-tuple-element.95), channel_id=1, source_target_pairs={{0,2},{1,3},{2,0},{3,1},{4,6},{5,7},{6,4},{7,5},{8,10},{9,11},{10,... | collective-permute-start | bytes 3538952 | tf_op jit(solution)/shard_map/ppermute | solution.py:20
  6.9 1.5 %collective-permute-start = (bf16[192,3072]{1,0:T(8,128)(2,1)}, bf16[192,3072]{1,0:T(8,128)(2,1)}, u32[]{:S(2)}, u32[]{:S(2)}) collective-permute-start(bf16[192,3072]{1,0:T(8,128)(2,1)} %get-tuple-element.96), channel_id=1, source_target_pairs={{0,1},{1,0},{2,3},{3,2},{4,5},{5,4},{6,7},{7,6},{8,9},{9,8},{10,11... | collective-permute-start | bytes 3538952 | tf_op jit(solution)/shard_map/ppermute | solution.py:20
  9.1 1.3 %dynamic_slice.16 = s32[1,1]{0,1:T(1,128)} dynamic-slice(s32[8,4]{0,1:T(4,128)} %param.16, s32[]{:T(128)S(6)} %select_n.39, s32[]{:T(128)S(6)} %select_n.41), dynamic_slice_sizes={1,1} | dynamic-slice | bytes 12 | tf_op jit(solution)/shard_map/dynamic_slice | solution.py:532
  10.4 0.7 pad_add_fusion.where_ref
  11.1 8.2 %shard_map.128 = (bf16[2048,1024]{1,0:T(8,128)(2,1)}, bf16[192,8192]{1,0:T(8,128)(2,1)}, f32[192,1024]{1,0:T(8,128)S(1)}) custom-call(s32[4]{0:T(128)S(1)} %pad_add_fusion.where_ref, bf16[192,8192]{1,0:T(8,128)(2,1)S(1)} %bitcast.33, bf16[192,1024]{1,0:T(8,128)(2,1)S(1)} %bitcast.36, f32[2048,1024]{1,0:T(8,128)} %bitcast.42), custom_call_target="tpu_custom_call" | custom-call | flops 1 | bytes 1 | tf_op jit(solution)/shard_map/pallas_call | solution.py:81
  19.3 0.9 copy-done.9
  20.2 2.0 %shard_map.129 = (f32[256,1024]{1,0:T(8,128)}, f32[256,1024]{1,0:T(8,128)}, f32[256,256]{1,0:T(8,128)S(1)}, f32[256,256]{1,0:T(8,128)S(1)}) custom-call(s32[4]{0:T(128)S(1)} %pad_add_fusion.where_ref, f32[256,1024]{1,0:T(8,128)S(1)} %bitcast.40, f32[256,1024]{1,0:T(8,128)S(1)} %bitcast.41), custom_call_target="tpu_custom_call" | custom-call | flops 1 | bytes 1 | tf_op jit(solution)/shard_map/pallas_call | solution.py:308
  22.2 0.7 copy-done.5
  22.9 0.7 copy-done.7
  23.6 0.9 constant_dynamic-slice_fusion
  24.6 8.6 %collective-permute-done.1.y_ref.refs_2_.refs_5_.refs_6_ = bf16[192,3072]{1,0:T(8,128)(2,1)} collective-permute-done((bf16[192,3072]{1,0:T(8,128)(2,1)}, bf16[192,3072]{1,0:T(8,128)(2,1)}, u32[]{:S(2)}, u32[]{:S(2)}) %collective-permute-start.1) | collective-permute-done | bytes 1179680 | tf_op jit(solution)/shard_map/ppermute | solution.py:20
  33.2 1.5 %collective-permute-done.x_ref.refs_1_.refs_4_.refs_5_ = bf16[192,3072]{1,0:T(8,128)(2,1)} collective-permute-done((bf16[192,3072]{1,0:T(8,128)(2,1)}, bf16[192,3072]{1,0:T(8,128)(2,1)}, u32[]{:S(2)}, u32[]{:S(2)}) %collective-permute-start) | collective-permute-done | bytes 1179680 | tf_op jit(solution)/shard_map/ppermute | solution.py:20
  34.7 1.4 %collective-permute-start.2 = (bf16[192,2048]{1,0:T(8,128)(2,1)}, bf16[192,2048]{1,0:T(8,128)(2,1)S(1)}, u32[]{:S(2)}, u32[]{:S(2)}) collective-permute-start(bf16[192,2048]{1,0:T(8,128)(2,1)} %constant_dynamic-slice_fusion), channel_id=1, source_target_pairs={{0,3},{1,2},{2,1},{3,0},{4,7},{5,6},{6,5},{7,4},{8,11},{9,10},{10,... | collective-permute-start | bytes 2359304 | tf_op jit(solution)/shard_map/ppermute | solution.py:20
  36.1 1.8 %shard_map.130 = (bf16[96,1024]{1,0:T(8,128)(2,1)}, bf16[96,1024]{1,0:T(8,128)(2,1)}) custom-call(bf16[192,3072]{1,0:T(8,128)(2,1)} %collective-permute-done.x_ref.refs_1_.refs_4_.refs_5_, bf16[192,3072]{1,0:T(8,128)(2,1)} %collective-permute-done.1.y_ref.refs_2_.refs_5_.refs_6_), custom_call_target="tpu_custom_call" | custom-call | flops 1 | bytes 1 | tf_op jit(solution)/shard_map/pallas_call | solution.py:287
  37.9 1.5 %collective-permute-start.4 = (bf16[96,1024]{1,0:T(8,128)(2,1)}, bf16[96,1024]{1,0:T(8,128)(2,1)S(1)}, u32[]{:S(2)}, u32[]{:S(2)}) collective-permute-start(bf16[96,1024]{1,0:T(8,128)(2,1)} %get-tuple-element.57), channel_id=1, source_target_pairs={{0,2},{1,3},{2,0},{3,1},{4,6},{5,7},{6,4},{7,5},{8,10},{9,11},{10,... | collective-permute-start | bytes 589832 | tf_op jit(solution)/shard_map/ppermute | solution.py:20
  39.4 0.5 collective-permute-start.3
  40.0 10.1 %shard_map.131 = (f32[2048,1024]{1,0:T(8,128)}, bf16[192,3072]{1,0:T(8,128)(2,1)}, bf16[192,3072]{1,0:T(8,128)(2,1)}) custom-call(s32[4]{0:T(128)S(1)} %pad_add_fusion.where_ref, bf16[192,8192]{1,0:T(8,128)(2,1)} %bitcast.30, bf16[192,3072]{1,0:T(8,128)(2,1)} %collective-permute-done.x_ref.refs_1_.refs_4_.refs_5_, ...), custom_call_target="tpu_custom_call" | custom-call | flops 1 | bytes 1 | tf_op jit(solution)/shard_map/pallas_call | solution.py:138
  50.0 0.3 collective-permute-start.11
  50.3 1.7 %collective-permute-start.10 = (bf16[192,3072]{1,0:T(8,128)(2,1)}, bf16[192,3072]{1,0:T(8,128)(2,1)}, u32[]{:S(2)}, u32[]{:S(2)}) collective-permute-start(bf16[192,3072]{1,0:T(8,128)(2,1)} %get-tuple-element.60), channel_id=1, source_target_pairs={{0,1},{1,0},{2,3},{3,2},{4,5},{5,4},{6,7},{7,6},{8,9},{9,8},{10,11... | collective-permute-start | bytes 3538952 | tf_op jit(solution)/shard_map/ppermute | solution.py:20
  52.2 0.1 pad_maximum_fusion.4.scal_ref
  52.3 5.8 %collective-permute-done.4.refs_1_.refs_11_ = bf16[96,1024]{1,0:T(8,128)(2,1)S(1)} collective-permute-done((bf16[96,1024]{1,0:T(8,128)(2,1)}, bf16[96,1024]{1,0:T(8,128)(2,1)S(1)}, u32[]{:S(2)}, u32[]{:S(2)}) %collective-permute-start.4) | collective-permute-done | bytes 196640 | tf_op jit(solution)/shard_map/ppermute | solution.py:20
  58.2 1.2 %collective-permute-done.3.refs_0_.refs_10_ = bf16[96,1024]{1,0:T(8,128)(2,1)S(1)} collective-permute-done((bf16[96,1024]{1,0:T(8,128)(2,1)}, bf16[96,1024]{1,0:T(8,128)(2,1)S(1)}, u32[]{:S(2)}, u32[]{:S(2)}) %collective-permute-start.3) | collective-permute-done | bytes 196640 | tf_op jit(solution)/shard_map/ppermute | solution.py:20
  59.3 5.7 %shard_map.132 = (bf16[4,256,256]{2,1,0:T(8,128)(2,1)S(1)}, bf16[4,256,256]{2,1,0:T(8,128)(2,1)S(1)}) custom-call(s32[4]{0:T(128)S(1)} %pad_add_fusion.where_ref, f32[4]{0:T(128)S(1)} %pad_maximum_fusion.4.scal_ref, bf16[192,2048]{1,0:T(8,128)(2,1)S(1)} %collective-permute-done.2.hid_ref.refs_3_, ...), custom_call_target="tpu_custom_call" | custom-call | flops 1 | bytes 1 | tf_op jit(solution)/shard_map/pallas_call | solution.py:243
  65.0 0.1 collective-permute-start.6
  65.1 3.3 %shard_map.133 = bf16[192,3072]{1,0:T(8,128)(2,1)S(1)} custom-call(bf16[192,2048]{1,0:T(8,128)(2,1)S(1)} %collective-permute-done.2.hid_ref.refs_3_, bf16[2048,1024]{1,0:T(8,128)(2,1)S(1)} %copy-done.1, bf16[96,1024]{1,0:T(8,128)(2,1)S(1)} %collective-permute-done.3.refs_0_.refs_10_, bf16[96,1024]{1,0:T(8,128)(2,1)S(1)} %collective-permute-done.4.refs_1_.refs_11_), custom_call_target="tpu_custom_call" | custom-call | flops 1 | bytes 1 | tf_op jit(solution)/shard_map/pallas_call | solution.py:171
  68.4 0.7 shard_map.134
  69.1 1.9 %collective-permute-start.7 = (bf16[2,256,256]{2,1,0:T(8,128)(2,1)S(1)}, bf16[2,256,256]{2,1,0:T(8,128)(2,1)S(1)}, u32[]{:S(2)}, u32[]{:S(2)}) collective-permute-start(bf16[2,256,256]{2,1,0:T(8,128)(2,1)S(1)} %get-tuple-element.70), channel_id=1, source_target_pairs={{0,8},{4,12},{8,0},{12,4},{16,24},{20,28},{24,16},{28,20},{1,9},{5... | collective-permute-start | bytes 786440 | tf_op jit(solution)/shard_map/ppermute | solution.py:20
  71.0 9.3 %shard_map.135.refs_12_ = f32[2048,1024]{1,0:T(8,128)} custom-call(s32[4]{0:T(128)S(1)} %pad_add_fusion.where_ref, f32[4]{0:T(128)S(1)} %pad_maximum_fusion.4.scal_ref, bf16[192,8192]{1,0:T(8,128)(2,1)} %bitcast.31, bf16[192,3072]{1,0:T(8,128)(2,1)} %collective-permute-done.x_ref.refs_1_.refs_4_.refs_5_, ...), custom_call_target="tpu_custom_call" | custom-call | flops 1 | bytes 1 | tf_op jit(solution)/shard_map/pallas_call | solution.py:441
  80.3 0.6 shard_map.136
  80.9 2.6 %collective-permute-start.8 = (bf16[1,256,256]{2,1,0:T(8,128)(2,1)S(1)}, bf16[1,256,256]{2,1,0:T(8,128)(2,1)S(1)}, u32[]{:S(2)}, u32[]{:S(2)}) collective-permute-start(bf16[1,256,256]{2,1,0:T(8,128)(2,1)S(1)} %get-tuple-element.74), channel_id=1, source_target_pairs={{0,16},{4,20},{8,24},{12,28},{16,0},{20,4},{24,8},{28,12},{1,17},{... | collective-permute-start | bytes 393224 | tf_op jit(solution)/shard_map/ppermute | solution.py:20
  83.6 2.4 %collective-permute-start.5 = (bf16[192,3072]{1,0:T(8,128)(2,1)S(1)}, bf16[192,3072]{1,0:T(8,128)(2,1)S(1)}, u32[]{:S(2)}, u32[]{:S(2)}) collective-permute-start(bf16[192,3072]{1,0:T(8,128)(2,1)S(1)} %shard_map.133), channel_id=1, source_target_pairs={{0,3},{1,2},{2,1},{3,0},{4,7},{5,6},{6,5},{7,4},{8,11},{9,10},{10,... | collective-permute-start | bytes 3538952 | tf_op jit(solution)/shard_map/ppermute | solution.py:20
  86.0 4.1 %collective-permute-done.8.refs_1_.got_ref = bf16[1,256,256]{2,1,0:T(8,128)(2,1)S(1)} collective-permute-done((bf16[1,256,256]{2,1,0:T(8,128)(2,1)S(1)}, bf16[1,256,256]{2,1,0:T(8,128)(2,1)S(1)}, u32[]{:S(2)}, u32[]{:S(2)}) %collective-permute-start.8) | collective-permute-done | bytes 131104 | tf_op jit(solution)/shard_map/ppermute | solution.py:20
  90.1 0.1 shard_map.137
  90.2 0.1 collective-permute-start.9
  90.3 1.4 %shard_map.138 = (f32[256,1024]{1,0:T(8,128)}, f32[256,1024]{1,0:T(8,128)}) custom-call(s32[4]{0:T(128)S(1)} %pad_add_fusion.where_ref, f32[1,256,256]{2,1,0:T(8,128)S(1)} %get-tuple-element.77.refs_0_.stay_ref, bf16[1,256,256]{2,1,0:T(8,128)(2,1)S(1)} %collective-permute-done.8.refs_1_.got_ref, ...), custom_call_target="tpu_custom_call", output_to_operand_aliasing={{0}: (5, {}), {1}: (6, {})} | custom-call | flops 1 | bytes 1 | tf_op jit(solution)/shard_map/pallas_call | solution.py:360
  91.8 2.4 %shard_map.139 = (bf16[192,8192]{1,0:T(8,128)(2,1)}, f32[192,1024]{1,0:T(8,128)S(1)}) custom-call(s32[4]{0:T(128)S(1)} %pad_add_fusion.where_ref, bf16[192,3072]{1,0:T(8,128)(2,1)} %collective-permute-done.10.refs_0_, bf16[192,3072]{1,0:T(8,128)(2,1)S(1)} %collective-permute-done.11.refs_1_, ...), custom_call_target="tpu_custom_call", output_to_operand_aliasing={{0}: (4, {})} | custom-call | flops 1 | bytes 1 | tf_op jit(solution)/shard_map/pallas_call | solution.py:400
  94.3 4.5 %collective-permute-done.9 = bf16[1,256,256]{2,1,0:T(8,128)(2,1)S(1)} collective-permute-done((bf16[1,256,256]{2,1,0:T(8,128)(2,1)S(1)}, bf16[1,256,256]{2,1,0:T(8,128)(2,1)S(1)}, u32[]{:S(2)}, u32[]{:S(2)}) %collective-permute-start.9) | collective-permute-done | bytes 131104 | tf_op jit(solution)/shard_map/ppermute | solution.py:20
  98.8 0.1 collective-permute-start.12
  98.9 9.3 %shard_map.140.base_ref = f32[2048,1024]{1,0:T(8,128)} custom-call(s32[4]{0:T(128)S(1)} %pad_add_fusion.where_ref, f32[4]{0:T(128)S(1)} %pad_maximum_fusion.4.scal_ref, bf16[192,8192]{1,0:T(8,128)(2,1)} %bitcast.32, bf16[192,3072]{1,0:T(8,128)(2,1)} %collective-permute-done.x_ref.refs_1_.refs_4_.refs_5_, ...), custom_call_target="tpu_custom_call", output_to_operand_aliasing={{}: (14, {})} | custom-call | flops 1 | bytes 1 | tf_op jit(solution)/shard_map/pallas_call | solution.py:441
  108.2 0.1 pad_maximum_fusion.2.same_ref
  108.3 0.1 collective-permute-start.13
  108.4 1.9 %collective-permute-done.13.other_ref = bf16[4,256,256]{2,1,0:T(8,128)(2,1)S(1)} collective-permute-done((bf16[4,256,256]{2,1,0:T(8,128)(2,1)S(1)}, bf16[4,256,256]{2,1,0:T(8,128)(2,1)S(1)}, u32[]{:S(2)}, u32[]{:S(2)}) %collective-permute-start.13) | collective-permute-done | bytes 524320 | tf_op jit(solution)/shard_map/ppermute | solution.py:20
  110.2 2.0 %shard_map.141 = f32[2048,1024]{1,0:T(8,128)} custom-call(s32[4]{0:T(128)S(1)} %pad_add_fusion.where_ref, bf16[4,256,256]{2,1,0:T(8,128)(2,1)S(1)} %pad_maximum_fusion.2.same_ref, bf16[4,256,256]{2,1,0:T(8,128)(2,1)S(1)} %collective-permute-done.13.other_ref, f32[2048,1024]{1,0:T(8,128)} %shard_map.140.base_ref), custom_call_target="tpu_custom_call", output_to_operand_aliasing={{}: (3, {})} | custom-call | flops 1 | bytes 1 | tf_op jit(solution)/shard_map/pallas_call | solution.py:491
  112.2 0.0 collective-permute-done.5.refs_0_
  112.2 2.2 %shard_map.142 = (bf16[192,8192]{1,0:T(8,128)(2,1)}, bf16[192,1024]{1,0:T(8,128)(2,1)}) custom-call(s32[4]{0:T(128)S(1)} %pad_add_fusion.where_ref, bf16[192,3072]{1,0:T(8,128)(2,1)S(1)} %collective-permute-done.5.refs_0_, f32[192,1024]{1,0:T(8,128)S(1)} %get-tuple-element.84.refs_1_, ...), custom_call_target="tpu_custom_call", output_to_operand_aliasing={{0}: (3, {})} | custom-call | flops 1 | bytes 1 | tf_op jit(solution)/shard_map/pallas_call | solution.py:400
  (25 shorter events, 0.1 us)
Async XLA Ops:
  0.6 1.6 %copy-start.2 = (bf16[1,192,1024]{2,1,0:T(8,128)(2,1)S(1)}, bf16[1,192,1024]{2,1,0:T(8,128)(2,1)}, u32[]{:S(2)}) copy-start(bf16[1,192,1024]{2,1,0:T(8,128)(2,1)} %param.10) | copy-start | bytes 1179652
  2.2 8.9 %copy-start = (bf16[1,192,8192]{2,1,0:T(8,128)(2,1)S(1)}, bf16[1,192,8192]{2,1,0:T(8,128)(2,1)}, u32[]{:S(2)}) copy-start(bf16[1,192,8192]{2,1,0:T(8,128)(2,1)} %param.9) | copy-start | bytes 9437188
  3.9 29.2 %collective-permute-start.1 = (bf16[192,3072]{1,0:T(8,128)(2,1)}, bf16[192,3072]{1,0:T(8,128)(2,1)}, u32[]{:S(2)}, u32[]{:S(2)}) collective-permute-start(bf16[192,3072]{1,0:T(8,128)(2,1)} %get-tuple-element.95), channel_id=1, source_target_pairs={{0,2},{1,3},{2,0},{3,1},{4,6},{5,7},{6,4},{7,5},{8,10},{9,11},{10,... | collective-permute-start | bytes 3538952 | tf_op jit(solution)/shard_map/ppermute | solution.py:20
  6.9 27.7 %collective-permute-start = (bf16[192,3072]{1,0:T(8,128)(2,1)}, bf16[192,3072]{1,0:T(8,128)(2,1)}, u32[]{:S(2)}, u32[]{:S(2)}) collective-permute-start(bf16[192,3072]{1,0:T(8,128)(2,1)} %get-tuple-element.96), channel_id=1, source_target_pairs={{0,1},{1,0},{2,3},{3,2},{4,5},{5,4},{6,7},{7,6},{8,9},{9,8},{10,11... | collective-permute-start | bytes 3538952 | tf_op jit(solution)/shard_map/ppermute | solution.py:20
  11.1 9.1 %copy-start.3 = (f32[1,256,1024]{2,1,0:T(8,128)S(1)}, f32[1,256,1024]{2,1,0:T(8,128)}, u32[]{:S(2)}) copy-start(f32[1,256,1024]{2,1,0:T(8,128)} %param.14) | copy-start | bytes 3145732
  11.1 9.1 %copy-start.4 = (f32[1,256,1024]{2,1,0:T(8,128)S(1)}, f32[1,256,1024]{2,1,0:T(8,128)}, u32[]{:S(2)}) copy-start(f32[1,256,1024]{2,1,0:T(8,128)} %param.15) | copy-start | bytes 3145732
  19.3 0.9 copy-start.9
  22.2 0.7 copy-start.5
  22.9 0.7 copy-start.7
  34.7 24.7 %collective-permute-start.2 = (bf16[192,2048]{1,0:T(8,128)(2,1)}, bf16[192,2048]{1,0:T(8,128)(2,1)S(1)}, u32[]{:S(2)}, u32[]{:S(2)}) collective-permute-start(bf16[192,2048]{1,0:T(8,128)(2,1)} %constant_dynamic-slice_fusion), channel_id=1, source_target_pairs={{0,3},{1,2},{2,1},{3,0},{4,7},{5,6},{6,5},{7,4},{8,11},{9,10},{10,... | collective-permute-start | bytes 2359304 | tf_op jit(solution)/shard_map/ppermute | solution.py:20
  37.9 20.3 %collective-permute-start.4 = (bf16[96,1024]{1,0:T(8,128)(2,1)}, bf16[96,1024]{1,0:T(8,128)(2,1)S(1)}, u32[]{:S(2)}, u32[]{:S(2)}) collective-permute-start(bf16[96,1024]{1,0:T(8,128)(2,1)} %get-tuple-element.57), channel_id=1, source_target_pairs={{0,2},{1,3},{2,0},{3,1},{4,6},{5,7},{6,4},{7,5},{8,10},{9,11},{10,... | collective-permute-start | bytes 589832 | tf_op jit(solution)/shard_map/ppermute | solution.py:20
  39.4 19.9 %collective-permute-start.3 = (bf16[96,1024]{1,0:T(8,128)(2,1)}, bf16[96,1024]{1,0:T(8,128)(2,1)S(1)}, u32[]{:S(2)}, u32[]{:S(2)}) collective-permute-start(bf16[96,1024]{1,0:T(8,128)(2,1)} %get-tuple-element.55), channel_id=1, source_target_pairs={{0,1},{1,0},{2,3},{3,2},{4,5},{5,4},{6,7},{7,6},{8,9},{9,8},{10,11... | collective-permute-start | bytes 589832 | tf_op jit(solution)/shard_map/ppermute | solution.py:20
  50.0 41.8 %collective-permute-start.11 = (bf16[192,3072]{1,0:T(8,128)(2,1)}, bf16[192,3072]{1,0:T(8,128)(2,1)S(1)}, u32[]{:S(2)}, u32[]{:S(2)}) collective-permute-start(bf16[192,3072]{1,0:T(8,128)(2,1)} %get-tuple-element.61), channel_id=1, source_target_pairs={{0,2},{1,3},{2,0},{3,1},{4,6},{5,7},{6,4},{7,5},{8,10},{9,11},{10,... | collective-permute-start | bytes 3538952 | tf_op jit(solution)/shard_map/ppermute | solution.py:20
  50.3 41.5 %collective-permute-start.10 = (bf16[192,3072]{1,0:T(8,128)(2,1)}, bf16[192,3072]{1,0:T(8,128)(2,1)}, u32[]{:S(2)}, u32[]{:S(2)}) collective-permute-start(bf16[192,3072]{1,0:T(8,128)(2,1)} %get-tuple-element.60), channel_id=1, source_target_pairs={{0,1},{1,0},{2,3},{3,2},{4,5},{5,4},{6,7},{7,6},{8,9},{9,8},{10,11... | collective-permute-start | bytes 3538952 | tf_op jit(solution)/shard_map/ppermute | solution.py:20
  59.3 5.8 %copy-start.1 = (bf16[2048,1024]{1,0:T(8,128)(2,1)S(1)}, bf16[2048,1024]{1,0:T(8,128)(2,1)}, u32[]{:S(2)}) copy-start(bf16[2048,1024]{1,0:T(8,128)(2,1)} %get-tuple-element.49.refs_6_.weight_ref) | copy-start | bytes 12582916
  65.0 3.4 %collective-permute-start.6 = (bf16[4,256,256]{2,1,0:T(8,128)(2,1)S(1)}, bf16[4,256,256]{2,1,0:T(8,128)(2,1)S(1)}, u32[]{:S(2)}, u32[]{:S(2)}) collective-permute-start(bf16[4,256,256]{2,1,0:T(8,128)(2,1)S(1)} %get-tuple-element.67), channel_id=1, source_target_pairs={{0,4},{4,0},{8,12},{12,8},{16,20},{20,16},{24,28},{28,24},{1,5},{5... | collective-permute-start | bytes 1572872 | tf_op jit(solution)/shard_map/ppermute | solution.py:20
  69.1 21.0 %copy-start.6 = (f32[256,256]{1,0:T(8,128)S(1)}, f32[256,256]{1,0:T(8,128)}, u32[]{:S(2)}) copy-start(f32[256,256]{1,0:T(8,128)} %copy-done.5) | copy-start | bytes 786436
  69.1 21.0 %copy-start.8 = (f32[256,256]{1,0:T(8,128)S(1)}, f32[256,256]{1,0:T(8,128)}, u32[]{:S(2)}) copy-start(f32[256,256]{1,0:T(8,128)} %copy-done.7) | copy-start | bytes 786436
  69.1 11.2 %collective-permute-start.7 = (bf16[2,256,256]{2,1,0:T(8,128)(2,1)S(1)}, bf16[2,256,256]{2,1,0:T(8,128)(2,1)S(1)}, u32[]{:S(2)}, u32[]{:S(2)}) collective-permute-start(bf16[2,256,256]{2,1,0:T(8,128)(2,1)S(1)} %get-tuple-element.70), channel_id=1, source_target_pairs={{0,8},{4,12},{8,0},{12,4},{16,24},{20,28},{24,16},{28,20},{1,9},{5... | collective-permute-start | bytes 786440 | tf_op jit(solution)/shard_map/ppermute | solution.py:20
  80.3 11.5 %copy-start.10 = (f32[192,1024]{1,0:T(8,128)S(1)}, f32[192,1024]{1,0:T(8,128)}, u32[]{:S(2)}) copy-start(f32[192,1024]{1,0:T(8,128)} %copy-done.9) | copy-start | bytes 2359300
  80.9 9.2 %collective-permute-start.8 = (bf16[1,256,256]{2,1,0:T(8,128)(2,1)S(1)}, bf16[1,256,256]{2,1,0:T(8,128)(2,1)S(1)}, u32[]{:S(2)}, u32[]{:S(2)}) collective-permute-start(bf16[1,256,256]{2,1,0:T(8,128)(2,1)S(1)} %get-tuple-element.74), channel_id=1, source_target_pairs={{0,16},{4,20},{8,24},{12,28},{16,0},{20,4},{24,8},{28,12},{1,17},{... | collective-permute-start | bytes 393224 | tf_op jit(solution)/shard_map/ppermute | solution.py:20
  83.6 28.7 %collective-permute-start.5 = (bf16[192,3072]{1,0:T(8,128)(2,1)S(1)}, bf16[192,3072]{1,0:T(8,128)(2,1)S(1)}, u32[]{:S(2)}, u32[]{:S(2)}) collective-permute-start(bf16[192,3072]{1,0:T(8,128)(2,1)S(1)} %shard_map.133), channel_id=1, source_target_pairs={{0,3},{1,2},{2,1},{3,0},{4,7},{5,6},{6,5},{7,4},{8,11},{9,10},{10,... | collective-permute-start | bytes 3538952 | tf_op jit(solution)/shard_map/ppermute | solution.py:20
  90.2 8.6 %collective-permute-start.9 = (bf16[1,256,256]{2,1,0:T(8,128)(2,1)S(1)}, bf16[1,256,256]{2,1,0:T(8,128)(2,1)S(1)}, u32[]{:S(2)}, u32[]{:S(2)}) collective-permute-start(bf16[1,256,256]{2,1,0:T(8,128)(2,1)S(1)} %shard_map.137), channel_id=1, source_target_pairs={{0,16},{4,20},{8,24},{12,28},{16,0},{20,4},{24,8},{28,12},{1,17},{... | collective-permute-start | bytes 393224 | tf_op jit(solution)/shard_map/ppermute | solution.py:20
  98.8 9.4 %collective-permute-start.12 = (bf16[2,256,256]{2,1,0:T(8,128)(2,1)S(1)}, bf16[2,256,256]{2,1,0:T(8,128)(2,1)S(1)}, u32[]{:S(2)}, u32[]{:S(2)}) collective-permute-start(bf16[2,256,256]{2,1,0:T(8,128)(2,1)S(1)} %pad_maximum_fusion.3), channel_id=1, source_target_pairs={{0,8},{4,12},{8,0},{12,4},{16,24},{20,28},{24,16},{28,20},{1,9},{5... | collective-permute-start | bytes 786440 | tf_op jit(solution)/shard_map/ppermute | solution.py:20
  108.3 2.0 %collective-permute-start.13 = (bf16[4,256,256]{2,1,0:T(8,128)(2,1)S(1)}, bf16[4,256,256]{2,1,0:T(8,128)(2,1)S(1)}, u32[]{:S(2)}, u32[]{:S(2)}) collective-permute-start(bf16[4,256,256]{2,1,0:T(8,128)(2,1)S(1)} %pad_maximum_fusion.2.same_ref), channel_id=1, source_target_pairs={{0,4},{4,0},{8,12},{12,8},{16,20},{20,16},{24,28},{28,24},{1,5},{5... | collective-permute-start | bytes 1572872 | tf_op jit(solution)/shard_map/ppermute | solution.py:20

commit v5 on v4

--- a/solution.py
+++ b/solution.py
@@ -422,33 +422,32 @@
     out_ref[...] = adam_step(grad, weight_ref[...], first_ref[...], second_ref[...], scal_ref)
 
 
-def adam_call(tokens, cot, packs, hid_last, cot_last, weight, first, second, where, scal, factor, frag_cols, part, *base):
+def adam_call(tokens, cot, packs, hid_last, cot_last, weight, first, second, where, scal, factor, frag_cols, j, *base):
     rows, keys = weight.shape
     toks = tokens.shape[0]
     tile = min(1024, rows // 2)
     steps = rows // tile
-    lo = part * (steps // 2)
     skip = keys // tile
     groups = len(packs) + 2
 
-    def col(j, w):
-        return j + (j >= w[1]).astype(jnp.int32)
+    def col(w):
+        return j + (w[1] <= j).astype(jnp.int32)
 
     def block(height):
-        return pl.BlockSpec((height, frag_cols), lambda i, j, w: (0, col(j, w)))
-
-    state = pl.BlockSpec((tile, frag_cols), lambda i, j, w: (lo + i, col(j, w)))
+        return pl.BlockSpec((height, frag_cols), lambda i, w: (0, col(w)))
+
+    state = pl.BlockSpec((tile, frag_cols), lambda i, w: (i, col(w)))
     return pl.pallas_call(
         functools.partial(adam_kernel, groups, len(cot_last), factor),
         grid_spec=pltpu.PrefetchScalarGridSpec(
             num_scalar_prefetch=1,
-            grid=(steps // 2, keys // frag_cols - 1),
+            grid=(steps,),
             in_specs=[
                 pl.BlockSpec(memory_space=pltpu.SMEM),
-                pl.BlockSpec((toks, tile), lambda i, j, w: (0, w[0] * steps + lo + i)),
+                pl.BlockSpec((toks, tile), lambda i, w: (0, w[0] * steps + i)),
             ]
-            + [pl.BlockSpec((toks, tile), lambda i, j, w: (0, skip + lo + i))] * len(packs)
-            + [pl.BlockSpec((toks, tile), lambda i, j, w: (0, lo + i))]
+            + [pl.BlockSpec((toks, tile), lambda i, w: (0, skip + i))] * len(packs)
+            + [pl.BlockSpec((toks, tile), lambda i, w: (0, i))]
             + [block(toks)] * (groups - 1)
             + [state] * 3
             + [block(c.shape[0]) for c in cot_last]
@@ -568,11 +567,19 @@
     backs = [pair(x, "fsdp", m) for x, m in zip(gives, offsets)]
     cot_last = [after(c, *gives) for c in cot_last]
 
-    def inner_half(part, hid, *base):
-        return adam_call(
-            tokens, cotangent, packs, hid, cot_last, weight, first, second, where, scal, factor,
-            frag_cols, part, *base,
-        )
+    inner = []
+
+    def inner_step(blocks, *ready):
+        for _ in range(blocks):
+            if len(inner) < FRAGS - 1:
+                hid = after(hid_last, *ready)
+                inner.append(
+                    adam_call(
+                        tokens, cotangent, packs, hid, cot_last, weight, first, second, where, scal,
+                        factor, frag_cols, len(inner), *inner[-1:],
+                    )
+                )
+        return inner[-1]
 
     keep, give = frag_call(
         hid_last, cot_last, grad_frag, weight, first, second, where, scal, factor, own_rows,
@@ -585,9 +592,8 @@
     for k in bits:
         keep, leave = split_call(k, where, keep, got)
         got = pair(leave, "rep", 2 << k)
-        if k == 0:
-            inner = inner_half(0, after(hid_last, leave))
-            got = after(got, inner)
+        if k in (0, bits[-1]):
+            got = after(got, inner_step(1, leave))
     backs.append(pair(give_last, "fsdp", offsets[-1]))
     outer_args = (keep, got, *outer_frag)
     spread = outer_call(replicas, *outer_args)
@@ -603,11 +609,10 @@
             )
             got = after(got, key_acc)
         if k == 0:
-            inner = inner_half(1, after(hid_last, spread), inner)
-            got = after(got, inner)
+            got = after(got, inner_step(FRAGS, spread))
         spread = jnp.concatenate([spread, got], axis=0)
     got = pair(spread, "rep", 1)
-    new_local = spread_call(bits, where, spread, got, inner)
+    new_local = spread_call(bits, where, spread, got, inner[-1])
     back_out, keys_out = place_call(
         where, [after(backs[-1], new_local)], key_acc, back_out, offsets[-1:], True, factor
     )

time: 115 us -> 114 us (level)
  waiting for transfers between devices: 27.7 us -> 23.9 us
  Pallas kernels: 59.1 us -> 61.6 us
    ppermute x14, waiting for transfers between devices: 27.7 us -> 23.9 us  [pair(): return lax.ppermute(x, axis, [(i, i ^ offset) for i in range(size)])]
    pallas_call x2 -> x3, Pallas kernels: 18.6 us -> 21.1 us  [adam_call(): pl.pallas_call(functools.partial(adam_kernel, groups, len(cot_last), fact...]
  transfers between devices with their start and end apart: 14 -> 14, of which waited for: 7 -> 7; matrix products, arithmetic and copies ran while one was open for 3% -> 3% of each run, Pallas kernels for 50% -> 52%
where the time goes in v5:
time: 114 us
  Pallas kernels  61.6 us (54%)
  waiting for transfers between devices  23.9 us (21%)
  starting transfers between devices  17.6 us (15%)
  local copies, waits for them, and re-layouts  6.06 us (5%)
  other arithmetic  2.61 us (2%)
  between operations  1.76 us (2%)
    ppermute x14, waiting for transfers between devices, pair(): return lax.ppermute(x, axis, [(i, i ^ offset) for i in range(size)])  23.9 us
    pallas_call x3, Pallas kernels, adam_call(): pl.pallas_call(functools.partial(adam_kernel, groups, len(cot_last), fact...  21.1 us
    ppermute x14, starting transfers between devices, pair(): return lax.ppermute(x, axis, [(i, i ^ offset) for i in range(size)])  17.6 us
    pallas_call x1, Pallas kernels, near_call(): pl.pallas_call(functools.partial(near_kernel, groups, factor, steps), gri...  10 us
    pallas_call x1, Pallas kernels, own_call(): pl.pallas_call(functools.partial(own_kernel, factor), grid_spec=pltpu.Pre...  8.23 us
    pallas_call x1, Pallas kernels, frag_call(): pl.pallas_call(functools.partial(frag_kernel, factor), in_specs=[pl.Block...  5.66 us
    pallas_call x2, Pallas kernels, place_call(): pl.pallas_call(functools.partial(place_kernel, tuple(offsets), final, fac...  4.63 us
    pallas_call x1, Pallas kernels, last_call(): pl.pallas_call(functools.partial(last_kernel, factor, steps), grid=(steps...  3.29 us
  transfers between devices with their start and end apart: 14, of which 7 were waited for; matrix products, arithmetic and copies ran while one was open for 3% of the time, Pallas kernels for 52%

profile of v5, /device:TPU:0, one launch (start us, length us, event | category | flops | bytes accessed | tf_op | source)
XLA Modules:
  0.0 113.5 jit_solution(8978632093169527050)
XLA Ops:
  0.7 1.5 %dynamic-slice_bitcast_fusion = (bf16[192,2048]{1,0:T(8,128)(2,1)S(1)}, bf16[192,2048]{1,0:T(8,128)(2,1)S(1)}) fusion(bf16[1,192,8192]{2,1,0:T(8,128)(2,1)} %param.9, s32[]{:T(128)S(6)} %select_n.46, s32[]{:T(128)S(6)} %select_n.45), kind=kLoop, calls=%fused_computation.2 | loop fusion | bytes 3145736 | tf_op jit(solution)/shard_map/dynamic_slice | solution.py:544
  2.2 1.7 %pad_maximum_fusion = (bf16[192,3072]{1,0:T(8,128)(2,1)}, bf16[192,3072]{1,0:T(8,128)(2,1)}) fusion(bf16[192,1024]{1,0:T(8,128)(2,1)S(1)} %bitcast.36, bf16[192,2048]{1,0:T(8,128)(2,1)S(1)} %get-tuple-element.97, bf16[192,2048]{1,0:T(8,128)(2,1)S(1)} %get-tuple-element.98), kind=kLoop, calls=%fused_computation | loop fusion | flops 4128768 | bytes 4325376 | tf_op jit(solution)/shard_map/concatenate | solution.py:547
  3.9 3.0 %collective-permute-start.1 = (bf16[192,3072]{1,0:T(8,128)(2,1)}, bf16[192,3072]{1,0:T(8,128)(2,1)}, u32[]{:S(2)}, u32[]{:S(2)}) collective-permute-start(bf16[192,3072]{1,0:T(8,128)(2,1)} %get-tuple-element.99), channel_id=1, source_target_pairs={{0,2},{1,3},{2,0},{3,1},{4,6},{5,7},{6,4},{7,5},{8,10},{9,11},{10,... | collective-permute-start | bytes 3538952 | tf_op jit(solution)/shard_map/ppermute | solution.py:20
  6.9 1.5 %collective-permute-start = (bf16[192,3072]{1,0:T(8,128)(2,1)}, bf16[192,3072]{1,0:T(8,128)(2,1)}, u32[]{:S(2)}, u32[]{:S(2)}) collective-permute-start(bf16[192,3072]{1,0:T(8,128)(2,1)} %get-tuple-element.100), channel_id=1, source_target_pairs={{0,1},{1,0},{2,3},{3,2},{4,5},{5,4},{6,7},{7,6},{8,9},{9,8},{10,11... | collective-permute-start | bytes 3538952 | tf_op jit(solution)/shard_map/ppermute | solution.py:20
  9.1 1.3 %dynamic_slice.16 = s32[1,1]{0,1:T(1,128)} dynamic-slice(s32[8,4]{0,1:T(4,128)} %param.16, s32[]{:T(128)S(6)} %select_n.39, s32[]{:T(128)S(6)} %select_n.41), dynamic_slice_sizes={1,1} | dynamic-slice | bytes 12 | tf_op jit(solution)/shard_map/dynamic_slice | solution.py:531
  10.4 0.7 pad_add_fusion.where_ref
  11.1 8.2 %shard_map.128 = (bf16[2048,1024]{1,0:T(8,128)(2,1)}, bf16[192,8192]{1,0:T(8,128)(2,1)}, f32[192,1024]{1,0:T(8,128)S(1)}) custom-call(s32[4]{0:T(128)S(1)} %pad_add_fusion.where_ref, bf16[192,8192]{1,0:T(8,128)(2,1)S(1)} %bitcast.34, bf16[192,1024]{1,0:T(8,128)(2,1)S(1)} %bitcast.37, f32[2048,1024]{1,0:T(8,128)} %bitcast.44), custom_call_target="tpu_custom_call" | custom-call | flops 1 | bytes 1 | tf_op jit(solution)/shard_map/pallas_call | solution.py:81
  19.3 0.9 copy-done.9
  20.2 2.0 %shard_map.129 = (f32[256,1024]{1,0:T(8,128)}, f32[256,1024]{1,0:T(8,128)}, f32[256,256]{1,0:T(8,128)S(1)}, f32[256,256]{1,0:T(8,128)S(1)}) custom-call(s32[4]{0:T(128)S(1)} %pad_add_fusion.where_ref, f32[256,1024]{1,0:T(8,128)S(1)} %bitcast.42, f32[256,1024]{1,0:T(8,128)S(1)} %bitcast.43), custom_call_target="tpu_custom_call" | custom-call | flops 1 | bytes 1 | tf_op jit(solution)/shard_map/pallas_call | solution.py:308
  22.2 0.7 copy-done.5
  22.9 0.7 copy-done.7
  23.6 0.9 constant_dynamic-slice_fusion
  24.6 8.6 %collective-permute-done.1.y_ref.refs_2_.refs_5_.refs_6_ = bf16[192,3072]{1,0:T(8,128)(2,1)} collective-permute-done((bf16[192,3072]{1,0:T(8,128)(2,1)}, bf16[192,3072]{1,0:T(8,128)(2,1)}, u32[]{:S(2)}, u32[]{:S(2)}) %collective-permute-start.1) | collective-permute-done | bytes 1179680 | tf_op jit(solution)/shard_map/ppermute | solution.py:20
  33.2 1.5 %collective-permute-done.x_ref.refs_1_.refs_4_.refs_5_ = bf16[192,3072]{1,0:T(8,128)(2,1)} collective-permute-done((bf16[192,3072]{1,0:T(8,128)(2,1)}, bf16[192,3072]{1,0:T(8,128)(2,1)}, u32[]{:S(2)}, u32[]{:S(2)}) %collective-permute-start) | collective-permute-done | bytes 1179680 | tf_op jit(solution)/shard_map/ppermute | solution.py:20
  34.7 1.4 %collective-permute-start.2 = (bf16[192,2048]{1,0:T(8,128)(2,1)}, bf16[192,2048]{1,0:T(8,128)(2,1)S(1)}, u32[]{:S(2)}, u32[]{:S(2)}) collective-permute-start(bf16[192,2048]{1,0:T(8,128)(2,1)} %constant_dynamic-slice_fusion), channel_id=1, source_target_pairs={{0,3},{1,2},{2,1},{3,0},{4,7},{5,6},{6,5},{7,4},{8,11},{9,10},{10,... | collective-permute-start | bytes 2359304 | tf_op jit(solution)/shard_map/ppermute | solution.py:20
  36.1 1.8 %shard_map.130 = (bf16[96,1024]{1,0:T(8,128)(2,1)}, bf16[96,1024]{1,0:T(8,128)(2,1)}) custom-call(bf16[192,3072]{1,0:T(8,128)(2,1)} %collective-permute-done.x_ref.refs_1_.refs_4_.refs_5_, bf16[192,3072]{1,0:T(8,128)(2,1)} %collective-permute-done.1.y_ref.refs_2_.refs_5_.refs_6_), custom_call_target="tpu_custom_call" | custom-call | flops 1 | bytes 1 | tf_op jit(solution)/shard_map/pallas_call | solution.py:287
  37.9 1.5 %collective-permute-start.4 = (bf16[96,1024]{1,0:T(8,128)(2,1)}, bf16[96,1024]{1,0:T(8,128)(2,1)S(1)}, u32[]{:S(2)}, u32[]{:S(2)}) collective-permute-start(bf16[96,1024]{1,0:T(8,128)(2,1)} %get-tuple-element.59), channel_id=1, source_target_pairs={{0,2},{1,3},{2,0},{3,1},{4,6},{5,7},{6,4},{7,5},{8,10},{9,11},{10,... | collective-permute-start | bytes 589832 | tf_op jit(solution)/shard_map/ppermute | solution.py:20
  39.4 0.5 collective-permute-start.3
  40.0 10.0 %shard_map.131 = (f32[2048,1024]{1,0:T(8,128)}, bf16[192,3072]{1,0:T(8,128)(2,1)}, bf16[192,3072]{1,0:T(8,128)(2,1)}) custom-call(s32[4]{0:T(128)S(1)} %pad_add_fusion.where_ref, bf16[192,8192]{1,0:T(8,128)(2,1)} %bitcast.30, bf16[192,3072]{1,0:T(8,128)(2,1)} %collective-permute-done.x_ref.refs_1_.refs_4_.refs_5_, ...), custom_call_target="tpu_custom_call" | custom-call | flops 1 | bytes 1 | tf_op jit(solution)/shard_map/pallas_call | solution.py:138
  50.0 0.3 collective-permute-start.11
  50.3 1.7 %collective-permute-start.10 = (bf16[192,3072]{1,0:T(8,128)(2,1)}, bf16[192,3072]{1,0:T(8,128)(2,1)}, u32[]{:S(2)}, u32[]{:S(2)}) collective-permute-start(bf16[192,3072]{1,0:T(8,128)(2,1)} %get-tuple-element.62), channel_id=1, source_target_pairs={{0,1},{1,0},{2,3},{3,2},{4,5},{5,4},{6,7},{7,6},{8,9},{9,8},{10,11... | collective-permute-start | bytes 3538952 | tf_op jit(solution)/shard_map/ppermute | solution.py:20
  52.2 0.1 pad_maximum_fusion.4.scal_ref
  52.3 5.9 %collective-permute-done.4.refs_1_.refs_11_ = bf16[96,1024]{1,0:T(8,128)(2,1)S(1)} collective-permute-done((bf16[96,1024]{1,0:T(8,128)(2,1)}, bf16[96,1024]{1,0:T(8,128)(2,1)S(1)}, u32[]{:S(2)}, u32[]{:S(2)}) %collective-permute-start.4) | collective-permute-done | bytes 196640 | tf_op jit(solution)/shard_map/ppermute | solution.py:20
  58.2 1.2 %collective-permute-done.3.refs_0_.refs_10_ = bf16[96,1024]{1,0:T(8,128)(2,1)S(1)} collective-permute-done((bf16[96,1024]{1,0:T(8,128)(2,1)}, bf16[96,1024]{1,0:T(8,128)(2,1)S(1)}, u32[]{:S(2)}, u32[]{:S(2)}) %collective-permute-start.3) | collective-permute-done | bytes 196640 | tf_op jit(solution)/shard_map/ppermute | solution.py:20
  59.3 5.7 %shard_map.132 = (bf16[4,256,256]{2,1,0:T(8,128)(2,1)S(1)}, bf16[4,256,256]{2,1,0:T(8,128)(2,1)S(1)}) custom-call(s32[4]{0:T(128)S(1)} %pad_add_fusion.where_ref, f32[4]{0:T(128)S(1)} %pad_maximum_fusion.4.scal_ref, bf16[192,2048]{1,0:T(8,128)(2,1)S(1)} %collective-permute-done.2.hid_ref.refs_3_, ...), custom_call_target="tpu_custom_call" | custom-call | flops 1 | bytes 1 | tf_op jit(solution)/shard_map/pallas_call | solution.py:243
  65.0 0.1 collective-permute-start.6
  65.1 3.3 %shard_map.133 = bf16[192,3072]{1,0:T(8,128)(2,1)S(1)} custom-call(bf16[192,2048]{1,0:T(8,128)(2,1)S(1)} %collective-permute-done.2.hid_ref.refs_3_, bf16[2048,1024]{1,0:T(8,128)(2,1)S(1)} %copy-done.1, bf16[96,1024]{1,0:T(8,128)(2,1)S(1)} %collective-permute-done.3.refs_0_.refs_10_, bf16[96,1024]{1,0:T(8,128)(2,1)S(1)} %collective-permute-done.4.refs_1_.refs_11_), custom_call_target="tpu_custom_call" | custom-call | flops 1 | bytes 1 | tf_op jit(solution)/shard_map/pallas_call | solution.py:171
  68.4 0.7 shard_map.134
  69.1 1.9 %collective-permute-start.7 = (bf16[2,256,256]{2,1,0:T(8,128)(2,1)S(1)}, bf16[2,256,256]{2,1,0:T(8,128)(2,1)S(1)}, u32[]{:S(2)}, u32[]{:S(2)}) collective-permute-start(bf16[2,256,256]{2,1,0:T(8,128)(2,1)S(1)} %get-tuple-element.72), channel_id=1, source_target_pairs={{0,8},{4,12},{8,0},{12,4},{16,24},{20,28},{24,16},{28,20},{1,9},{5... | collective-permute-start | bytes 786440 | tf_op jit(solution)/shard_map/ppermute | solution.py:20
  70.9 7.0 %shard_map.135.refs_12_ = f32[2048,1024]{1,0:T(8,128)} custom-call(s32[4]{0:T(128)S(1)} %pad_add_fusion.where_ref, f32[4]{0:T(128)S(1)} %pad_maximum_fusion.4.scal_ref, bf16[192,8192]{1,0:T(8,128)(2,1)} %bitcast.31, bf16[192,3072]{1,0:T(8,128)(2,1)} %collective-permute-done.x_ref.refs_1_.refs_4_.refs_5_, ...), custom_call_target="tpu_custom_call" | custom-call | flops 1 | bytes 1 | tf_op jit(solution)/shard_map/pallas_call | solution.py:440
  78.0 0.6 shard_map.136
  78.6 0.0 copy-start.6
  78.6 2.7 %collective-permute-start.8 = (bf16[1,256,256]{2,1,0:T(8,128)(2,1)S(1)}, bf16[1,256,256]{2,1,0:T(8,128)(2,1)S(1)}, u32[]{:S(2)}, u32[]{:S(2)}) collective-permute-start(bf16[1,256,256]{2,1,0:T(8,128)(2,1)S(1)} %get-tuple-element.76), channel_id=1, source_target_pairs={{0,16},{4,20},{8,24},{12,28},{16,0},{20,4},{24,8},{28,12},{1,17},{... | collective-permute-start | bytes 393224 | tf_op jit(solution)/shard_map/ppermute | solution.py:20
  81.4 2.4 %collective-permute-start.5 = (bf16[192,3072]{1,0:T(8,128)(2,1)S(1)}, bf16[192,3072]{1,0:T(8,128)(2,1)S(1)}, u32[]{:S(2)}, u32[]{:S(2)}) collective-permute-start(bf16[192,3072]{1,0:T(8,128)(2,1)S(1)} %shard_map.133), channel_id=1, source_target_pairs={{0,3},{1,2},{2,1},{3,0},{4,7},{5,6},{6,5},{7,4},{8,11},{9,10},{10,... | collective-permute-start | bytes 3538952 | tf_op jit(solution)/shard_map/ppermute | solution.py:20
  83.8 7.0 %shard_map.137.refs_12_ = f32[2048,1024]{1,0:T(8,128)} custom-call(s32[4]{0:T(128)S(1)} %pad_add_fusion.where_ref, f32[4]{0:T(128)S(1)} %pad_maximum_fusion.4.scal_ref, bf16[192,8192]{1,0:T(8,128)(2,1)} %bitcast.32, bf16[192,3072]{1,0:T(8,128)(2,1)} %collective-permute-done.x_ref.refs_1_.refs_4_.refs_5_, ...), custom_call_target="tpu_custom_call", output_to_operand_aliasing={{}: (14, {})} | custom-call | flops 1 | bytes 1 | tf_op jit(solution)/shard_map/pallas_call | solution.py:440
  90.9 0.1 shard_map.138
  91.0 0.4 collective-permute-start.9
  91.4 1.4 %shard_map.139 = (f32[256,1024]{1,0:T(8,128)}, f32[256,1024]{1,0:T(8,128)}) custom-call(s32[4]{0:T(128)S(1)} %pad_add_fusion.where_ref, f32[1,256,256]{2,1,0:T(8,128)S(1)} %get-tuple-element.81.refs_0_.stay_ref, bf16[1,256,256]{2,1,0:T(8,128)(2,1)S(1)} %collective-permute-done.8.refs_1_.got_ref, ...), custom_call_target="tpu_custom_call", output_to_operand_aliasing={{0}: (5, {}), {1}: (6, {})} | custom-call | flops 1 | bytes 1 | tf_op jit(solution)/shard_map/pallas_call | solution.py:360
  92.9 2.4 %shard_map.140 = (bf16[192,8192]{1,0:T(8,128)(2,1)}, f32[192,1024]{1,0:T(8,128)S(1)}) custom-call(s32[4]{0:T(128)S(1)} %pad_add_fusion.where_ref, bf16[192,3072]{1,0:T(8,128)(2,1)} %collective-permute-done.10.refs_0_, bf16[192,3072]{1,0:T(8,128)(2,1)S(1)} %collective-permute-done.11.refs_1_, ...), custom_call_target="tpu_custom_call", output_to_operand_aliasing={{0}: (4, {})} | custom-call | flops 1 | bytes 1 | tf_op jit(solution)/shard_map/pallas_call | solution.py:400
  95.3 4.4 %collective-permute-done.9 = bf16[1,256,256]{2,1,0:T(8,128)(2,1)S(1)} collective-permute-done((bf16[1,256,256]{2,1,0:T(8,128)(2,1)S(1)}, bf16[1,256,256]{2,1,0:T(8,128)(2,1)S(1)}, u32[]{:S(2)}, u32[]{:S(2)}) %collective-permute-start.9) | collective-permute-done | bytes 131104 | tf_op jit(solution)/shard_map/ppermute | solution.py:20
  99.8 0.1 collective-permute-start.12
  99.8 7.1 %shard_map.141.base_ref = f32[2048,1024]{1,0:T(8,128)} custom-call(s32[4]{0:T(128)S(1)} %pad_add_fusion.where_ref, f32[4]{0:T(128)S(1)} %pad_maximum_fusion.4.scal_ref, bf16[192,8192]{1,0:T(8,128)(2,1)} %bitcast.33, bf16[192,3072]{1,0:T(8,128)(2,1)} %collective-permute-done.x_ref.refs_1_.refs_4_.refs_5_, ...), custom_call_target="tpu_custom_call", output_to_operand_aliasing={{}: (14, {})} | custom-call | flops 1 | bytes 1 | tf_op jit(solution)/shard_map/pallas_call | solution.py:440
  106.9 0.4 collective-permute-done.12
  107.3 0.1 pad_maximum_fusion.2.same_ref
  107.4 0.1 collective-permute-start.13
  107.4 1.9 %collective-permute-done.13.other_ref = bf16[4,256,256]{2,1,0:T(8,128)(2,1)S(1)} collective-permute-done((bf16[4,256,256]{2,1,0:T(8,128)(2,1)S(1)}, bf16[4,256,256]{2,1,0:T(8,128)(2,1)S(1)}, u32[]{:S(2)}, u32[]{:S(2)}) %collective-permute-start.13) | collective-permute-done | bytes 524320 | tf_op jit(solution)/shard_map/ppermute | solution.py:20
  109.3 2.0 %shard_map.142 = f32[2048,1024]{1,0:T(8,128)} custom-call(s32[4]{0:T(128)S(1)} %pad_add_fusion.where_ref, bf16[4,256,256]{2,1,0:T(8,128)(2,1)S(1)} %pad_maximum_fusion.2.same_ref, bf16[4,256,256]{2,1,0:T(8,128)(2,1)S(1)} %collective-permute-done.13.other_ref, f32[2048,1024]{1,0:T(8,128)} %shard_map.141.base_ref), custom_call_target="tpu_custom_call", output_to_operand_aliasing={{}: (3, {})} | custom-call | flops 1 | bytes 1 | tf_op jit(solution)/shard_map/pallas_call | solution.py:490
  111.3 2.2 %shard_map.143 = (bf16[192,8192]{1,0:T(8,128)(2,1)}, bf16[192,1024]{1,0:T(8,128)(2,1)}) custom-call(s32[4]{0:T(128)S(1)} %pad_add_fusion.where_ref, bf16[192,3072]{1,0:T(8,128)(2,1)S(1)} %collective-permute-done.5.refs_0_, f32[192,1024]{1,0:T(8,128)S(1)} %get-tuple-element.88.refs_1_, ...), custom_call_target="tpu_custom_call", output_to_operand_aliasing={{0}: (3, {})} | custom-call | flops 1 | bytes 1 | tf_op jit(solution)/shard_map/pallas_call | solution.py:400
  (26 shorter events, 0.1 us)
Async XLA Ops:
  0.6 1.6 %copy-start.2 = (bf16[1,192,1024]{2,1,0:T(8,128)(2,1)S(1)}, bf16[1,192,1024]{2,1,0:T(8,128)(2,1)}, u32[]{:S(2)}) copy-start(bf16[1,192,1024]{2,1,0:T(8,128)(2,1)} %param.10) | copy-start | bytes 1179652
  2.2 8.9 %copy-start = (bf16[1,192,8192]{2,1,0:T(8,128)(2,1)S(1)}, bf16[1,192,8192]{2,1,0:T(8,128)(2,1)}, u32[]{:S(2)}) copy-start(bf16[1,192,8192]{2,1,0:T(8,128)(2,1)} %param.9) | copy-start | bytes 9437188
  3.9 29.2 %collective-permute-start.1 = (bf16[192,3072]{1,0:T(8,128)(2,1)}, bf16[192,3072]{1,0:T(8,128)(2,1)}, u32[]{:S(2)}, u32[]{:S(2)}) collective-permute-start(bf16[192,3072]{1,0:T(8,128)(2,1)} %get-tuple-element.99), channel_id=1, source_target_pairs={{0,2},{1,3},{2,0},{3,1},{4,6},{5,7},{6,4},{7,5},{8,10},{9,11},{10,... | collective-permute-start | bytes 3538952 | tf_op jit(solution)/shard_map/ppermute | solution.py:20
  6.9 27.7 %collective-permute-start = (bf16[192,3072]{1,0:T(8,128)(2,1)}, bf16[192,3072]{1,0:T(8,128)(2,1)}, u32[]{:S(2)}, u32[]{:S(2)}) collective-permute-start(bf16[192,3072]{1,0:T(8,128)(2,1)} %get-tuple-element.100), channel_id=1, source_target_pairs={{0,1},{1,0},{2,3},{3,2},{4,5},{5,4},{6,7},{7,6},{8,9},{9,8},{10,11... | collective-permute-start | bytes 3538952 | tf_op jit(solution)/shard_map/ppermute | solution.py:20
  11.1 9.1 %copy-start.3 = (f32[1,256,1024]{2,1,0:T(8,128)S(1)}, f32[1,256,1024]{2,1,0:T(8,128)}, u32[]{:S(2)}) copy-start(f32[1,256,1024]{2,1,0:T(8,128)} %param.14) | copy-start | bytes 3145732
  11.1 9.1 %copy-start.4 = (f32[1,256,1024]{2,1,0:T(8,128)S(1)}, f32[1,256,1024]{2,1,0:T(8,128)}, u32[]{:S(2)}) copy-start(f32[1,256,1024]{2,1,0:T(8,128)} %param.15) | copy-start | bytes 3145732
  19.3 0.9 copy-start.9
  22.2 0.7 copy-start.5
  22.9 0.7 copy-start.7
  34.7 24.7 %collective-permute-start.2 = (bf16[192,2048]{1,0:T(8,128)(2,1)}, bf16[192,2048]{1,0:T(8,128)(2,1)S(1)}, u32[]{:S(2)}, u32[]{:S(2)}) collective-permute-start(bf16[192,2048]{1,0:T(8,128)(2,1)} %constant_dynamic-slice_fusion), channel_id=1, source_target_pairs={{0,3},{1,2},{2,1},{3,0},{4,7},{5,6},{6,5},{7,4},{8,11},{9,10},{10,... | collective-permute-start | bytes 2359304 | tf_op jit(solution)/shard_map/ppermute | solution.py:20
  37.9 20.3 %collective-permute-start.4 = (bf16[96,1024]{1,0:T(8,128)(2,1)}, bf16[96,1024]{1,0:T(8,128)(2,1)S(1)}, u32[]{:S(2)}, u32[]{:S(2)}) collective-permute-start(bf16[96,1024]{1,0:T(8,128)(2,1)} %get-tuple-element.59), channel_id=1, source_target_pairs={{0,2},{1,3},{2,0},{3,1},{4,6},{5,7},{6,4},{7,5},{8,10},{9,11},{10,... | collective-permute-start | bytes 589832 | tf_op jit(solution)/shard_map/ppermute | solution.py:20
  39.4 19.9 %collective-permute-start.3 = (bf16[96,1024]{1,0:T(8,128)(2,1)}, bf16[96,1024]{1,0:T(8,128)(2,1)S(1)}, u32[]{:S(2)}, u32[]{:S(2)}) collective-permute-start(bf16[96,1024]{1,0:T(8,128)(2,1)} %get-tuple-element.57), channel_id=1, source_target_pairs={{0,1},{1,0},{2,3},{3,2},{4,5},{5,4},{6,7},{7,6},{8,9},{9,8},{10,11... | collective-permute-start | bytes 589832 | tf_op jit(solution)/shard_map/ppermute | solution.py:20
  50.0 42.9 %collective-permute-start.11 = (bf16[192,3072]{1,0:T(8,128)(2,1)}, bf16[192,3072]{1,0:T(8,128)(2,1)S(1)}, u32[]{:S(2)}, u32[]{:S(2)}) collective-permute-start(bf16[192,3072]{1,0:T(8,128)(2,1)} %get-tuple-element.63), channel_id=1, source_target_pairs={{0,2},{1,3},{2,0},{3,1},{4,6},{5,7},{6,4},{7,5},{8,10},{9,11},{10,... | collective-permute-start | bytes 3538952 | tf_op jit(solution)/shard_map/ppermute | solution.py:20
  50.3 42.5 %collective-permute-start.10 = (bf16[192,3072]{1,0:T(8,128)(2,1)}, bf16[192,3072]{1,0:T(8,128)(2,1)}, u32[]{:S(2)}, u32[]{:S(2)}) collective-permute-start(bf16[192,3072]{1,0:T(8,128)(2,1)} %get-tuple-element.62), channel_id=1, source_target_pairs={{0,1},{1,0},{2,3},{3,2},{4,5},{5,4},{6,7},{7,6},{8,9},{9,8},{10,11... | collective-permute-start | bytes 3538952 | tf_op jit(solution)/shard_map/ppermute | solution.py:20
  59.3 5.8 %copy-start.1 = (bf16[2048,1024]{1,0:T(8,128)(2,1)S(1)}, bf16[2048,1024]{1,0:T(8,128)(2,1)}, u32[]{:S(2)}) copy-start(bf16[2048,1024]{1,0:T(8,128)(2,1)} %get-tuple-element.51.refs_6_.weight_ref) | copy-start | bytes 12582916
  65.0 3.4 %collective-permute-start.6 = (bf16[4,256,256]{2,1,0:T(8,128)(2,1)S(1)}, bf16[4,256,256]{2,1,0:T(8,128)(2,1)S(1)}, u32[]{:S(2)}, u32[]{:S(2)}) collective-permute-start(bf16[4,256,256]{2,1,0:T(8,128)(2,1)S(1)} %get-tuple-element.69), channel_id=1, source_target_pairs={{0,4},{4,0},{8,12},{12,8},{16,20},{20,16},{24,28},{28,24},{1,5},{5... | collective-permute-start | bytes 1572872 | tf_op jit(solution)/shard_map/ppermute | solution.py:20
  69.1 8.9 %collective-permute-start.7 = (bf16[2,256,256]{2,1,0:T(8,128)(2,1)S(1)}, bf16[2,256,256]{2,1,0:T(8,128)(2,1)S(1)}, u32[]{:S(2)}, u32[]{:S(2)}) collective-permute-start(bf16[2,256,256]{2,1,0:T(8,128)(2,1)S(1)} %get-tuple-element.72), channel_id=1, source_target_pairs={{0,8},{4,12},{8,0},{12,4},{16,24},{20,28},{24,16},{28,20},{1,9},{5... | collective-permute-start | bytes 786440 | tf_op jit(solution)/shard_map/ppermute | solution.py:20
  78.6 12.2 %copy-start.6 = (f32[256,256]{1,0:T(8,128)S(1)}, f32[256,256]{1,0:T(8,128)}, u32[]{:S(2)}) copy-start(f32[256,256]{1,0:T(8,128)} %copy-done.5) | copy-start | bytes 786436
  78.6 12.2 %copy-start.8 = (f32[256,256]{1,0:T(8,128)S(1)}, f32[256,256]{1,0:T(8,128)}, u32[]{:S(2)}) copy-start(f32[256,256]{1,0:T(8,128)} %copy-done.7) | copy-start | bytes 786436
  78.6 12.2 %collective-permute-start.8 = (bf16[1,256,256]{2,1,0:T(8,128)(2,1)S(1)}, bf16[1,256,256]{2,1,0:T(8,128)(2,1)S(1)}, u32[]{:S(2)}, u32[]{:S(2)}) collective-permute-start(bf16[1,256,256]{2,1,0:T(8,128)(2,1)S(1)} %get-tuple-element.76), channel_id=1, source_target_pairs={{0,16},{4,20},{8,24},{12,28},{16,0},{20,4},{24,8},{28,12},{1,17},{... | collective-permute-start | bytes 393224 | tf_op jit(solution)/shard_map/ppermute | solution.py:20
  81.4 30.0 %collective-permute-start.5 = (bf16[192,3072]{1,0:T(8,128)(2,1)S(1)}, bf16[192,3072]{1,0:T(8,128)(2,1)S(1)}, u32[]{:S(2)}, u32[]{:S(2)}) collective-permute-start(bf16[192,3072]{1,0:T(8,128)(2,1)S(1)} %shard_map.133), channel_id=1, source_target_pairs={{0,3},{1,2},{2,1},{3,0},{4,7},{5,6},{6,5},{7,4},{8,11},{9,10},{10,... | collective-permute-start | bytes 3538952 | tf_op jit(solution)/shard_map/ppermute | solution.py:20
  90.8 2.0 %copy-start.10 = (f32[192,1024]{1,0:T(8,128)S(1)}, f32[192,1024]{1,0:T(8,128)}, u32[]{:S(2)}) copy-start(f32[192,1024]{1,0:T(8,128)} %copy-done.9) | copy-start | bytes 2359300
  91.0 8.7 %collective-permute-start.9 = (bf16[1,256,256]{2,1,0:T(8,128)(2,1)S(1)}, bf16[1,256,256]{2,1,0:T(8,128)(2,1)S(1)}, u32[]{:S(2)}, u32[]{:S(2)}) collective-permute-start(bf16[1,256,256]{2,1,0:T(8,128)(2,1)S(1)} %shard_map.138), channel_id=1, source_target_pairs={{0,16},{4,20},{8,24},{12,28},{16,0},{20,4},{24,8},{28,12},{1,17},{... | collective-permute-start | bytes 393224 | tf_op jit(solution)/shard_map/ppermute | solution.py:20
  99.8 7.6 %collective-permute-start.12 = (bf16[2,256,256]{2,1,0:T(8,128)(2,1)S(1)}, bf16[2,256,256]{2,1,0:T(8,128)(2,1)S(1)}, u32[]{:S(2)}, u32[]{:S(2)}) collective-permute-start(bf16[2,256,256]{2,1,0:T(8,128)(2,1)S(1)} %pad_maximum_fusion.3), channel_id=1, source_target_pairs={{0,8},{4,12},{8,0},{12,4},{16,24},{20,28},{24,16},{28,20},{1,9},{5... | collective-permute-start | bytes 786440 | tf_op jit(solution)/shard_map/ppermute | solution.py:20
  107.4 2.0 %collective-permute-start.13 = (bf16[4,256,256]{2,1,0:T(8,128)(2,1)S(1)}, bf16[4,256,256]{2,1,0:T(8,128)(2,1)S(1)}, u32[]{:S(2)}, u32[]{:S(2)}) collective-permute-start(bf16[4,256,256]{2,1,0:T(8,128)(2,1)S(1)} %pad_maximum_fusion.2.same_ref), channel_id=1, source_target_pairs={{0,4},{4,0},{8,12},{12,8},{16,20},{20,16},{24,28},{28,24},{1,5},{5... | collective-permute-start | bytes 1572872 | tf_op jit(solution)/shard_map/ppermute | solution.py:20
